TPU v7x, 128 devices: a whole 4x4x4 slice. The times are simulated.
128 devices in a mesh: section: 2 (over x_hi), replica: 16 (over z, y), tensor: 4 (over x_lo, core).
Axes of the slice: x: 4 (x_hi: 2, x_lo: 2; x = x_hi * 2 + x_lo), y: 4, z: 4, core: 2. Of those that a mesh axis runs over, the one named last changes fastest.
Arguments:
- inner_input: bfloat16 [3, 512, 8192], P(None, 'replica', 'tensor'), may hold values from -6 to 6
- gate_input: bfloat16 [3, 512, 8192], P(None, 'replica', 'tensor'), may hold values from -6 to 6
- residual: bfloat16 [3, 512, 4096], P(None, 'replica'), may hold values from -24 to 24
- projection: bfloat16 [2, 8192, 4096], P('section', 'tensor'), may hold values from -0.0625 to 0.0625
- state_proj: bfloat16 [2, 8192, 288], P('section', 'tensor'), may hold values from -0.0625 to 0.0625
- step_proj: bfloat16 [2, 256, 8192], P('section', None, 'tensor'), may hold values from -0.375 to 0.375
- conv_weight: float32 [2, 4, 8192], P('section', None, 'tensor'), may hold values from -3 to 3
- conv_bias: float32 [2, 8192], P('section', 'tensor'), may hold values from -3 to 3
- decay_rate: float32 [2, 16, 8192], P('section', None, 'tensor'), may hold values from 1 to 16
- skip_gain: float32 [2, 8192], P('section', 'tensor'), may hold values from 0.5 to 1.5
- step_bias: float32 [2, 8192], P('section', 'tensor'), may hold values from -4 to -1
- norm_gain: bfloat16 [4096], replicated, may hold values from 0.099609375 to 1.8984375
- state_codes: bfloat16 [2, 512, 16, 8192], P('section', 'replica', None, 'tensor'), may hold values from -4 to 4
- state_scales: bfloat16 [2, 512, 64], P('section', 'replica', 'tensor'), may hold values from 0.19921875 to 2
- conv_window: bfloat16 [2, 512, 3, 8192], P('section', 'replica', None, 'tensor'), may hold values from -6 to 6
- cache_codes: bfloat16 [2, 64, 16, 8192], P('section', 'replica', None, 'tensor'), may hold values from -4 to 4
- cache_scales: bfloat16 [2, 64, 64], P('section', 'replica', 'tensor'), may hold values from 0.19921875 to 2
- cache_window: bfloat16 [2, 64, 3, 8192], P('section', 'replica', None, 'tensor'), may hold values from -6 to 6
- finished: int32 [3, 512], P(None, 'replica'), may hold values from 0 to 1
- refill_source: int32 [3, 512], replicated, may hold values from -1 to 63, as said below
Outputs:
- stream_out: bfloat16 [3, 512, 4096], P(None, 'replica', 'tensor')
- scan_out: bfloat16 [2, 3, 512, 8192], P('section', None, 'replica', 'tensor')
- codes_out: bfloat16 [2, 512, 16, 8192], P('section', 'replica', None, 'tensor')
- scales_out: bfloat16 [2, 512, 64], P('section', 'replica', 'tensor')
- window_out: bfloat16 [2, 512, 3, 8192], P('section', 'replica', None, 'tensor')
Inputs may be any that keep to these rules, and one draw needn't show every extreme that they name: `refill_source`: -1 wherever finished is 0. A row index r >= 0 lies on replica r // 4. In each tick at most 2 slots of one replica take rows that lie on one replica, and at most 23 slots of one replica take rows; both bounds are reached in every tick.
All inputs are finite; a program needn't handle non-finite values.
Results may differ from a plain program's by a relative error of at most 0.025.
Values may be sent and summed in bfloat16 or wider, within the bound.
No kernel may reach another device: no remote copies, remote signals or barrier semaphores. Data moves between devices by JAX's collectives and lax.ppermute only.
A program may use at most 128 MiB of HBM per device.

v0:
```python
import functools
import math

import jax
import jax.numpy as jnp
from jax import lax
from jax.experimental import pallas as pl
from jax.experimental.pallas import tpu as pltpu
from jax.sharding import PartitionSpec as P

RANK = 256
STATES = 16
TICKS = 3
SLOTS = 32
ROWS = TICKS * SLOTS
CHANNELS = 2048
FEATURES = 4096
SHARE = FEATURES // 4
CB = 512
STEPS = CHANNELS // CB
LANES = 128
TERMS = RANK + 2 * STATES
POOL = 64
WIDE = 4 * CB
CODE_LANES = STATES * CB
GROUP = CODE_LANES + WIDE
LOG2E = math.log2(math.e)
F32 = jnp.float32
BF16 = jnp.bfloat16
MIB = 1024 * 1024
COST = pl.CostEstimate(flops=1, transcendentals=0, bytes_accessed=1)


def cat_kernel(a, b, c, d, first, last):
    for block, out in enumerate((first, last)):
        cols = slice(block * GROUP, (block + 1) * GROUP)
        out[...] = jnp.concatenate([a[:, cols], b[:, cols], c[:, cols], d[:, cols]], axis=0)


def cat_rows(pieces):
    shape = jax.ShapeDtypeStruct((16, GROUP), BF16)
    return pl.pallas_call(
        cat_kernel,
        out_shape=[shape, shape],
        compiler_params=pltpu.CompilerParams(vmem_limit_bytes=48 * MIB),
        cost_estimate=COST,
        name="cat_rows",
    )(*pieces)


HELD = pl.BlockSpec(memory_space=pltpu.VMEM)
SCALARS = pl.BlockSpec(memory_space=pltpu.SMEM)
ANYWHERE = pl.BlockSpec(memory_space=pltpu.HBM)


def held(shape, dtype):
    return pltpu.VMEM(shape, dtype)


def call(kernel, name, mebibytes, in_specs, out_shape, scratch, args):
    return pl.pallas_call(
        kernel,
        in_specs=in_specs,
        out_specs=[HELD] * len(out_shape) if isinstance(out_shape, list) else HELD,
        out_shape=out_shape,
        scratch_shapes=scratch,
        compiler_params=pltpu.CompilerParams(vmem_limit_bytes=mebibytes * MIB),
        cost_estimate=COST,
        name=name,
    )(*args)


def silu(x):
    return x / (1.0 + jnp.exp(-x))


def softplus(x):
    return jnp.maximum(x, 0.0) + jnp.log1p(jnp.exp(-jnp.abs(x)))


def column_of(table, lane):
    index = lax.broadcasted_iota(jnp.int32, table.shape, 1)
    return jnp.sum(jnp.where(index == lane, table, 0.0), axis=1, keepdims=True)


def tile(index):
    return pl.ds(pl.multiple_of(index * LANES, LANES), LANES)


def fill_kernel(*refs):
    sources, target, arrived = refs[:-2], refs[-2], refs[-1]
    copies, row = [], 0
    for i, source in enumerate(sources):
        count = source.shape[0]
        copies.append(
            pltpu.make_async_copy(source, target.at[pl.ds(row, count)], arrived.at[i])
        )
        copies[-1].start()
        row += count
    for copy in copies:
        copy.wait()


def fill_call(name, arrays):
    rows = sum(array.shape[0] for array in arrays)
    return call(
        fill_kernel,
        name,
        14,
        [ANYWHERE] * len(arrays),
        held((rows, arrays[0].shape[1]), BF16),
        [pltpu.SemaphoreType.DMA((len(arrays),))],
        arrays,
    )


def unfold_kernel(codes, scales, states, natural):
    def unfold(block, carry):
        cols = tile(block)
        natural[...] = codes[:, :, cols].astype(F32).reshape(SLOTS * STATES, LANES)
        scale = jnp.broadcast_to(column_of(scales[...].astype(F32), block), (SLOTS, LANES))
        for n in range(STATES):
            states[n, :, cols] = natural[pl.ds(n, SLOTS, stride=STATES), :] * scale
        return carry

    lax.fori_loop(0, CHANNELS // LANES, unfold, 0)


def unfold_call(codes, scales):
    return call(
        unfold_kernel,
        "unfold_states",
        14,
        [HELD] * 2,
        held((STATES, SLOTS, CHANNELS), F32),
        [pltpu.VMEM((SLOTS * STATES, LANES), F32)],
        [codes, scales],
    )


def pool_kernel(*refs):
    pieces, pool, arrived = refs[: 4 * STEPS], refs[-2], refs[-1]
    copies = [
        pltpu.make_async_copy(piece, pool.at[i // 4, pl.ds(i % 4 * 16, 16)], arrived.at[i])
        for i, piece in enumerate(pieces)
    ]
    for copy in copies:
        copy.start()
    for copy in copies:
        copy.wait()


def pool_call(pieces):
    return call(
        pool_kernel,
        "pool_rows",
        14,
        [ANYWHERE] * (4 * STEPS),
        held((STEPS, POOL, GROUP), BF16),
        [pltpu.SemaphoreType.DMA((4 * STEPS,))],
        pieces,
    )


STEP_ROWS, INPUT_ROWS, GATE_ROWS, WINDOW_ROWS = 0, RANK, RANK + ROWS, RANK + 2 * ROWS
TAP_ROW, BIAS_ROW, DECAY_ROW, SKIP_ROW, OFFSET_ROW = 0, 4, 5, 21, 22


def conv_block(inputs, store, fetched, keep, gains, cols):
    past = [
        store[WINDOW_ROWS + k * SLOTS : WINDOW_ROWS + (k + 1) * SLOTS, cols].astype(F32)
        for k in range(3)
    ]
    outs = []
    for tick in range(TICKS):
        rows = slice(tick * SLOTS, (tick + 1) * SLOTS)
        taps = past + [inputs[rows].astype(F32)]
        total = gains[BIAS_ROW : BIAS_ROW + 1, cols]
        for k in range(4):
            total = total + gains[TAP_ROW + k : TAP_ROW + k + 1, cols] * taps[k]
        outs.append(silu(total))
        stays = keep[rows, :1] > 0.5
        past = [
            jnp.where(stays, taps[k + 1], fetched[rows, k * CB : (k + 1) * CB]) for k in range(3)
        ]
    return jnp.concatenate(outs, axis=0), past


def conv_kernel(store, onehot, keep, gains, proj, pool, conv_out, terms, scales):
    total = jnp.zeros((ROWS, TERMS), F32)
    for block in range(STEPS):
        cols = slice(block * CB, (block + 1) * CB)
        fetched = jnp.dot(
            onehot[block // 2], pool[block, :, CODE_LANES:], preferred_element_type=F32
        )
        if block == 0:
            scales[...] = fetched[:, 3 * CB : 3 * CB + LANES]
        inputs = store[INPUT_ROWS : INPUT_ROWS + ROWS, cols]
        conv, _ = conv_block(inputs, store, fetched, keep, gains, cols)
        conv_out[:, cols] = conv
        total = total + jnp.dot(conv.astype(BF16), proj[cols], preferred_element_type=F32)
    terms[...] = total.astype(BF16)


def conv_call(args):
    return call(
        conv_kernel,
        "conv_terms",
        14,
        [HELD] * len(args),
        [
            jax.ShapeDtypeStruct((ROWS, CHANNELS), F32),
            jax.ShapeDtypeStruct((ROWS, TERMS), BF16),
            jax.ShapeDtypeStruct((ROWS, LANES), F32),
        ],
        [],
        args,
    )


def project_kernel(
    where,
    s_own,
    s_a,
    s_b,
    s_c,
    first,
    gain,
    store,
    onehot,
    keep,
    gains,
    proj,
    pool,
    big,
    conv_out,
    terms,
    win_out,
    stream_out,
    values,
    normed,
    entering,
    weight,
    loaded,
):
    section, column = where[0], where[1]
    parts = [
        pltpu.make_async_copy(big.at[pl.ds(b * CB, CB)], weight.at[b], loaded.at[b])
        for b in range(STEPS)
    ]
    for part in parts:
        part.start()

    @pl.when(section == 0)
    def _():
        stream_out[...] = first[...]
        entering[...] = store[INPUT_ROWS : INPUT_ROWS + ROWS]

    @pl.when(section == 1)
    def _():
        values[column ^ 2] = s_own[...]
        values[column] = s_a[...]
        values[column ^ 3] = s_b[...]
        values[column ^ 1] = s_c[...]
        stream_out[...] = s_a[...]
        total = jnp.zeros((ROWS, 1), F32)
        for f in range(4):
            v = values[f].astype(F32)
            total = total + jnp.sum(v * v, axis=1, keepdims=True)
        factor = lax.rsqrt(total * (1.0 / FEATURES) + 1e-05)
        for f in range(4):
            cols = slice(f * SHARE, (f + 1) * SHARE)
            v = values[f].astype(F32)
            normed[:, cols] = (v * factor * gain[:, cols].astype(F32)).astype(BF16)

    total = jnp.zeros((ROWS, TERMS), F32)
    for block in range(STEPS):
        cols = slice(block * CB, (block + 1) * CB)
        parts[block].wait()

        @pl.when(section == 1)
        def _():
            entering[:, cols] = lax.dot_general(
                normed[...], weight[block], (((1,), (1,)), ((), ())), preferred_element_type=F32
            ).astype(BF16)

        fetched = jnp.dot(
            onehot[block // 2], pool[block, :, CODE_LANES:], preferred_element_type=F32
        )
        conv, past = conv_block(entering[:, cols], store, fetched, keep, gains, cols)
        conv_out[:, cols] = conv
        for k in range(3):
            win_out[k, :, cols] = past[k].astype(BF16)
        total = total + jnp.dot(conv.astype(BF16), proj[cols], preferred_element_type=F32)
    terms[...] = total.astype(BF16)


def project_call(where, shares, args):
    return call(
        project_kernel,
        "norm_project_conv",
        36,
        [SCALARS] + [HELD] * (3 + len(args)) + [ANYWHERE],
        [
            jax.ShapeDtypeStruct((ROWS, CHANNELS), F32),
            jax.ShapeDtypeStruct((ROWS, TERMS), BF16),
            jax.ShapeDtypeStruct((3, SLOTS, CHANNELS), BF16),
            jax.ShapeDtypeStruct((ROWS, SHARE), BF16),
        ],
        [
            pltpu.VMEM((4, ROWS, SHARE), BF16),
            pltpu.VMEM((ROWS, FEATURES), BF16),
            pltpu.VMEM((ROWS, CHANNELS), BF16),
            pltpu.VMEM((STEPS, CB, FEATURES), BF16),
            pltpu.SemaphoreType.DMA((STEPS,)),
        ],
        [where, *shares, *args],
    )


def scan_kernel(final, *refs):
    refs = list(refs)
    take = lambda count: [refs.pop(0) for _ in range(count)]
    (where,) = take(1)
    terms = take(4)
    onehot, keep, cached_scales, pool, conv, start, store, gains = take(8)
    if final:
        scan_out, codes_out, scales_out = take(3)
    else:
        (big,) = take(1)
        sends = take(4)
    entry, readout, fetched, sizes = take(4)
    if final:
        states, natural, scale_acc = take(3)
    else:
        gated, weight, loaded = take(3)
        parts = [
            pltpu.make_async_copy(
                big.at[pl.ds(b * CB, CB)], weight.at[pl.ds(b * CB, CB)], loaded.at[b]
            )
            for b in range(STEPS)
        ]
        for copy in parts:
            copy.start()
    used = ROWS if final else 2 * SLOTS

    def gate(t, cols):
        first = GATE_ROWS + t * SLOTS
        return store[first : first + SLOTS, cols].astype(F32)

    total = terms[0][...].astype(F32)
    for piece in terms[1:]:
        total = total + piece[...].astype(F32)
    sizes[...] = softplus(
        jnp.dot(
            total[:, :RANK].astype(BF16),
            store[STEP_ROWS : STEP_ROWS + RANK],
            preferred_element_type=F32,
        )
        + gains[OFFSET_ROW : OFFSET_ROW + 1]
    )
    for n in range(STATES):
        e, r = RANK + n, RANK + STATES + n
        entry[n] = jnp.broadcast_to(total[:, e : e + 1], (ROWS, LANES))
        readout[n] = jnp.broadcast_to(total[:, r : r + 1], (ROWS, LANES))
    if final:
        scale_acc[...] = jnp.zeros_like(scale_acc)

    def scan_block(block, carry):
        fetched[...] = jnp.dot(
            onehot[block // 2, :used],
            pool[block, :, :CODE_LANES],
            preferred_element_type=F32,
        )
        for part in range(CB // LANES):
            index = block * (CB // LANES) + part
            scan_tile(index, part)
        return carry

    def scan_tile(index, part):
        cols = tile(index)
        new_scale = column_of(cached_scales[...], index)
        size = [sizes[t * SLOTS : (t + 1) * SLOTS, cols] for t in range(TICKS)]
        conv_now = [conv[t * SLOTS : (t + 1) * SLOTS, cols] for t in range(TICKS)]
        gain = [size[t] * conv_now[t] for t in range(TICKS)]
        total = [gains[SKIP_ROW : SKIP_ROW + 1, cols] * conv_now[t] for t in range(TICKS)]
        arrived_scale = [
            jnp.broadcast_to(new_scale[t * SLOTS : (t + 1) * SLOTS], (SLOTS, LANES))
            for t in range(TICKS - 1)
        ]
        square = jnp.zeros((SLOTS, LANES), F32)
        for n in range(STATES):
            rate = gains[DECAY_ROW + n : DECAY_ROW + n + 1, cols] * -LOG2E
            state = start[n, :, cols]
            lanes = slice(n * CB + part * LANES, n * CB + (part + 1) * LANES)
            for t in range(TICKS):
                rows = slice(t * SLOTS, (t + 1) * SLOTS)
                state = jnp.exp2(size[t] * rate) * state + gain[t] * entry[n, rows]
                total[t] = total[t] + readout[n, rows] * state
                if t < TICKS - 1:
                    state = keep[rows] * state + fetched[rows, lanes] * arrived_scale[t]
            if final:
                states[n] = state
                square = square + state * state
        if not final:
            for t in range(TICKS):
                rows = slice(t * SLOTS, (t + 1) * SLOTS)
                gated[rows, cols] = (total[t] * silu(gate(t, cols))).astype(BF16)
            return
        for t in range(TICKS):
            scan_out[t * SLOTS : (t + 1) * SLOTS, cols] = total[t].astype(BF16)
        mean = jnp.sum(square, axis=1, keepdims=True) * (1.0 / (STATES * LANES))
        scale = jnp.sqrt(mean + 1e-06).astype(BF16).astype(F32)
        inverse = jnp.broadcast_to(1.0 / scale, (SLOTS, LANES))
        last = slice((TICKS - 1) * SLOTS, TICKS * SLOTS)
        kept = keep[last] > 0.5
        for n in range(STATES):
            lanes = slice(n * CB + part * LANES, n * CB + (part + 1) * LANES)
            natural[pl.ds(n, SLOTS, stride=STATES), :] = jnp.where(
                kept, states[n] * inverse, fetched[last, lanes]
            )
        codes_out[:, :, cols] = natural[...].reshape(SLOTS, STATES, LANES).astype(BF16)
        chosen = jnp.where(kept, jnp.broadcast_to(scale, (SLOTS, LANES)), new_scale[last])
        lane = lax.broadcasted_iota(jnp.int32, (SLOTS, LANES), 1)
        scale_acc[...] = jnp.where(lane == index, chosen, scale_acc[...])

    lax.fori_loop(0, STEPS, scan_block, 0)
    if final:
        scales_out[...] = scale_acc[...].astype(BF16)
        return
    for copy in parts:
        copy.wait()
    column = where[1]
    for k, out in enumerate(sends):
        cols = pl.ds(pl.multiple_of((column ^ k) * SHARE, SHARE), SHARE)
        out[...] = jnp.dot(gated[...], weight[:, cols], preferred_element_type=F32).astype(out.dtype)


def scan_call(final, where, terms, args):
    scratch = [
        pltpu.VMEM((STATES, ROWS, LANES), F32),
        pltpu.VMEM((STATES, ROWS, LANES), F32),
        pltpu.VMEM((ROWS if final else 2 * SLOTS, STATES * CB), F32),
        pltpu.VMEM((ROWS, CHANNELS), F32),
    ]
    if final:
        out_shape = [
            jax.ShapeDtypeStruct((ROWS, CHANNELS), BF16),
            jax.ShapeDtypeStruct((SLOTS, STATES, CHANNELS), BF16),
            jax.ShapeDtypeStruct((SLOTS, LANES), BF16),
        ]
        scratch += [
            pltpu.VMEM((STATES, SLOTS, LANES), F32),
            pltpu.VMEM((SLOTS * STATES, LANES), F32),
            pltpu.VMEM((SLOTS, LANES), F32),
        ]
    else:
        out_shape = [jax.ShapeDtypeStruct((ROWS, SHARE), F32)] + [
            jax.ShapeDtypeStruct((ROWS, SHARE), BF16)
        ] * 3
        scratch += [
            pltpu.VMEM((ROWS, CHANNELS), BF16),
            pltpu.VMEM((CHANNELS, FEATURES), BF16),
            pltpu.SemaphoreType.DMA((STEPS,)),
        ]
    return call(
        functools.partial(scan_kernel, final),
        "scan_final" if final else "scan_gate_project",
        16 if final else 36,
        [SCALARS] + [HELD] * (4 + len(args) - (not final)) + [ANYWHERE] * (not final),
        out_shape,
        scratch,
        [where, *terms, *args],
    )


def add_kernel(residual, own, a, b, c, out):
    total = residual[...].astype(F32) + (
        own[...] + a[...].astype(F32) + b[...].astype(F32) + c[...].astype(F32)
    )
    out[...] = total.astype(BF16)


def add_call(args):
    return call(
        add_kernel,
        "add_residual",
        14,
        [HELD] * 5,
        [jax.ShapeDtypeStruct((ROWS, SHARE), BF16)],
        [],
        args,
    )[0]


def exchange(value, step):
    return lax.ppermute(value, "tensor", [(i, i ^ step) for i in range(4)])


def along(value, axis, step):
    if axis == "y":
        pairs = [(i, (i // 4) * 4 + (i + step) % 4) for i in range(16)]
    else:
        pairs = [(i, (i + 4 * step) % 16) for i in range(16)]
    return lax.ppermute(value, "replica", pairs)


def gather_pool(value, near, far):
    first, last = cat_rows([value] + [along(value, near, k) for k in (1, 2, 3)])
    first_below, last_above = along(first, far, 1), along(last, far, 3)
    last_below, first_above = along(last, far, 1), along(first, far, 3)
    first_far, last_far = along(first_below, far, 1), along(last_above, far, 3)
    return [first, first_below, first_far, first_above, last, last_below, last_far, last_above]


def in_section_one(value, step):
    pairs = [(4 + i, 4 + (i ^ step)) for i in range(4)]
    return lax.ppermute(value, ("section", "tensor"), pairs)


def local(
    inner_input,
    gate_input,
    residual,
    projection,
    state_proj,
    step_proj,
    conv_weight,
    conv_bias,
    decay_rate,
    skip_gain,
    step_bias,
    norm_gain,
    state_codes,
    state_scales,
    conv_window,
    cache_codes,
    cache_scales,
    cache_window,
    finished,
    refill_source,
):
    section = lax.axis_index("section")
    column = lax.axis_index("tensor")
    replica = lax.axis_index("replica")
    where = jnp.stack([section, column]).astype(jnp.int32)

    rows = cache_window.shape[1]
    blocks = STEPS // 2
    codes = cache_codes[0].reshape(rows, STATES, 2, blocks, CB).transpose(2, 0, 3, 1, 4)
    windows = cache_window[0].reshape(rows, 3, 2, blocks, CB).transpose(2, 0, 3, 1, 4)
    room = CB - cache_scales.shape[2]
    tail = jnp.pad(cache_scales[0], ((0, 0), (0, room)))[None, :, None]
    cached = jnp.concatenate(
        [
            codes.reshape(2, rows, blocks, CODE_LANES),
            windows.reshape(2, rows, blocks, 3 * CB),
            jnp.broadcast_to(tail, (2, rows, blocks, CB)),
        ],
        axis=3,
    ).reshape(2, rows, blocks * GROUP)
    pieces = gather_pool(cached[0], "y", "z") + gather_pool(cached[1], "z", "y")

    sources = lax.dynamic_slice_in_dim(refill_source, replica * SLOTS, SLOTS, 1).reshape(ROWS)
    ended = finished.reshape(ROWS) == 1
    taken = (sources >= 0) & ended
    owner, within = sources // rows, sources % rows
    up = (replica // 4 - owner // 4) % 4
    over = (replica % 4 - owner % 4) % 4
    places = jnp.stack([(up * 4 + over) * rows + within, (over * 4 + up) * rows + within])
    onehot = (
        (places[:, :, None] == jnp.arange(POOL)[None, None, :]) & taken[None, :, None]
    ).astype(BF16)
    keep = jnp.broadcast_to(~ended[:, None], (ROWS, LANES)).astype(F32)

    gains = jnp.concatenate(
        [conv_weight[0], conv_bias, decay_rate[0], skip_gain, step_bias], axis=0
    )

    small = (onehot, keep, gains, where, residual.reshape(ROWS, FEATURES))
    flat = (
        step_proj[0],
        inner_input.reshape(ROWS, CHANNELS),
        gate_input.reshape(ROWS, CHANNELS),
        conv_window[0].transpose(1, 0, 2).reshape(ROWS, CHANNELS),
    )
    small, flat, codes, weight, pieces[0] = lax.optimization_barrier(
        (small, flat, state_codes[0], projection[0], pieces[0])
    )
    onehot, keep, gains, where, residual_rows = small
    store = fill_call("hold_store", list(flat))
    states = unfold_call(codes, state_scales[0])
    column_share = lax.dynamic_slice_in_dim(residual_rows, column * SHARE, SHARE, 1)
    pool = pool_call(pieces)

    conv_args = (store, onehot, keep, gains, state_proj[0], pool)
    conv_out, terms, cached_scales = conv_call(conv_args)
    all_terms = [terms] + [exchange(terms, k) for k in (1, 2, 3)]
    shared = (onehot, keep, cached_scales, pool)
    layer = (states, store, gains)
    own, *sends = scan_call(False, where, all_terms, (*shared, conv_out, *layer, weight))
    arrived = [exchange(value, k + 1) for k, value in enumerate(sends)]
    first = add_call((column_share, own, *arrived))

    got = lax.ppermute(first, ("section", "tensor"), [(i, 4 + (i ^ 2)) for i in range(4)])
    got_a = in_section_one(got, 2)
    got_b = in_section_one(got, 1)
    got_c = in_section_one(got_a, 1)

    conv_out, terms, window_out, stream_out = project_call(
        where, (got, got_a, got_b, got_c), (first, norm_gain[None], *conv_args, weight)
    )
    all_terms = [terms] + [exchange(terms, k) for k in (1, 2, 3)]
    scan_out, codes_out, scales_out = scan_call(
        True, where, all_terms, (*shared, conv_out, *layer)
    )
    return (
        stream_out.reshape(TICKS, SLOTS, SHARE),
        scan_out.reshape(1, TICKS, SLOTS, CHANNELS),
        codes_out[None],
        scales_out[None, :, : state_scales.shape[2]],
        window_out.transpose(1, 0, 2)[None],
    )


def solution(mesh):
    return jax.shard_map(
        local,
        mesh=mesh,
        in_specs=(
            P(None, "replica", "tensor"),
            P(None, "replica", "tensor"),
            P(None, "replica", None),
            P("section", "tensor", None),
            P("section", "tensor", None),
            P("section", None, "tensor"),
            P("section", None, "tensor"),
            P("section", "tensor"),
            P("section", None, "tensor"),
            P("section", "tensor"),
            P("section", "tensor"),
            P(),
            P("section", "replica", None, "tensor"),
            P("section", "replica", "tensor"),
            P("section", "replica", None, "tensor"),
            P("section", "replica", None, "tensor"),
            P("section", "replica", "tensor"),
            P("section", "replica", None, "tensor"),
            P(None, "replica"),
            P(),
        ),
        out_specs=(
            P(None, "replica", "tensor"),
            P("section", None, "replica", "tensor"),
            P("section", "replica", None, "tensor"),
            P("section", "replica", "tensor"),
            P("section", "replica", None, "tensor"),
        ),
        check_vma=False,
    )
```

profile of v0, /device:TPU:6, one launch (start us, length us, event | category | flops | bytes accessed | tf_op | source)
XLA Modules:
  0.0 147.7 jit_solution(13493053658083594542)
XLA Ops:
  1.7 1.1 reshape_squeeze.6
  4.5 3.1 %collective-permute-start.2 = (bf16[4,20480]{1,0:T(4,128)(2,1)S(1)}, bf16[4,20480]{1,0:T(4,128)(2,1)S(1)}, u32[]{:S(2)}, u32[]{:S(2)}) collective-permute-start(bf16[4,20480]{1,0:T(4,128)(2,1)S(1)} %bitcast.49), channel_id=1, source_target_pairs={{0,12},{4,0},{8,4},{12,8},{16,28},{20,16},{24,20},{28,24},{32,44},... | collective-permute-start | bytes 491528 | tf_op jit(solution)/shard_map/ppermute | solution.py:505
  8.3 4.1 %collective-permute-start.11 = (bf16[4,20480]{1,0:T(4,128)(2,1)S(1)}, bf16[4,20480]{1,0:T(4,128)(2,1)S(1)}, u32[]{:S(2)}, u32[]{:S(2)}) collective-permute-start(bf16[4,20480]{1,0:T(4,128)(2,1)S(1)} %bitcast.53), channel_id=1, source_target_pairs={{0,48},{4,52},{8,56},{12,60},{16,0},{20,4},{24,8},{28,12},{32,16},... | collective-permute-start | bytes 491528 | tf_op jit(solution)/shard_map/ppermute | solution.py:505
  12.4 1.3 collective-permute-start.9
  14.5 4.3 %collective-permute-done.11.d = bf16[4,20480]{1,0:T(4,128)(2,1)S(1)} collective-permute-done((bf16[4,20480]{1,0:T(4,128)(2,1)S(1)}, bf16[4,20480]{1,0:T(4,128)(2,1)S(1)}, u32[]{:S(2)}, u32[]{:S(2)}) %collective-permute-start.11) | collective-permute-done | bytes 163872 | tf_op jit(solution)/shard_map/ppermute | solution.py:505
  18.8 1.0 collective-permute-start
  19.7 1.0 collective-permute-done.10.c
  20.8 1.4 collective-permute-done.9.b
  22.4 1.1 collective-permute-start.14
  23.5 1.0 collective-permute-start.12
  24.7 2.5 %copy.32 = bf16[1,2048,288]{2,1,0:T(8,128)(2,1)} copy(bf16[1,2048,288]{1,2,0:T(8,128)(2,1)} %param.24) | data formatting | bytes 2359296 | tf_op args[4]
  27.5 2.3 %collective-permute-start.16 = (bf16[16,10240]{1,0:T(8,128)(2,1)S(1)}, bf16[16,10240]{1,0:T(8,128)(2,1)S(1)}, u32[]{:S(2)}, u32[]{:S(2)}) collective-permute-start(bf16[16,10240]{1,0:T(8,128)(2,1)S(1)} %get-tuple-element.48.refs_12_), channel_id=1, source_target_pairs={{0,12},{4,0},{8,4},{12,8},{16,28},{20,16},{24,20},{28,24},{32,44},... | collective-permute-start | bytes 983048 | tf_op jit(solution)/shard_map/ppermute | solution.py:505
  30.1 2.5 %collective-permute-start.5 = (bf16[16,10240]{1,0:T(8,128)(2,1)S(1)}, bf16[16,10240]{1,0:T(8,128)(2,1)S(1)}, u32[]{:S(2)}, u32[]{:S(2)}) collective-permute-start(bf16[16,10240]{1,0:T(8,128)(2,1)S(1)} %get-tuple-element.45.refs_0_), channel_id=1, source_target_pairs={{0,48},{4,52},{8,56},{12,60},{16,0},{20,4},{24,8},{28,12},{32,16},... | collective-permute-start | bytes 983048 | tf_op jit(solution)/shard_map/ppermute | solution.py:505
  33.8 1.2 collective-permute-done.12.refs_9_
  35.0 2.9 %collective-permute-start.7 = (bf16[16,10240]{1,0:T(8,128)(2,1)S(1)}, bf16[16,10240]{1,0:T(8,128)(2,1)S(1)}, u32[]{:S(2)}, u32[]{:S(2)}) collective-permute-start(bf16[16,10240]{1,0:T(8,128)(2,1)S(1)} %get-tuple-element.46.refs_4_), channel_id=1, source_target_pairs={{0,48},{4,52},{8,56},{12,60},{16,0},{20,4},{24,8},{28,12},{32,16},... | collective-permute-start | bytes 983048 | tf_op jit(solution)/shard_map/ppermute | solution.py:505
  38.8 2.0 %collective-permute-done.15.refs_13_ = bf16[16,10240]{1,0:T(8,128)(2,1)S(1)} collective-permute-done((bf16[16,10240]{1,0:T(8,128)(2,1)S(1)}, bf16[16,10240]{1,0:T(8,128)(2,1)S(1)}, u32[]{:S(2)}, u32[]{:S(2)}) %collective-permute-start.15) | collective-permute-done | bytes 327712 | tf_op jit(solution)/shard_map/ppermute | solution.py:505
  40.8 3.2 %collective-permute-start.17 = (bf16[16,10240]{1,0:T(8,128)(2,1)S(1)}, bf16[16,10240]{1,0:T(8,128)(2,1)S(1)}, u32[]{:S(2)}, u32[]{:S(2)}) collective-permute-start(bf16[16,10240]{1,0:T(8,128)(2,1)S(1)} %collective-permute-done.16.refs_15_), channel_id=1, source_target_pairs={{0,12},{4,0},{8,4},{12,8},{16,28},{20,16},{24,20},{28,24},{32,44},... | collective-permute-start | bytes 983048 | tf_op jit(solution)/shard_map/ppermute | solution.py:505
  44.0 1.6 %collective-permute-done.7.refs_7_ = bf16[16,10240]{1,0:T(8,128)(2,1)S(1)} collective-permute-done((bf16[16,10240]{1,0:T(8,128)(2,1)S(1)}, bf16[16,10240]{1,0:T(8,128)(2,1)S(1)}, u32[]{:S(2)}, u32[]{:S(2)}) %collective-permute-start.7) | collective-permute-done | bytes 327712 | tf_op jit(solution)/shard_map/ppermute | solution.py:505
  45.6 2.7 %collective-permute-start.8 = (bf16[16,10240]{1,0:T(8,128)(2,1)S(1)}, bf16[16,10240]{1,0:T(8,128)(2,1)S(1)}, u32[]{:S(2)}, u32[]{:S(2)}) collective-permute-start(bf16[16,10240]{1,0:T(8,128)(2,1)S(1)} %collective-permute-done.7.refs_7_), channel_id=1, source_target_pairs={{0,48},{4,52},{8,56},{12,60},{16,0},{20,4},{24,8},{28,12},{32,16},... | collective-permute-start | bytes 983048 | tf_op jit(solution)/shard_map/ppermute | solution.py:505
  48.6 1.2 copy-done.9
  49.9 1.0 copy-done.12
  50.8 1.0 copy-done.13
  51.8 1.0 copy-done.14
  53.6 2.7 %collective-permute-done.4.refs_2_ = bf16[16,10240]{1,0:T(8,128)(2,1)S(1)} collective-permute-done((bf16[16,10240]{1,0:T(8,128)(2,1)S(1)}, bf16[16,10240]{1,0:T(8,128)(2,1)S(1)}, u32[]{:S(2)}, u32[]{:S(2)}) %collective-permute-start.4) | collective-permute-done | bytes 327712 | tf_op jit(solution)/shard_map/ppermute | solution.py:505
  56.2 2.1 %pool_rows.1.pool.refs_8_ = bf16[4,64,10240]{2,1,0:T(8,128)(2,1)S(1)} custom-call(bf16[16,10240]{1,0:T(8,128)(2,1)S(1)} %get-tuple-element.45.refs_0_, bf16[16,10240]{1,0:T(8,128)(2,1)S(1)} %collective-permute-done.3.refs_1_, bf16[16,10240]{1,0:T(8,128)(2,1)S(1)} %collective-permute-done.4.refs_2_, bf16[16,10240]{1,0:T(8,128)(2,1)S(1)} %collective-permute-done.5.refs_3_, ...), custom_call_target="tpu_custom_call" | custom-call | flops 1 | bytes 1 | tf_op jit(solution)/shard_map/pool_rows/pallas_call | solution.py:61
  58.3 1.1 conv_terms.1
  59.5 1.2 copy-done.1
  62.4 1.0 collective-permute-start.18
  63.5 1.6 %copy-done.8 = bf16[1,32,16,2048]{3,2,1,0:T(8,128)(2,1)S(1)} copy-done((bf16[1,32,16,2048]{3,2,1,0:T(8,128)(2,1)S(1)}, bf16[1,32,16,2048]{3,2,1,0:T(8,128)(2,1)}, u32[]{:S(2)}) %copy-start.8) | copy-done | bytes 2097176
  65.1 2.2 %unfold_states.1.refs_10_ = f32[16,32,2048]{2,1,0:T(8,128)S(1)} custom-call(bf16[32,16,2048]{2,1,0:T(8,128)(2,1)S(1)} %bitcast.47, bf16[32,16]{1,0:T(8,128)(2,1)S(1)} %bitcast.60), custom_call_target="tpu_custom_call" | custom-call | flops 1 | bytes 1 | tf_op jit(solution)/shard_map/unfold_states/pallas_call | solution.py:61
  67.8 11.9 %scan_gate_project.1 = (f32[96,1024]{1,0:T(8,128)S(1)}, bf16[96,1024]{1,0:T(8,128)(2,1)}, bf16[96,1024]{1,0:T(8,128)(2,1)}, bf16[96,1024]{1,0:T(8,128)(2,1)}) custom-call(s32[2]{0:T(128)S(1)} %pad_add_fusion.1.refs_0_.where, bf16[96,288]{1,0:T(8,128)(2,1)S(1)} %get-tuple-element.49.refs_1_, bf16[96,288]{1,0:T(8,128)(2,1)} %collective-permute-done.18.refs_2_, ...), custom_call_target="tpu_custom_call" | custom-call | flops 1 | bytes 1 | tf_op jit(solution)/shard_map/scan_gate_project/pallas_call | solution.py:61
  81.3 1.0 collective-permute-start.23
  82.3 6.1 %collective-permute-done.22.b = bf16[96,1024]{1,0:T(8,128)(2,1)} collective-permute-done((bf16[96,1024]{1,0:T(8,128)(2,1)}, bf16[96,1024]{1,0:T(8,128)(2,1)}, u32[]{:S(2)}, u32[]{:S(2)}) %collective-permute-start.22) | collective-permute-done | bytes 196640 | tf_op jit(solution)/shard_map/ppermute | solution.py:497
  88.5 3.4 %collective-permute-done.23.c = bf16[96,1024]{1,0:T(8,128)(2,1)} collective-permute-done((bf16[96,1024]{1,0:T(8,128)(2,1)}, bf16[96,1024]{1,0:T(8,128)(2,1)}, u32[]{:S(2)}, u32[]{:S(2)}) %collective-permute-start.23) | collective-permute-done | bytes 196640 | tf_op jit(solution)/shard_map/ppermute | solution.py:497
  91.9 1.0 copy-done.16
  92.9 1.1 add_residual.1.first
  94.0 1.3 collective-permute-start.24
  95.3 8.8 %collective-permute-done.24.s_own = bf16[96,1024]{1,0:T(8,128)(2,1)S(1)} collective-permute-done((bf16[96,1024]{1,0:T(8,128)(2,1)S(1)}, bf16[96,1024]{1,0:T(8,128)(2,1)S(1)}, u32[]{:S(2)}, u32[]{:S(2)}) %collective-permute-start.24) | collective-permute-done | bytes 196640 | tf_op jit(solution)/shard_map/ppermute | solution.py:605
  104.2 1.9 %collective-permute-start.25 = (bf16[96,1024]{1,0:T(8,128)(2,1)S(1)}, bf16[96,1024]{1,0:T(8,128)(2,1)S(1)}, u32[]{:S(2)}, u32[]{:S(2)}) collective-permute-start(bf16[96,1024]{1,0:T(8,128)(2,1)S(1)} %collective-permute-done.24.s_own), channel_id=1, source_target_pairs={{64,66},{65,67},{66,64},{67,65},{68,70},{69,71},{70,68},{71,69},{7... | collective-permute-start | bytes 589832 | tf_op jit(solution)/shard_map/ppermute | solution.py:518
  106.1 1.9 %collective-permute-start.26 = (bf16[96,1024]{1,0:T(8,128)(2,1)S(1)}, bf16[96,1024]{1,0:T(8,128)(2,1)S(1)}, u32[]{:S(2)}, u32[]{:S(2)}) collective-permute-start(bf16[96,1024]{1,0:T(8,128)(2,1)S(1)} %collective-permute-done.24.s_own), channel_id=1, source_target_pairs={{64,65},{65,64},{66,67},{67,66},{68,69},{69,68},{70,71},{71,70},{7... | collective-permute-start | bytes 589832 | tf_op jit(solution)/shard_map/ppermute | solution.py:518
  108.0 4.2 %collective-permute-done.25.s_a = bf16[96,1024]{1,0:T(8,128)(2,1)S(1)} collective-permute-done((bf16[96,1024]{1,0:T(8,128)(2,1)S(1)}, bf16[96,1024]{1,0:T(8,128)(2,1)S(1)}, u32[]{:S(2)}, u32[]{:S(2)}) %collective-permute-start.25) | collective-permute-done | bytes 196640 | tf_op jit(solution)/shard_map/ppermute | solution.py:518
  112.2 1.9 %collective-permute-start.27 = (bf16[96,1024]{1,0:T(8,128)(2,1)S(1)}, bf16[96,1024]{1,0:T(8,128)(2,1)S(1)}, u32[]{:S(2)}, u32[]{:S(2)}) collective-permute-start(bf16[96,1024]{1,0:T(8,128)(2,1)S(1)} %collective-permute-done.25.s_a), channel_id=1, source_target_pairs={{64,65},{65,64},{66,67},{67,66},{68,69},{69,68},{70,71},{71,70},{7... | collective-permute-start | bytes 589832 | tf_op jit(solution)/shard_map/ppermute | solution.py:518
  115.6 2.5 %copy-done.3 = bf16[4,64,10240]{2,1,0:T(8,128)(2,1)S(1)} copy-done((bf16[4,64,10240]{2,1,0:T(8,128)(2,1)S(1)}, bf16[4,64,10240]{2,1,0:T(8,128)(2,1)}, u32[]{:S(2)}) %copy-start.3) | copy-done | bytes 5242904
  118.7 10.9 %norm_project_conv.1 = (f32[96,2048]{1,0:T(8,128)S(1)}, bf16[96,288]{1,0:T(8,128)(2,1)S(1)}, bf16[3,32,2048]{2,1,0:T(8,128)(2,1)}, bf16[96,1024]{1,0:T(8,128)(2,1)}) custom-call(s32[2]{0:T(128)S(1)} %copy-done.24, bf16[96,1024]{1,0:T(8,128)(2,1)S(1)} %collective-permute-done.24.s_own, bf16[96,1024]{1,0:T(8,128)(2,1)S(1)} %collective-permute-done.25.s_a, ...), custom_call_target="tpu_custom_call" | custom-call | flops 1 | bytes 1 | tf_op jit(solution)/shard_map/norm_project_conv/pallas_call | solution.py:61
  129.7 1.7 %collective-permute-start.29 = (bf16[96,288]{1,0:T(8,128)(2,1)S(1)}, bf16[96,288]{1,0:T(8,128)(2,1)S(1)}, u32[]{:S(2)}, u32[]{:S(2)}) collective-permute-start(bf16[96,288]{1,0:T(8,128)(2,1)S(1)} %get-tuple-element.59.refs_1_), channel_id=1, source_target_pairs={{0,2},{1,3},{2,0},{3,1},{4,6},{5,7},{6,4},{7,5},{8,10},{9,11},{10,... | collective-permute-start | bytes 165896 | tf_op jit(solution)/shard_map/ppermute | solution.py:497
  131.5 2.4 %collective-permute-done.30.refs_4_ = bf16[96,288]{1,0:T(8,128)(2,1)S(1)} collective-permute-done((bf16[96,288]{1,0:T(8,128)(2,1)S(1)}, bf16[96,288]{1,0:T(8,128)(2,1)S(1)}, u32[]{:S(2)}, u32[]{:S(2)}) %collective-permute-start.30) | collective-permute-done | bytes 55328 | tf_op jit(solution)/shard_map/ppermute | solution.py:497
  133.9 1.9 %collective-permute-done.29.refs_3_ = bf16[96,288]{1,0:T(8,128)(2,1)S(1)} collective-permute-done((bf16[96,288]{1,0:T(8,128)(2,1)S(1)}, bf16[96,288]{1,0:T(8,128)(2,1)S(1)}, u32[]{:S(2)}, u32[]{:S(2)}) %collective-permute-start.29) | collective-permute-done | bytes 55328 | tf_op jit(solution)/shard_map/ppermute | solution.py:497
  135.8 11.2 %scan_final.1 = (bf16[96,2048]{1,0:T(8,128)(2,1)}, bf16[32,16,2048]{2,1,0:T(8,128)(2,1)}, bf16[32,128]{1,0:T(8,128)(2,1)S(1)}) custom-call(s32[2]{0:T(128)S(1)} %copy-done.24, bf16[96,288]{1,0:T(8,128)(2,1)S(1)} %get-tuple-element.59.refs_1_, bf16[96,288]{1,0:T(8,128)(2,1)S(1)} %collective-permute-done.28.refs_2_, ...), custom_call_target="tpu_custom_call" | custom-call | flops 1 | bytes 1 | tf_op jit(solution)/shard_map/scan_final/pallas_call | solution.py:61
  (119 shorter events, 14.8 us)
Async XLA Ops:
  0.6 47.9 %copy-start = (bf16[3,32,4096]{2,1,0:T(8,128)(2,1)S(1)}, bf16[3,32,4096]{2,1,0:T(8,128)(2,1)}, u32[]{:S(2)}) copy-start(bf16[3,32,4096]{2,1,0:T(8,128)(2,1)} %param.22) | copy-start | bytes 2359300
  0.6 13.0 %copy-start.31 = (s32[3,32]{1,0:T(4,128)S(1)}, s32[3,32]{1,0:T(4,128)}, u32[]{:S(2)}) copy-start(s32[3,32]{1,0:T(4,128)} %param.38) | copy-start | bytes 1156
  4.3 22.9 %copy-start.25 = (f32[1,16,2048]{2,1,0:T(8,128)S(1)}, f32[1,16,2048]{2,1,0:T(8,128)}, u32[]{:S(2)}) copy-start(f32[1,16,2048]{2,1,0:T(8,128)} %param.28) | copy-start | bytes 393220
  4.3 22.9 %copy-start.26 = (f32[1,4,2048]{2,1,0:T(4,128)S(1)}, f32[1,4,2048]{2,1,0:T(4,128)}, u32[]{:S(2)}) copy-start(f32[1,4,2048]{2,1,0:T(4,128)} %param.26) | copy-start | bytes 98308
  4.3 22.9 %copy-start.27 = (f32[1,2048]{1,0:T(1,128)S(1)}, f32[1,2048]{1,0:T(1,128)}, u32[]{:S(2)}) copy-start(f32[1,2048]{1,0:T(1,128)} %param.27) | copy-start | bytes 24580
  4.3 22.9 %copy-start.28 = (f32[1,2048]{1,0:T(1,128)S(1)}, f32[1,2048]{1,0:T(1,128)}, u32[]{:S(2)}) copy-start(f32[1,2048]{1,0:T(1,128)} %param.29) | copy-start | bytes 24580
  4.3 22.9 %copy-start.29 = (f32[1,2048]{1,0:T(1,128)S(1)}, f32[1,2048]{1,0:T(1,128)}, u32[]{:S(2)}) copy-start(f32[1,2048]{1,0:T(1,128)} %param.30) | copy-start | bytes 24580
  4.5 23.1 %collective-permute-start.2 = (bf16[4,20480]{1,0:T(4,128)(2,1)S(1)}, bf16[4,20480]{1,0:T(4,128)(2,1)S(1)}, u32[]{:S(2)}, u32[]{:S(2)}) collective-permute-start(bf16[4,20480]{1,0:T(4,128)(2,1)S(1)} %bitcast.49), channel_id=1, source_target_pairs={{0,12},{4,0},{8,4},{12,8},{16,28},{20,16},{24,20},{28,24},{32,44},... | collective-permute-start | bytes 491528 | tf_op jit(solution)/shard_map/ppermute | solution.py:505
  7.5 22.3 %collective-permute-start.1 = (bf16[4,20480]{1,0:T(4,128)(2,1)S(1)}, bf16[4,20480]{1,0:T(4,128)(2,1)S(1)}, u32[]{:S(2)}, u32[]{:S(2)}) collective-permute-start(bf16[4,20480]{1,0:T(4,128)(2,1)S(1)} %bitcast.50), channel_id=1, source_target_pairs={{0,8},{4,12},{8,0},{12,4},{16,24},{20,28},{24,16},{28,20},{32,40},... | collective-permute-start | bytes 491528 | tf_op jit(solution)/shard_map/ppermute | solution.py:505
  8.3 10.5 %collective-permute-start.11 = (bf16[4,20480]{1,0:T(4,128)(2,1)S(1)}, bf16[4,20480]{1,0:T(4,128)(2,1)S(1)}, u32[]{:S(2)}, u32[]{:S(2)}) collective-permute-start(bf16[4,20480]{1,0:T(4,128)(2,1)S(1)} %bitcast.53), channel_id=1, source_target_pairs={{0,48},{4,52},{8,56},{12,60},{16,0},{20,4},{24,8},{28,12},{32,16},... | collective-permute-start | bytes 491528 | tf_op jit(solution)/shard_map/ppermute | solution.py:505
  12.4 8.4 %collective-permute-start.10 = (bf16[4,20480]{1,0:T(4,128)(2,1)S(1)}, bf16[4,20480]{1,0:T(4,128)(2,1)S(1)}, u32[]{:S(2)}, u32[]{:S(2)}) collective-permute-start(bf16[4,20480]{1,0:T(4,128)(2,1)S(1)} %bitcast.54), channel_id=1, source_target_pairs={{0,32},{4,36},{8,40},{12,44},{16,48},{20,52},{24,56},{28,60},{32,0... | collective-permute-start | bytes 491528 | tf_op jit(solution)/shard_map/ppermute | solution.py:505
  12.4 9.8 %collective-permute-start.9 = (bf16[4,20480]{1,0:T(4,128)(2,1)S(1)}, bf16[4,20480]{1,0:T(4,128)(2,1)S(1)}, u32[]{:S(2)}, u32[]{:S(2)}) collective-permute-start(bf16[4,20480]{1,0:T(4,128)(2,1)S(1)} %bitcast.55), channel_id=1, source_target_pairs={{0,16},{4,20},{8,24},{12,28},{16,32},{20,36},{24,40},{28,44},{32,4... | collective-permute-start | bytes 491528 | tf_op jit(solution)/shard_map/ppermute | solution.py:505
  18.8 11.1 %collective-permute-start = (bf16[4,20480]{1,0:T(4,128)(2,1)S(1)}, bf16[4,20480]{1,0:T(4,128)(2,1)S(1)}, u32[]{:S(2)}, u32[]{:S(2)}) collective-permute-start(bf16[4,20480]{1,0:T(4,128)(2,1)S(1)} %bitcast.51), channel_id=1, source_target_pairs={{0,4},{4,8},{8,12},{12,0},{16,20},{20,24},{24,28},{28,16},{32,36},... | collective-permute-start | bytes 491528 | tf_op jit(solution)/shard_map/ppermute | solution.py:505
  22.4 26.1 %copy-start.17 = (bf16[16,10240]{1,0:T(8,128)(2,1)}, bf16[16,10240]{1,0:T(8,128)(2,1)S(1)}, u32[]{:S(2)}) copy-start(bf16[16,10240]{1,0:T(8,128)(2,1)S(1)} %get-tuple-element.47.refs_8_) | copy-start | bytes 983044
  22.4 26.1 %copy-start.19 = (bf16[16,10240]{1,0:T(8,128)(2,1)}, bf16[16,10240]{1,0:T(8,128)(2,1)S(1)}, u32[]{:S(2)}) copy-start(bf16[16,10240]{1,0:T(8,128)(2,1)S(1)} %get-tuple-element.48.refs_12_) | copy-start | bytes 983044
  22.4 10.7 %collective-permute-start.14 = (bf16[16,10240]{1,0:T(8,128)(2,1)S(1)}, bf16[16,10240]{1,0:T(8,128)(2,1)S(1)}, u32[]{:S(2)}, u32[]{:S(2)}) collective-permute-start(bf16[16,10240]{1,0:T(8,128)(2,1)S(1)} %get-tuple-element.47.refs_8_), channel_id=1, source_target_pairs={{0,12},{4,0},{8,4},{12,8},{16,28},{20,16},{24,20},{28,24},{32,44},... | collective-permute-start | bytes 983048 | tf_op jit(solution)/shard_map/ppermute | solution.py:505
  23.5 11.5 %collective-permute-start.12 = (bf16[16,10240]{1,0:T(8,128)(2,1)S(1)}, bf16[16,10240]{1,0:T(8,128)(2,1)}, u32[]{:S(2)}, u32[]{:S(2)}) collective-permute-start(bf16[16,10240]{1,0:T(8,128)(2,1)S(1)} %get-tuple-element.47.refs_8_), channel_id=1, source_target_pairs={{0,4},{4,8},{8,12},{12,0},{16,20},{20,24},{24,28},{28,16},{32,36},... | collective-permute-start | bytes 983048 | tf_op jit(solution)/shard_map/ppermute | solution.py:505
  27.5 11.2 %collective-permute-start.16 = (bf16[16,10240]{1,0:T(8,128)(2,1)S(1)}, bf16[16,10240]{1,0:T(8,128)(2,1)S(1)}, u32[]{:S(2)}, u32[]{:S(2)}) collective-permute-start(bf16[16,10240]{1,0:T(8,128)(2,1)S(1)} %get-tuple-element.48.refs_12_), channel_id=1, source_target_pairs={{0,12},{4,0},{8,4},{12,8},{16,28},{20,16},{24,20},{28,24},{32,44},... | collective-permute-start | bytes 983048 | tf_op jit(solution)/shard_map/ppermute | solution.py:505
  29.9 10.9 %collective-permute-start.15 = (bf16[16,10240]{1,0:T(8,128)(2,1)S(1)}, bf16[16,10240]{1,0:T(8,128)(2,1)S(1)}, u32[]{:S(2)}, u32[]{:S(2)}) collective-permute-start(bf16[16,10240]{1,0:T(8,128)(2,1)S(1)} %get-tuple-element.48.refs_12_), channel_id=1, source_target_pairs={{0,4},{4,8},{8,12},{12,0},{16,20},{20,24},{24,28},{28,16},{32,36},... | collective-permute-start | bytes 983048 | tf_op jit(solution)/shard_map/ppermute | solution.py:505
  30.1 10.7 %collective-permute-start.5 = (bf16[16,10240]{1,0:T(8,128)(2,1)S(1)}, bf16[16,10240]{1,0:T(8,128)(2,1)S(1)}, u32[]{:S(2)}, u32[]{:S(2)}) collective-permute-start(bf16[16,10240]{1,0:T(8,128)(2,1)S(1)} %get-tuple-element.45.refs_0_), channel_id=1, source_target_pairs={{0,48},{4,52},{8,56},{12,60},{16,0},{20,4},{24,8},{28,12},{32,16},... | collective-permute-start | bytes 983048 | tf_op jit(solution)/shard_map/ppermute | solution.py:505
  33.8 10.2 %collective-permute-start.3 = (bf16[16,10240]{1,0:T(8,128)(2,1)S(1)}, bf16[16,10240]{1,0:T(8,128)(2,1)S(1)}, u32[]{:S(2)}, u32[]{:S(2)}) collective-permute-start(bf16[16,10240]{1,0:T(8,128)(2,1)S(1)} %get-tuple-element.45.refs_0_), channel_id=1, source_target_pairs={{0,16},{4,20},{8,24},{12,28},{16,32},{20,36},{24,40},{28,44},{32,4... | collective-permute-start | bytes 983048 | tf_op jit(solution)/shard_map/ppermute | solution.py:505
  35.0 10.6 %collective-permute-start.7 = (bf16[16,10240]{1,0:T(8,128)(2,1)S(1)}, bf16[16,10240]{1,0:T(8,128)(2,1)S(1)}, u32[]{:S(2)}, u32[]{:S(2)}) collective-permute-start(bf16[16,10240]{1,0:T(8,128)(2,1)S(1)} %get-tuple-element.46.refs_4_), channel_id=1, source_target_pairs={{0,48},{4,52},{8,56},{12,60},{16,0},{20,4},{24,8},{28,12},{32,16},... | collective-permute-start | bytes 983048 | tf_op jit(solution)/shard_map/ppermute | solution.py:505
  38.8 14.8 %collective-permute-start.6 = (bf16[16,10240]{1,0:T(8,128)(2,1)S(1)}, bf16[16,10240]{1,0:T(8,128)(2,1)S(1)}, u32[]{:S(2)}, u32[]{:S(2)}) collective-permute-start(bf16[16,10240]{1,0:T(8,128)(2,1)S(1)} %get-tuple-element.46.refs_4_), channel_id=1, source_target_pairs={{0,16},{4,20},{8,24},{12,28},{16,32},{20,36},{24,40},{28,44},{32,4... | collective-permute-start | bytes 983048 | tf_op jit(solution)/shard_map/ppermute | solution.py:505
  40.8 12.8 %collective-permute-start.13 = (bf16[16,10240]{1,0:T(8,128)(2,1)}, bf16[16,10240]{1,0:T(8,128)(2,1)S(1)}, u32[]{:S(2)}, u32[]{:S(2)}) collective-permute-start(bf16[16,10240]{1,0:T(8,128)(2,1)} %collective-permute-done.12.refs_9_), channel_id=1, source_target_pairs={{0,4},{4,8},{8,12},{12,0},{16,20},{20,24},{24,28},{28,16},{32,36},... | collective-permute-start | bytes 983048 | tf_op jit(solution)/shard_map/ppermute | solution.py:505
  40.8 12.7 %collective-permute-start.17 = (bf16[16,10240]{1,0:T(8,128)(2,1)S(1)}, bf16[16,10240]{1,0:T(8,128)(2,1)S(1)}, u32[]{:S(2)}, u32[]{:S(2)}) collective-permute-start(bf16[16,10240]{1,0:T(8,128)(2,1)S(1)} %collective-permute-done.16.refs_15_), channel_id=1, source_target_pairs={{0,12},{4,0},{8,4},{12,8},{16,28},{20,16},{24,20},{28,24},{32,44},... | collective-permute-start | bytes 983048 | tf_op jit(solution)/shard_map/ppermute | solution.py:505
  44.0 12.2 %collective-permute-start.4 = (bf16[16,10240]{1,0:T(8,128)(2,1)S(1)}, bf16[16,10240]{1,0:T(8,128)(2,1)S(1)}, u32[]{:S(2)}, u32[]{:S(2)}) collective-permute-start(bf16[16,10240]{1,0:T(8,128)(2,1)S(1)} %collective-permute-done.3.refs_1_), channel_id=1, source_target_pairs={{0,16},{4,20},{8,24},{12,28},{16,32},{20,36},{24,40},{28,44},{32,4... | collective-permute-start | bytes 983048 | tf_op jit(solution)/shard_map/ppermute | solution.py:505
  45.6 10.6 %collective-permute-start.8 = (bf16[16,10240]{1,0:T(8,128)(2,1)S(1)}, bf16[16,10240]{1,0:T(8,128)(2,1)S(1)}, u32[]{:S(2)}, u32[]{:S(2)}) collective-permute-start(bf16[16,10240]{1,0:T(8,128)(2,1)S(1)} %collective-permute-done.7.refs_7_), channel_id=1, source_target_pairs={{0,48},{4,52},{8,56},{12,60},{16,0},{20,4},{24,8},{28,12},{32,16},... | collective-permute-start | bytes 983048 | tf_op jit(solution)/shard_map/ppermute | solution.py:505
  48.4 19.0 %copy-start.23 = (s32[2]{0:T(128)}, s32[2]{0:T(128)S(1)}, u32[]{:S(2)}) copy-start(s32[2]{0:T(128)S(1)} %pad_add_fusion.1.refs_0_.where) | copy-start | bytes 28
  52.8 3.4 %copy-start.20 = (bf16[16,10240]{1,0:T(8,128)(2,1)S(1)}, bf16[16,10240]{1,0:T(8,128)(2,1)}, u32[]{:S(2)}) copy-start(bf16[16,10240]{1,0:T(8,128)(2,1)} %copy-done.19) | copy-start | bytes 983044
  52.8 3.4 %copy-start.22 = (bf16[16,10240]{1,0:T(8,128)(2,1)S(1)}, bf16[16,10240]{1,0:T(8,128)(2,1)}, u32[]{:S(2)}) copy-start(bf16[16,10240]{1,0:T(8,128)(2,1)} %copy-done.21) | copy-start | bytes 983044
  53.5 4.8 %copy-start.6 = (bf16[1,2048,288]{2,1,0:T(8,128)(2,1)S(1)}, bf16[1,2048,288]{2,1,0:T(8,128)(2,1)}, u32[]{:S(2)}) copy-start(bf16[1,2048,288]{2,1,0:T(8,128)(2,1)} %copy.32) | copy-start | bytes 3538948
  58.3 5.1 %copy-start.30 = (bf16[1,32,16]{1,2,0:T(8,128)(2,1)S(1)}, bf16[1,32,16]{1,2,0:T(8,128)(2,1)}, u32[]{:S(2)}) copy-start(bf16[1,32,16]{1,2,0:T(8,128)(2,1)} %param.33) | copy-start | bytes 3076
  61.6 5.8 %collective-permute-start.20 = (bf16[96,288]{1,0:T(8,128)(2,1)S(1)}, bf16[96,288]{1,0:T(8,128)(2,1)S(1)}, u32[]{:S(2)}, u32[]{:S(2)}) collective-permute-start(bf16[96,288]{1,0:T(8,128)(2,1)S(1)} %get-tuple-element.49.refs_1_), channel_id=1, source_target_pairs={{0,3},{1,2},{2,1},{3,0},{4,7},{5,6},{6,5},{7,4},{8,11},{9,10},{10,... | collective-permute-start | bytes 165896 | tf_op jit(solution)/shard_map/ppermute | solution.py:497
  61.6 5.8 %collective-permute-start.19 = (bf16[96,288]{1,0:T(8,128)(2,1)S(1)}, bf16[96,288]{1,0:T(8,128)(2,1)}, u32[]{:S(2)}, u32[]{:S(2)}) collective-permute-start(bf16[96,288]{1,0:T(8,128)(2,1)S(1)} %get-tuple-element.49.refs_1_), channel_id=1, source_target_pairs={{0,2},{1,3},{2,0},{3,1},{4,6},{5,7},{6,4},{7,5},{8,10},{9,11},{10,... | collective-permute-start | bytes 165896 | tf_op jit(solution)/shard_map/ppermute | solution.py:497
  62.4 5.0 %collective-permute-start.18 = (bf16[96,288]{1,0:T(8,128)(2,1)S(1)}, bf16[96,288]{1,0:T(8,128)(2,1)}, u32[]{:S(2)}, u32[]{:S(2)}) collective-permute-start(bf16[96,288]{1,0:T(8,128)(2,1)S(1)} %get-tuple-element.49.refs_1_), channel_id=1, source_target_pairs={{0,1},{1,0},{2,3},{3,2},{4,5},{5,4},{6,7},{7,6},{8,9},{9,8},{10,11... | collective-permute-start | bytes 165896 | tf_op jit(solution)/shard_map/ppermute | solution.py:497
  67.3 12.3 %copy-start.4 = (f32[16,32,2048]{2,1,0:T(8,128)}, f32[16,32,2048]{2,1,0:T(8,128)S(1)}, u32[]{:S(2)}) copy-start(f32[16,32,2048]{2,1,0:T(8,128)S(1)} %unfold_states.1.refs_10_) | copy-start | bytes 12582916
  80.4 1.9 %collective-permute-start.21 = (bf16[96,1024]{1,0:T(8,128)(2,1)}, bf16[96,1024]{1,0:T(8,128)(2,1)S(1)}, u32[]{:S(2)}, u32[]{:S(2)}) collective-permute-start(bf16[96,1024]{1,0:T(8,128)(2,1)} %get-tuple-element.55), channel_id=1, source_target_pairs={{0,1},{1,0},{2,3},{3,2},{4,5},{5,4},{6,7},{7,6},{8,9},{9,8},{10,11... | collective-permute-start | bytes 589832 | tf_op jit(solution)/shard_map/ppermute | solution.py:497
  80.4 8.0 %collective-permute-start.22 = (bf16[96,1024]{1,0:T(8,128)(2,1)}, bf16[96,1024]{1,0:T(8,128)(2,1)}, u32[]{:S(2)}, u32[]{:S(2)}) collective-permute-start(bf16[96,1024]{1,0:T(8,128)(2,1)} %get-tuple-element.56), channel_id=1, source_target_pairs={{0,2},{1,3},{2,0},{3,1},{4,6},{5,7},{6,4},{7,5},{8,10},{9,11},{10,... | collective-permute-start | bytes 589832 | tf_op jit(solution)/shard_map/ppermute | solution.py:497
  81.3 10.6 %collective-permute-start.23 = (bf16[96,1024]{1,0:T(8,128)(2,1)}, bf16[96,1024]{1,0:T(8,128)(2,1)}, u32[]{:S(2)}, u32[]{:S(2)}) collective-permute-start(bf16[96,1024]{1,0:T(8,128)(2,1)} %get-tuple-element.57), channel_id=1, source_target_pairs={{0,3},{1,2},{2,1},{3,0},{4,7},{5,6},{6,5},{7,4},{8,11},{9,10},{10,... | collective-permute-start | bytes 589832 | tf_op jit(solution)/shard_map/ppermute | solution.py:497
  82.3 33.3 %copy-start.7 = (bf16[1,2048,288]{2,1,0:T(8,128)(2,1)S(1)}, bf16[1,2048,288]{2,1,0:T(8,128)(2,1)}, u32[]{:S(2)}) copy-start(bf16[1,2048,288]{2,1,0:T(8,128)(2,1)} %copy.32) | copy-start | bytes 3538948
  94.0 10.1 %collective-permute-start.24 = (bf16[96,1024]{1,0:T(8,128)(2,1)S(1)}, bf16[96,1024]{1,0:T(8,128)(2,1)S(1)}, u32[]{:S(2)}, u32[]{:S(2)}) collective-permute-start(bf16[96,1024]{1,0:T(8,128)(2,1)S(1)} %add_residual.1.first), channel_id=1, source_target_pairs={{0,66},{1,67},{2,64},{3,65},{4,70},{5,71},{6,68},{7,69},{8,74},{9,... | collective-permute-start | bytes 589832 | tf_op jit(solution)/shard_map/ppermute | solution.py:605
  104.2 8.1 %collective-permute-start.25 = (bf16[96,1024]{1,0:T(8,128)(2,1)S(1)}, bf16[96,1024]{1,0:T(8,128)(2,1)S(1)}, u32[]{:S(2)}, u32[]{:S(2)}) collective-permute-start(bf16[96,1024]{1,0:T(8,128)(2,1)S(1)} %collective-permute-done.24.s_own), channel_id=1, source_target_pairs={{64,66},{65,67},{66,64},{67,65},{68,70},{69,71},{70,68},{71,69},{7... | collective-permute-start | bytes 589832 | tf_op jit(solution)/shard_map/ppermute | solution.py:518
  106.1 8.8 %collective-permute-start.26 = (bf16[96,1024]{1,0:T(8,128)(2,1)S(1)}, bf16[96,1024]{1,0:T(8,128)(2,1)S(1)}, u32[]{:S(2)}, u32[]{:S(2)}) collective-permute-start(bf16[96,1024]{1,0:T(8,128)(2,1)S(1)} %collective-permute-done.24.s_own), channel_id=1, source_target_pairs={{64,65},{65,64},{66,67},{67,66},{68,69},{69,68},{70,71},{71,70},{7... | collective-permute-start | bytes 589832 | tf_op jit(solution)/shard_map/ppermute | solution.py:518
  112.2 3.3 %collective-permute-start.27 = (bf16[96,1024]{1,0:T(8,128)(2,1)S(1)}, bf16[96,1024]{1,0:T(8,128)(2,1)S(1)}, u32[]{:S(2)}, u32[]{:S(2)}) collective-permute-start(bf16[96,1024]{1,0:T(8,128)(2,1)S(1)} %collective-permute-done.25.s_a), channel_id=1, source_target_pairs={{64,65},{65,64},{66,67},{67,66},{68,69},{69,68},{70,71},{71,70},{7... | collective-permute-start | bytes 589832 | tf_op jit(solution)/shard_map/ppermute | solution.py:518
  118.7 17.2 %copy-start.5 = (f32[16,32,2048]{2,1,0:T(8,128)S(1)}, f32[16,32,2048]{2,1,0:T(8,128)}, u32[]{:S(2)}) copy-start(f32[16,32,2048]{2,1,0:T(8,128)} %copy-done.4) | copy-start | bytes 12582916
  129.6 4.3 %collective-permute-start.30 = (bf16[96,288]{1,0:T(8,128)(2,1)S(1)}, bf16[96,288]{1,0:T(8,128)(2,1)S(1)}, u32[]{:S(2)}, u32[]{:S(2)}) collective-permute-start(bf16[96,288]{1,0:T(8,128)(2,1)S(1)} %get-tuple-element.59.refs_1_), channel_id=1, source_target_pairs={{0,3},{1,2},{2,1},{3,0},{4,7},{5,6},{6,5},{7,4},{8,11},{9,10},{10,... | collective-permute-start | bytes 165896 | tf_op jit(solution)/shard_map/ppermute | solution.py:497
  129.7 6.1 %collective-permute-start.29 = (bf16[96,288]{1,0:T(8,128)(2,1)S(1)}, bf16[96,288]{1,0:T(8,128)(2,1)S(1)}, u32[]{:S(2)}, u32[]{:S(2)}) collective-permute-start(bf16[96,288]{1,0:T(8,128)(2,1)S(1)} %get-tuple-element.59.refs_1_), channel_id=1, source_target_pairs={{0,2},{1,3},{2,0},{3,1},{4,6},{5,7},{6,4},{7,5},{8,10},{9,11},{10,... | collective-permute-start | bytes 165896 | tf_op jit(solution)/shard_map/ppermute | solution.py:497
  131.5 4.4 %collective-permute-start.28 = (bf16[96,288]{1,0:T(8,128)(2,1)S(1)}, bf16[96,288]{1,0:T(8,128)(2,1)S(1)}, u32[]{:S(2)}, u32[]{:S(2)}) collective-permute-start(bf16[96,288]{1,0:T(8,128)(2,1)S(1)} %get-tuple-element.59.refs_1_), channel_id=1, source_target_pairs={{0,1},{1,0},{2,3},{3,2},{4,5},{5,4},{6,7},{7,6},{8,9},{9,8},{10,11... | collective-permute-start | bytes 165896 | tf_op jit(solution)/shard_map/ppermute | solution.py:497
  (15 other events, 23.2 us)
where the time goes:
time: 148 us
  waiting for transfers between devices  43.1 us (29%)
  Pallas kernels  41.6 us (28%)
  starting transfers between devices  38.6 us (26%)
  local copies, waits for them, and re-layouts  22 us (15%)
    pallas_call x8, Pallas kernels, call(): pl.pallas_call(kernel, in_specs=in_specs, out_specs=[HELD] * len(out_shap...  41.2 us
    ppermute x18, starting transfers between devices, along(): return lax.ppermute(value, 'replica', pairs)  25.9 us
    unnamed x70, local copies, waits for them, and re-layouts  17.6 us
    ppermute x18, waiting for transfers between devices, along(): return lax.ppermute(value, 'replica', pairs)  15.5 us
    ppermute x9, waiting for transfers between devices, exchange(): return lax.ppermute(value, 'tensor', [(i, i ^ step) for i in range(4)])  13.9 us
    ppermute x1, waiting for transfers between devices, local(): lax.ppermute(first, ('section', 'tensor'), [(i, 4 + (i ^ 2)) for i in ran...  8.83 us
    ppermute x3, starting transfers between devices, in_section_one(): return lax.ppermute(value, ('section', 'tensor'), pairs)  5.74 us
    ppermute x9, starting transfers between devices, exchange(): return lax.ppermute(value, 'tensor', [(i, i ^ step) for i in range(4)])  5.66 us
  transfers between devices with their start and end apart: 31, of which 16 were waited for; matrix products, arithmetic and copies ran while one was open for 3% of the time, Pallas kernels for 2%

commit v1 on v0

--- a/solution.py
+++ b/solution.py
@@ -31,23 +31,6 @@
 COST = pl.CostEstimate(flops=1, transcendentals=0, bytes_accessed=1)
 
 
-def cat_kernel(a, b, c, d, first, last):
-    for block, out in enumerate((first, last)):
-        cols = slice(block * GROUP, (block + 1) * GROUP)
-        out[...] = jnp.concatenate([a[:, cols], b[:, cols], c[:, cols], d[:, cols]], axis=0)
-
-
-def cat_rows(pieces):
-    shape = jax.ShapeDtypeStruct((16, GROUP), BF16)
-    return pl.pallas_call(
-        cat_kernel,
-        out_shape=[shape, shape],
-        compiler_params=pltpu.CompilerParams(vmem_limit_bytes=48 * MIB),
-        cost_estimate=COST,
-        name="cat_rows",
-    )(*pieces)
-
-
 HELD = pl.BlockSpec(memory_space=pltpu.VMEM)
 SCALARS = pl.BlockSpec(memory_space=pltpu.SMEM)
 ANYWHERE = pl.BlockSpec(memory_space=pltpu.HBM)
@@ -57,17 +40,46 @@
     return pltpu.VMEM(shape, dtype)
 
 
-def call(kernel, name, mebibytes, in_specs, out_shape, scratch, args):
+def call(kernel, name, mebibytes, in_specs, out_shape, scratch, args, out_specs=None):
+    if out_specs is None:
+        out_specs = [HELD] * len(out_shape) if isinstance(out_shape, list) else HELD
     return pl.pallas_call(
         kernel,
         in_specs=in_specs,
-        out_specs=[HELD] * len(out_shape) if isinstance(out_shape, list) else HELD,
+        out_specs=out_specs,
         out_shape=out_shape,
         scratch_shapes=scratch,
         compiler_params=pltpu.CompilerParams(vmem_limit_bytes=mebibytes * MIB),
         cost_estimate=COST,
         name=name,
     )(*args)
+
+
+def cat_kernel(a, b, c, d, first, last, held, left):
+    copies = []
+    for block, out in enumerate((first, last)):
+        cols = slice(block * GROUP, (block + 1) * GROUP)
+        held[block] = jnp.concatenate(
+            [a[:, cols], b[:, cols], c[:, cols], d[:, cols]], axis=0
+        )
+        copies.append(pltpu.make_async_copy(held.at[block], out, left.at[block]))
+        copies[-1].start()
+    for copy in copies:
+        copy.wait()
+
+
+def cat_rows(pieces):
+    shape = jax.ShapeDtypeStruct((16, GROUP), BF16)
+    return call(
+        cat_kernel,
+        "cat_rows",
+        48,
+        [HELD] * 4,
+        [shape, shape],
+        [pltpu.VMEM((2, 16, GROUP), BF16), pltpu.SemaphoreType.DMA((2,))],
+        pieces,
+        [ANYWHERE] * 2,
+    )
 
 
 def silu(x):
@@ -111,6 +123,82 @@
         held((rows, arrays[0].shape[1]), BF16),
         [pltpu.SemaphoreType.DMA((len(arrays),))],
         arrays,
+    )
+
+
+def arrange_kernel(codes, windows, scales, first, last, code_rows, window_rows):
+    rows = codes.shape[0]
+    for part in range(CHANNELS // LANES):
+        code_rows[part] = (
+            codes[:, :, part * LANES : (part + 1) * LANES]
+            .astype(F32)
+            .reshape(rows * STATES, LANES)
+        )
+    for k in range(3):
+        window_rows[k * 8 : k * 8 + rows] = windows[k].astype(F32)
+    for block in range(STEPS):
+        out = (first, last)[block // 2]
+        base = block % 2 * GROUP
+        cols = slice(block * CB, (block + 1) * CB)
+        for n in range(STATES):
+            for part in range(CB // LANES):
+                lanes = slice(base + n * CB + part * LANES, base + n * CB + (part + 1) * LANES)
+                out[:, lanes] = code_rows[
+                    block * (CB // LANES) + part, pl.ds(n, rows, stride=STATES), :
+                ].astype(BF16)
+        base += CODE_LANES
+        for k in range(3):
+            out[:, base + k * CB : base + (k + 1) * CB] = window_rows[
+                k * 8 : k * 8 + rows, cols
+            ].astype(BF16)
+        out[:, base + 3 * CB : base + 4 * CB] = jnp.zeros((rows, CB), BF16)
+        out[:, base + 3 * CB : base + 3 * CB + scales.shape[1]] = scales[...]
+
+
+def arrange_call(codes, windows, scales):
+    rows = codes.shape[0]
+    half = jax.ShapeDtypeStruct((rows, STEPS // 2 * GROUP), BF16)
+    return call(
+        arrange_kernel,
+        "arrange_rows",
+        60,
+        [HELD] * 3,
+        [half, half],
+        [
+            pltpu.VMEM((CHANNELS // LANES, rows * STATES, LANES), F32),
+            pltpu.VMEM((24, CHANNELS), F32),
+        ],
+        [codes, windows, scales],
+    )
+
+
+def plan_kernel(where, sources, ended, onehot, keep):
+    source, over = sources[...], ended[...]
+    owner, within = source >> 2, source & 3
+    z = (where[2] - (owner >> 2)) & 3
+    y = (where[3] - (owner & 3)) & 3
+    taken = (source >= 0) & (over == 1)
+    row = lax.broadcasted_iota(jnp.int32, (POOL, LANES), 0)
+    for half, place in enumerate((z * 16 + y * 4 + within, y * 16 + z * 4 + within)):
+        place = jnp.where(taken, place, -1)
+        chosen = jnp.where(row == place, 1.0, 0.0).astype(F32)
+        onehot[half] = chosen.T[:ROWS].astype(BF16)
+    stays = jnp.where(over == 1, 0.0, 1.0).astype(F32)
+    keep[...] = jnp.broadcast_to(stays, (LANES, LANES)).T[:ROWS]
+
+
+def plan_call(where, sources, ended):
+    return call(
+        plan_kernel,
+        "plan_rows",
+        14,
+        [SCALARS, HELD, HELD],
+        [
+            jax.ShapeDtypeStruct((2, ROWS, POOL), BF16),
+            jax.ShapeDtypeStruct((ROWS, LANES), F32),
+        ],
+        [],
+        [where, sources, ended],
     )
 
 
@@ -154,7 +242,7 @@
     return call(
         pool_kernel,
         "pool_rows",
-        14,
+        50,
         [ANYWHERE] * (4 * STEPS),
         held((STEPS, POOL, GROUP), BF16),
         [pltpu.SemaphoreType.DMA((4 * STEPS,))],
@@ -180,13 +268,14 @@
             total = total + gains[TAP_ROW + k : TAP_ROW + k + 1, cols] * taps[k]
         outs.append(silu(total))
         stays = keep[rows, :1] > 0.5
-        past = [
-            jnp.where(stays, taps[k + 1], fetched[rows, k * CB : (k + 1) * CB]) for k in range(3)
-        ]
+        past = [jnp.where(stays, taps[k + 1], fetched(k, rows)) for k in range(3)]
     return jnp.concatenate(outs, axis=0), past
 
 
-def conv_kernel(store, onehot, keep, gains, proj, pool, conv_out, terms, scales):
+def conv_kernel(
+    store, onehot, keep, gains, proj, pool, conv_out, terms, scales, taken_out, taken, left
+):
+    copies = []
     total = jnp.zeros((ROWS, TERMS), F32)
     for block in range(STEPS):
         cols = slice(block * CB, (block + 1) * CB)
@@ -195,11 +284,23 @@
         )
         if block == 0:
             scales[...] = fetched[:, 3 * CB : 3 * CB + LANES]
+        for k in range(3):
+            taken[block, k] = fetched[:, k * CB : (k + 1) * CB].astype(BF16)
+        copies.append(
+            pltpu.make_async_copy(taken.at[block], taken_out.at[block], left.at[block])
+        )
+        copies[-1].start()
         inputs = store[INPUT_ROWS : INPUT_ROWS + ROWS, cols]
-        conv, _ = conv_block(inputs, store, fetched, keep, gains, cols)
+        conv, _ = conv_block(
+            inputs, store, lambda k, rows: fetched[rows, k * CB : (k + 1) * CB], keep, gains, cols
+        )
         conv_out[:, cols] = conv
-        total = total + jnp.dot(conv.astype(BF16), proj[cols], preferred_element_type=F32)
+        total = total + lax.dot_general(
+            conv.astype(BF16), proj[:, cols], (((1,), (1,)), ((), ())), preferred_element_type=F32
+        )
     terms[...] = total.astype(BF16)
+    for copy in copies:
+        copy.wait()
 
 
 def conv_call(args):
@@ -212,9 +313,11 @@
             jax.ShapeDtypeStruct((ROWS, CHANNELS), F32),
             jax.ShapeDtypeStruct((ROWS, TERMS), BF16),
             jax.ShapeDtypeStruct((ROWS, LANES), F32),
+            jax.ShapeDtypeStruct((STEPS, 3, ROWS, CB), BF16),
         ],
-        [],
+        [pltpu.VMEM((STEPS, 3, ROWS, CB), BF16), pltpu.SemaphoreType.DMA((STEPS,))],
         args,
+        [HELD] * 3 + [ANYWHERE],
     )
 
 
@@ -224,45 +327,32 @@
     s_a,
     s_b,
     s_c,
-    first,
     gain,
     store,
-    onehot,
     keep,
     gains,
     proj,
-    pool,
+    taken,
     big,
     conv_out,
     terms,
     win_out,
-    stream_out,
     values,
     normed,
     entering,
-    weight,
-    loaded,
 ):
     section, column = where[0], where[1]
-    parts = [
-        pltpu.make_async_copy(big.at[pl.ds(b * CB, CB)], weight.at[b], loaded.at[b])
-        for b in range(STEPS)
-    ]
-    for part in parts:
-        part.start()
 
     @pl.when(section == 0)
     def _():
-        stream_out[...] = first[...]
         entering[...] = store[INPUT_ROWS : INPUT_ROWS + ROWS]
 
     @pl.when(section == 1)
     def _():
-        values[column ^ 2] = s_own[...]
-        values[column] = s_a[...]
-        values[column ^ 3] = s_b[...]
-        values[column ^ 1] = s_c[...]
-        stream_out[...] = s_a[...]
+        values[column] = s_own[...]
+        values[column ^ 2] = s_a[...]
+        values[column ^ 1] = s_b[...]
+        values[column ^ 3] = s_c[...]
         total = jnp.zeros((ROWS, 1), F32)
         for f in range(4):
             v = values[f].astype(F32)
@@ -276,22 +366,27 @@
     total = jnp.zeros((ROWS, TERMS), F32)
     for block in range(STEPS):
         cols = slice(block * CB, (block + 1) * CB)
-        parts[block].wait()
 
         @pl.when(section == 1)
         def _():
             entering[:, cols] = lax.dot_general(
-                normed[...], weight[block], (((1,), (1,)), ((), ())), preferred_element_type=F32
+                normed[...], big[cols], (((1,), (1,)), ((), ())), preferred_element_type=F32
             ).astype(BF16)
 
-        fetched = jnp.dot(
-            onehot[block // 2], pool[block, :, CODE_LANES:], preferred_element_type=F32
-        )
-        conv, past = conv_block(entering[:, cols], store, fetched, keep, gains, cols)
+        conv, past = conv_block(
+            entering[:, cols],
+            store,
+            lambda k, rows: taken[block, k, rows].astype(F32),
+            keep,
+            gains,
+            cols,
+        )
         conv_out[:, cols] = conv
         for k in range(3):
             win_out[k, :, cols] = past[k].astype(BF16)
-        total = total + jnp.dot(conv.astype(BF16), proj[cols], preferred_element_type=F32)
+        total = total + lax.dot_general(
+            conv.astype(BF16), proj[:, cols], (((1,), (1,)), ((), ())), preferred_element_type=F32
+        )
     terms[...] = total.astype(BF16)
 
 
@@ -299,20 +394,17 @@
     return call(
         project_kernel,
         "norm_project_conv",
-        36,
-        [SCALARS] + [HELD] * (3 + len(args)) + [ANYWHERE],
+        14,
+        [SCALARS] + [HELD] * (4 + len(args)),
         [
             jax.ShapeDtypeStruct((ROWS, CHANNELS), F32),
             jax.ShapeDtypeStruct((ROWS, TERMS), BF16),
             jax.ShapeDtypeStruct((3, SLOTS, CHANNELS), BF16),
-            jax.ShapeDtypeStruct((ROWS, SHARE), BF16),
         ],
         [
             pltpu.VMEM((4, ROWS, SHARE), BF16),
             pltpu.VMEM((ROWS, FEATURES), BF16),
             pltpu.VMEM((ROWS, CHANNELS), BF16),
-            pltpu.VMEM((STEPS, CB, FEATURES), BF16),
-            pltpu.SemaphoreType.DMA((STEPS,)),
         ],
         [where, *shares, *args],
     )
@@ -328,7 +420,7 @@
         scan_out, codes_out, scales_out = take(3)
     else:
         (big,) = take(1)
-        sends = take(4)
+        kept_out, sent_out = take(2)
     entry, readout, fetched, sizes = take(4)
     if final:
         states, natural, scale_acc = take(3)
@@ -388,6 +480,7 @@
             jnp.broadcast_to(new_scale[t * SLOTS : (t + 1) * SLOTS], (SLOTS, LANES))
             for t in range(TICKS - 1)
         ]
+        stays = [keep[t * SLOTS : (t + 1) * SLOTS] > 0.5 for t in range(TICKS - 1)]
         square = jnp.zeros((SLOTS, LANES), F32)
         for n in range(STATES):
             rate = gains[DECAY_ROW + n : DECAY_ROW + n + 1, cols] * -LOG2E
@@ -398,7 +491,9 @@
                 state = jnp.exp2(size[t] * rate) * state + gain[t] * entry[n, rows]
                 total[t] = total[t] + readout[n, rows] * state
                 if t < TICKS - 1:
-                    state = keep[rows] * state + fetched[rows, lanes] * arrived_scale[t]
+                    state = jnp.where(
+                        stays[t], state, fetched[rows, lanes] * arrived_scale[t]
+                    )
             if final:
                 states[n] = state
                 square = square + state * state
@@ -426,14 +521,17 @@
 
     lax.fori_loop(0, STEPS, scan_block, 0)
     if final:
-        scales_out[...] = scale_acc[...].astype(BF16)
+        scales_out[...] = scale_acc[...].T[: CHANNELS // LANES].astype(BF16)
         return
     for copy in parts:
         copy.wait()
-    column = where[1]
-    for k, out in enumerate(sends):
-        cols = pl.ds(pl.multiple_of((column ^ k) * SHARE, SHARE), SHARE)
-        out[...] = jnp.dot(gated[...], weight[:, cols], preferred_element_type=F32).astype(out.dtype)
+    core = where[1] % 2
+    for chip in range(2):
+        for offset, out in ((core, kept_out), (1 - core, sent_out)):
+            cols = pl.ds(pl.multiple_of((2 * chip + offset) * SHARE, SHARE), SHARE)
+            out[chip] = jnp.dot(
+                gated[...], weight[:, cols], preferred_element_type=F32
+            ).astype(out.dtype)
 
 
 def scan_call(final, where, terms, args):
@@ -447,7 +545,7 @@
         out_shape = [
             jax.ShapeDtypeStruct((ROWS, CHANNELS), BF16),
             jax.ShapeDtypeStruct((SLOTS, STATES, CHANNELS), BF16),
-            jax.ShapeDtypeStruct((SLOTS, LANES), BF16),
+            jax.ShapeDtypeStruct((CHANNELS // LANES, SLOTS), BF16),
         ]
         scratch += [
             pltpu.VMEM((STATES, SLOTS, LANES), F32),
@@ -455,9 +553,10 @@
             pltpu.VMEM((SLOTS, LANES), F32),
         ]
     else:
-        out_shape = [jax.ShapeDtypeStruct((ROWS, SHARE), F32)] + [
-            jax.ShapeDtypeStruct((ROWS, SHARE), BF16)
-        ] * 3
+        out_shape = [
+            jax.ShapeDtypeStruct((2, ROWS, SHARE), F32),
+            jax.ShapeDtypeStruct((2, ROWS, SHARE), BF16),
+        ]
         scratch += [
             pltpu.VMEM((ROWS, CHANNELS), BF16),
             pltpu.VMEM((CHANNELS, FEATURES), BF16),
@@ -474,22 +573,49 @@
     )
 
 
-def add_kernel(residual, own, a, b, c, out):
-    total = residual[...].astype(F32) + (
-        own[...] + a[...].astype(F32) + b[...].astype(F32) + c[...].astype(F32)
-    )
-    out[...] = total.astype(BF16)
-
-
-def add_call(args):
-    return call(
-        add_kernel,
-        "add_residual",
+def chip_kernel(where, kept, got, same, other):
+    chip = where[1] // 2
+    for place, out in ((chip, same), (1 - chip, other)):
+        out[...] = (kept[place] + got[place].astype(F32)).astype(BF16)
+
+
+def chip_call(where, kept, got):
+    share = jax.ShapeDtypeStruct((ROWS, SHARE), BF16)
+    return call(
+        chip_kernel,
+        "sum_on_chip",
         14,
-        [HELD] * 5,
+        [SCALARS, HELD, HELD],
+        [share, share],
+        [],
+        [where, kept, got],
+    )
+
+
+def add_kernel(residual, same, other, out):
+    total = same[...].astype(F32) + other[...].astype(F32)
+    out[...] = (residual[...].astype(F32) + total).astype(BF16)
+
+
+def add_first_kernel(where, residual, same, other, stream, out):
+    @pl.when(where[0] == 0)
+    def _():
+        add_kernel(residual, same, other, out)
+
+    @pl.when(where[0] == 1)
+    def _():
+        out[...] = stream[...]
+
+
+def add_call(kernel, name, args, scalars):
+    return call(
+        kernel,
+        name,
+        14,
+        [SCALARS] * len(scalars) + [HELD] * len(args),
         [jax.ShapeDtypeStruct((ROWS, SHARE), BF16)],
         [],
-        args,
+        [*scalars, *args],
     )[0]
 
 
@@ -505,8 +631,8 @@
     return lax.ppermute(value, "replica", pairs)
 
 
-def gather_pool(value, near, far):
-    first, last = cat_rows([value] + [along(value, near, k) for k in (1, 2, 3)])
+def gather_far(near, far):
+    first, last = cat_rows(near)
     first_below, last_above = along(first, far, 1), along(last, far, 3)
     last_below, first_above = along(last, far, 1), along(first, far, 3)
     first_far, last_far = along(first_below, far, 1), along(last_above, far, 3)
@@ -543,83 +669,87 @@
     section = lax.axis_index("section")
     column = lax.axis_index("tensor")
     replica = lax.axis_index("replica")
-    where = jnp.stack([section, column]).astype(jnp.int32)
+    where = jnp.stack([section, column, replica // 4, replica % 4]).astype(jnp.int32)
 
     rows = cache_window.shape[1]
-    blocks = STEPS // 2
-    codes = cache_codes[0].reshape(rows, STATES, 2, blocks, CB).transpose(2, 0, 3, 1, 4)
-    windows = cache_window[0].reshape(rows, 3, 2, blocks, CB).transpose(2, 0, 3, 1, 4)
-    room = CB - cache_scales.shape[2]
-    tail = jnp.pad(cache_scales[0], ((0, 0), (0, room)))[None, :, None]
-    cached = jnp.concatenate(
-        [
-            codes.reshape(2, rows, blocks, CODE_LANES),
-            windows.reshape(2, rows, blocks, 3 * CB),
-            jnp.broadcast_to(tail, (2, rows, blocks, CB)),
-        ],
-        axis=3,
-    ).reshape(2, rows, blocks * GROUP)
-    pieces = gather_pool(cached[0], "y", "z") + gather_pool(cached[1], "z", "y")
-
-    sources = lax.dynamic_slice_in_dim(refill_source, replica * SLOTS, SLOTS, 1).reshape(ROWS)
-    ended = finished.reshape(ROWS) == 1
-    taken = (sources >= 0) & ended
-    owner, within = sources // rows, sources % rows
-    up = (replica // 4 - owner // 4) % 4
-    over = (replica % 4 - owner % 4) % 4
-    places = jnp.stack([(up * 4 + over) * rows + within, (over * 4 + up) * rows + within])
-    onehot = (
-        (places[:, :, None] == jnp.arange(POOL)[None, None, :]) & taken[None, :, None]
-    ).astype(BF16)
-    keep = jnp.broadcast_to(~ended[:, None], (ROWS, LANES)).astype(F32)
+    cached = arrange_call(cache_codes[0], cache_window[0].transpose(1, 0, 2), cache_scales[0])
 
     gains = jnp.concatenate(
         [conv_weight[0], conv_bias, decay_rate[0], skip_gain, step_bias], axis=0
     )
-
-    small = (onehot, keep, gains, where, residual.reshape(ROWS, FEATURES))
+    near_a = [cached[0]] + [along(cached[0], "y", k) for k in (1, 2, 3)]
+    near_b = [cached[1]] + [along(cached[1], "z", k) for k in (1, 2, 3)]
+    near_a, near_b, gains, proj = lax.optimization_barrier(
+        (near_a, near_b, gains, state_proj[0].T)
+    )
+    pieces = gather_far(near_a, "z") + gather_far(near_b, "y")
+
+    sources = lax.dynamic_slice_in_dim(refill_source, replica * SLOTS, SLOTS, 1)
+    room = ((0, 0), (0, LANES - ROWS))
+    sources = jnp.pad(sources.reshape(1, ROWS), room, constant_values=-1)
+    ended = jnp.pad(finished.reshape(1, ROWS), room)
+
+    small = (sources, ended, where, residual.reshape(ROWS, FEATURES), norm_gain[None])
     flat = (
         step_proj[0],
         inner_input.reshape(ROWS, CHANNELS),
         gate_input.reshape(ROWS, CHANNELS),
         conv_window[0].transpose(1, 0, 2).reshape(ROWS, CHANNELS),
     )
-    small, flat, codes, weight, pieces[0] = lax.optimization_barrier(
-        (small, flat, state_codes[0], projection[0], pieces[0])
-    )
-    onehot, keep, gains, where, residual_rows = small
+    small, flat, codes, weight, pieces[0], pieces[8] = lax.optimization_barrier(
+        (small, flat, state_codes[0], projection[0], pieces[0], pieces[8])
+    )
+    sources, ended, where, residual_rows, gain = small
+    onehot, keep = plan_call(where, sources, ended)
     store = fill_call("hold_store", list(flat))
     states = unfold_call(codes, state_scales[0])
     column_share = lax.dynamic_slice_in_dim(residual_rows, column * SHARE, SHARE, 1)
+    states, store, onehot, keep, pieces = lax.optimization_barrier(
+        (states, store, onehot, keep, pieces)
+    )
     pool = pool_call(pieces)
 
-    conv_args = (store, onehot, keep, gains, state_proj[0], pool)
-    conv_out, terms, cached_scales = conv_call(conv_args)
+    conv_out, terms, cached_scales, taken = conv_call(
+        (store, onehot, keep, gains, proj, pool)
+    )
     all_terms = [terms] + [exchange(terms, k) for k in (1, 2, 3)]
     shared = (onehot, keep, cached_scales, pool)
     layer = (states, store, gains)
-    own, *sends = scan_call(False, where, all_terms, (*shared, conv_out, *layer, weight))
-    arrived = [exchange(value, k + 1) for k, value in enumerate(sends)]
-    first = add_call((column_share, own, *arrived))
-
-    got = lax.ppermute(first, ("section", "tensor"), [(i, 4 + (i ^ 2)) for i in range(4)])
-    got_a = in_section_one(got, 2)
-    got_b = in_section_one(got, 1)
+    kept, sent = scan_call(False, where, all_terms, (*shared, conv_out, *layer, weight))
+
+    same, other = chip_call(where, kept, exchange(sent, 1))
+    big, same, other = lax.optimization_barrier((weight, same, other))
+    big = fill_call("hold_projection", [big])
+    other_far = lax.ppermute(other, ("section", "tensor"), [(i, (i + 4) % 8 ^ 2) for i in range(8)])
+    same_far = lax.ppermute(same, "section", [(0, 1), (1, 0)])
+    big, same_far, other_far = lax.optimization_barrier((big, same_far, other_far))
+    stream = add_call(add_kernel, "add_residual", (column_share, same_far, other_far), ())
+    other, stream = lax.optimization_barrier((other, stream))
+    got_a = in_section_one(stream, 2)
+    got_b = in_section_one(stream, 1)
     got_c = in_section_one(got_a, 1)
-
-    conv_out, terms, window_out, stream_out = project_call(
-        where, (got, got_a, got_b, got_c), (first, norm_gain[None], *conv_args, weight)
+    other = exchange(other, 2)
+
+    conv_out, terms, window_out = project_call(
+        where, (stream, got_a, got_b, got_c), (gain, store, keep, gains, proj, taken, big)
     )
     all_terms = [terms] + [exchange(terms, k) for k in (1, 2, 3)]
+    other, conv_out = lax.optimization_barrier((other, conv_out))
+    stream = add_call(
+        add_first_kernel, "add_first", (column_share, same, other, stream), (where,)
+    )
+    window_out, stream, conv_out = lax.optimization_barrier(
+        (window_out.transpose(1, 0, 2), stream, conv_out)
+    )
     scan_out, codes_out, scales_out = scan_call(
         True, where, all_terms, (*shared, conv_out, *layer)
     )
     return (
-        stream_out.reshape(TICKS, SLOTS, SHARE),
+        stream.reshape(TICKS, SLOTS, SHARE),
         scan_out.reshape(1, TICKS, SLOTS, CHANNELS),
         codes_out[None],
-        scales_out[None, :, : state_scales.shape[2]],
-        window_out.transpose(1, 0, 2)[None],
+        scales_out.T[None],
+        window_out[None],
     )
 
 

time: 148 us -> 135 us (0.912)
  waiting for transfers between devices: 43.1 us -> 23.4 us
  Pallas kernels: 41.6 us -> 48.7 us
  starting transfers between devices: 38.6 us -> 44.8 us
  local copies, waits for them, and re-layouts: 22 us -> 16.7 us
    ppermute x18, waiting for transfers between devices: 15.5 us -> 8.18 us  [along(): return lax.ppermute(value, 'replica', pairs)]
    pallas_call x10 -> x15, Pallas kernels: 41.6 us -> 48.7 us  [call(): pl.pallas_call(kernel, in_specs=in_specs, out_specs=out_specs, out_shape=...]
    ppermute x1 -> x2, waiting for transfers between devices: 8.83 us -> 2.39 us  [the longest x1 2.39 us: local(): lax.ppermute(other, ('section', 'tensor'), [(i, (i + 4) % 8 ^ 2) for i in...]
    unnamed x70 -> x61, local copies, waits for them, and re-layouts: 17.6 us -> 11.2 us
    ppermute x9 -> x8, waiting for transfers between devices: 13.9 us -> 7.57 us  [exchange(): return lax.ppermute(value, 'tensor', [(i, i ^ step) for i in range(4)])]
    ppermute x18, starting transfers between devices: 25.9 us -> 31.2 us  [along(): return lax.ppermute(value, 'replica', pairs)]
    concatenate x1, local copies, waits for them, and re-layouts: 0.26 us -> 2.57 us  [local(): jnp.concatenate([conv_weight[0], conv_bias, decay_rate[0], skip_gain, ste...]
    ppermute x1 -> x2, starting transfers between devices: 1.29 us -> 3.42 us  [the longest x1 1.91 us: local(): same_far = lax.ppermute(same, 'section', [(0, 1), (1, 0)])]
  transfers between devices with their start and end apart: 31 -> 31, of which waited for: 16 -> 14; matrix products, arithmetic and copies ran while one was open for 3% -> 5% of each run, Pallas kernels for 2% -> 12%
where the time goes in v1:
time: 135 us
  Pallas kernels  48.7 us (36%)
  starting transfers between devices  44.8 us (33%)
  waiting for transfers between devices  23.4 us (17%)
  local copies, waits for them, and re-layouts  16.7 us (12%)
    pallas_call x15, Pallas kernels, call(): pl.pallas_call(kernel, in_specs=in_specs, out_specs=out_specs, out_shape=...  48.7 us
    ppermute x18, starting transfers between devices, along(): return lax.ppermute(value, 'replica', pairs)  31.2 us
    unnamed x61, local copies, waits for them, and re-layouts  11.2 us
    ppermute x18, waiting for transfers between devices, along(): return lax.ppermute(value, 'replica', pairs)  8.18 us
    ppermute x8, waiting for transfers between devices, exchange(): return lax.ppermute(value, 'tensor', [(i, i ^ step) for i in range(4)])  7.57 us
    ppermute x3, starting transfers between devices, in_section_one(): return lax.ppermute(value, ('section', 'tensor'), pairs)  5.79 us
    ppermute x3, waiting for transfers between devices, in_section_one(): return lax.ppermute(value, ('section', 'tensor'), pairs)  5.26 us
    ppermute x8, starting transfers between devices, exchange(): return lax.ppermute(value, 'tensor', [(i, i ^ step) for i in range(4)])  4.41 us
  transfers between devices with their start and end apart: 31, of which 14 were waited for; matrix products, arithmetic and copies ran while one was open for 5% of the time, Pallas kernels for 12%

profile of v1, /device:TPU:6, one launch (start us, length us, event | category | flops | bytes accessed | tf_op | source)
XLA Modules:
  0.0 134.8 jit_solution(4303496079985344865)
XLA Ops:
  0.7 2.1 %arrange_rows.1 = (bf16[4,20480]{1,0:T(4,128)(2,1)}, bf16[4,20480]{1,0:T(4,128)(2,1)}) custom-call(bf16[4,16,2048]{2,1,0:T(8,128)(2,1)} %bitcast.47, bf16[3,4,2048]{2,1,0:T(4,128)(2,1)} %bitcast.50, bf16[4,16]{1,0:T(4,128)(2,1)} %bitcast.52), custom_call_target="tpu_custom_call" | custom-call | flops 1 | bytes 1 | tf_op jit(solution)/shard_map/arrange_rows/pallas_call | solution.py:46
  2.7 3.0 %collective-permute-start.2 = (bf16[4,20480]{1,0:T(4,128)(2,1)}, bf16[4,20480]{1,0:T(4,128)(2,1)S(1)}, u32[]{:S(2)}, u32[]{:S(2)}) collective-permute-start(bf16[4,20480]{1,0:T(4,128)(2,1)} %get-tuple-element.85.a), channel_id=1, source_target_pairs={{0,12},{4,0},{8,4},{12,8},{16,28},{20,16},{24,20},{28,24},{32,44},... | collective-permute-start | bytes 491528 | tf_op jit(solution)/shard_map/ppermute | solution.py:631
  6.4 1.0 collective-permute-start
  7.3 4.0 %collective-permute-start.5 = (bf16[4,20480]{1,0:T(4,128)(2,1)}, bf16[4,20480]{1,0:T(4,128)(2,1)S(1)}, u32[]{:S(2)}, u32[]{:S(2)}) collective-permute-start(bf16[4,20480]{1,0:T(4,128)(2,1)} %get-tuple-element.90.a), channel_id=1, source_target_pairs={{0,48},{4,52},{8,56},{12,60},{16,0},{20,4},{24,8},{28,12},{32,16},... | collective-permute-start | bytes 491528 | tf_op jit(solution)/shard_map/ppermute | solution.py:631
  11.4 1.6 %collective-permute-done.2.d = bf16[4,20480]{1,0:T(4,128)(2,1)S(1)} collective-permute-done((bf16[4,20480]{1,0:T(4,128)(2,1)}, bf16[4,20480]{1,0:T(4,128)(2,1)S(1)}, u32[]{:S(2)}, u32[]{:S(2)}) %collective-permute-start.2) | collective-permute-done | bytes 163872 | tf_op jit(solution)/shard_map/ppermute | solution.py:631
  13.7 1.9 %collective-permute-start.3 = (bf16[4,20480]{1,0:T(4,128)(2,1)}, bf16[4,20480]{1,0:T(4,128)(2,1)}, u32[]{:S(2)}, u32[]{:S(2)}) collective-permute-start(bf16[4,20480]{1,0:T(4,128)(2,1)} %get-tuple-element.90.a), channel_id=1, source_target_pairs={{0,16},{4,20},{8,24},{12,28},{16,32},{20,36},{24,40},{28,44},{32,4... | collective-permute-start | bytes 491528 | tf_op jit(solution)/shard_map/ppermute | solution.py:631
  15.6 2.6 %concatenate.3.gains.refs_12_ = f32[23,2048]{1,0:T(8,128)S(1)} concatenate(f32[4,2048]{1,0:T(4,128)} %bitcast.51, f32[1,2048]{1,0:T(1,128)} %param.27, f32[16,2048]{1,0:T(8,128)} %bitcast.49, f32[1,2048]{1,0:T(1,128)} %param.29, f32[1,2048]{1,0:T(1,128)} %param.30), dimensions={0} | concatenate | bytes 376832 | tf_op jit(solution)/shard_map/concatenate | solution.py:677
  18.5 3.5 %collective-permute-done.3.b = bf16[4,20480]{1,0:T(4,128)(2,1)} collective-permute-done((bf16[4,20480]{1,0:T(4,128)(2,1)}, bf16[4,20480]{1,0:T(4,128)(2,1)}, u32[]{:S(2)}, u32[]{:S(2)}) %collective-permute-start.3) | collective-permute-done | bytes 163872 | tf_op jit(solution)/shard_map/ppermute | solution.py:631
  22.0 0.9 copy-done.19
  22.9 0.9 copy-done.21
  23.9 1.4 %cat_rows.2 = (bf16[16,10240]{1,0:T(8,128)(2,1)S(1)}, bf16[16,10240]{1,0:T(8,128)(2,1)S(1)}) custom-call(bf16[4,20480]{1,0:T(4,128)(2,1)S(1)} %copy-done.19, bf16[4,20480]{1,0:T(4,128)(2,1)} %collective-permute-done.b, bf16[4,20480]{1,0:T(4,128)(2,1)} %collective-permute-done.1.c, bf16[4,20480]{1,0:T(4,128)(2,1)S(1)} %copy-done.21), custom_call_target="tpu_custom_call" | custom-call | flops 1 | bytes 1 | tf_op jit(solution)/shard_map/cat_rows/pallas_call | solution.py:46
  25.3 1.4 %collective-permute-start.8 = (bf16[16,10240]{1,0:T(8,128)(2,1)S(1)}, bf16[16,10240]{1,0:T(8,128)(2,1)S(1)}, u32[]{:S(2)}, u32[]{:S(2)}) collective-permute-start(bf16[16,10240]{1,0:T(8,128)(2,1)S(1)} %get-tuple-element.115.refs_0_), channel_id=1, source_target_pairs={{0,48},{4,52},{8,56},{12,60},{16,0},{20,4},{24,8},{28,12},{32,16},... | collective-permute-start | bytes 983048 | tf_op jit(solution)/shard_map/ppermute | solution.py:631
  27.4 2.5 %collective-permute-start.10 = (bf16[16,10240]{1,0:T(8,128)(2,1)S(1)}, bf16[16,10240]{1,0:T(8,128)(2,1)}, u32[]{:S(2)}, u32[]{:S(2)}) collective-permute-start(bf16[16,10240]{1,0:T(8,128)(2,1)S(1)} %get-tuple-element.119.refs_4_), channel_id=1, source_target_pairs={{0,48},{4,52},{8,56},{12,60},{16,0},{20,4},{24,8},{28,12},{32,16},... | collective-permute-start | bytes 983048 | tf_op jit(solution)/shard_map/ppermute | solution.py:631
  30.0 0.9 copy-done.18
  30.9 2.0 %cat_rows.3 = (bf16[16,10240]{1,0:T(8,128)(2,1)S(1)}, bf16[16,10240]{1,0:T(8,128)(2,1)}) custom-call(bf16[4,20480]{1,0:T(4,128)(2,1)S(1)} %copy-done.18, bf16[4,20480]{1,0:T(4,128)(2,1)} %collective-permute-done.3.b, bf16[4,20480]{1,0:T(4,128)(2,1)S(1)} %collective-permute-done.4.c, bf16[4,20480]{1,0:T(4,128)(2,1)S(1)} %collective-permute-done.5.d), custom_call_target="tpu_custom_call" | custom-call | flops 1 | bytes 1 | tf_op jit(solution)/shard_map/cat_rows/pallas_call | solution.py:46
  32.9 3.7 %collective-permute-start.14 = (bf16[16,10240]{1,0:T(8,128)(2,1)S(1)}, bf16[16,10240]{1,0:T(8,128)(2,1)S(1)}, u32[]{:S(2)}, u32[]{:S(2)}) collective-permute-start(bf16[16,10240]{1,0:T(8,128)(2,1)S(1)} %get-tuple-element.123.refs_8_), channel_id=1, source_target_pairs={{0,12},{4,0},{8,4},{12,8},{16,28},{20,16},{24,20},{28,24},{32,44},... | collective-permute-start | bytes 983048 | tf_op jit(solution)/shard_map/ppermute | solution.py:631
  37.4 1.3 collective-permute-done.6.refs_1_
  38.7 3.6 %collective-permute-start.16 = (bf16[16,10240]{1,0:T(8,128)(2,1)}, bf16[16,10240]{1,0:T(8,128)(2,1)}, u32[]{:S(2)}, u32[]{:S(2)}) collective-permute-start(bf16[16,10240]{1,0:T(8,128)(2,1)} %get-tuple-element.127.refs_12_), channel_id=1, source_target_pairs={{0,12},{4,0},{8,4},{12,8},{16,28},{20,16},{24,20},{28,24},{32,44},... | collective-permute-start | bytes 983048 | tf_op jit(solution)/shard_map/ppermute | solution.py:631
  42.9 1.4 %collective-permute-done.14.refs_11_ = bf16[16,10240]{1,0:T(8,128)(2,1)S(1)} collective-permute-done((bf16[16,10240]{1,0:T(8,128)(2,1)S(1)}, bf16[16,10240]{1,0:T(8,128)(2,1)S(1)}, u32[]{:S(2)}, u32[]{:S(2)}) %collective-permute-start.14) | collective-permute-done | bytes 327712 | tf_op jit(solution)/shard_map/ppermute | solution.py:631
  44.3 3.0 %collective-permute-start.11 = (bf16[16,10240]{1,0:T(8,128)(2,1)}, bf16[16,10240]{1,0:T(8,128)(2,1)}, u32[]{:S(2)}, u32[]{:S(2)}) collective-permute-start(bf16[16,10240]{1,0:T(8,128)(2,1)} %collective-permute-done.10.refs_7_), channel_id=1, source_target_pairs={{0,48},{4,52},{8,56},{12,60},{16,0},{20,4},{24,8},{28,12},{32,16},... | collective-permute-start | bytes 983048 | tf_op jit(solution)/shard_map/ppermute | solution.py:631
  47.9 3.7 %collective-permute-start.17 = (bf16[16,10240]{1,0:T(8,128)(2,1)}, bf16[16,10240]{1,0:T(8,128)(2,1)}, u32[]{:S(2)}, u32[]{:S(2)}) collective-permute-start(bf16[16,10240]{1,0:T(8,128)(2,1)} %collective-permute-done.16.refs_15_), channel_id=1, source_target_pairs={{0,12},{4,0},{8,4},{12,8},{16,28},{20,16},{24,20},{28,24},{32,44},... | collective-permute-start | bytes 983048 | tf_op jit(solution)/shard_map/ppermute | solution.py:631
  54.0 1.3 broadcast_in_dim.12.gain
  55.4 2.2 %unfold_states.1.refs_10_ = f32[16,32,2048]{2,1,0:T(8,128)S(1)} custom-call(bf16[32,16,2048]{2,1,0:T(8,128)(2,1)S(1)} %bitcast.41, bf16[32,16]{1,0:T(8,128)(2,1)S(1)} %bitcast.46), custom_call_target="tpu_custom_call" | custom-call | flops 1 | bytes 1 | tf_op jit(solution)/shard_map/unfold_states/pallas_call | solution.py:46
  59.1 2.7 %pool_rows.1.pool.refs_8_ = bf16[4,64,10240]{2,1,0:T(8,128)(2,1)S(1)} custom-call(bf16[16,10240]{1,0:T(8,128)(2,1)} %copy-done.15, bf16[16,10240]{1,0:T(8,128)(2,1)} %collective-permute-done.6.refs_1_, bf16[16,10240]{1,0:T(8,128)(2,1)} %collective-permute-done.7.refs_2_, bf16[16,10240]{1,0:T(8,128)(2,1)} %copy-done.25, bf16[16,10240]{1,0:T(8,128)(2,1)} %copy-done.16, ...), custom_call_target="tpu_custom_call" | custom-call | flops 1 | bytes 1 | tf_op jit(solution)/shard_map/pool_rows/pallas_call | solution.py:46
  62.0 2.0 %conv_terms.1 = (f32[96,2048]{1,0:T(8,128)S(1)}, bf16[96,288]{1,0:T(8,128)(2,1)S(1)}, f32[96,128]{1,0:T(8,128)S(1)}, bf16[4,3,96,512]{3,2,1,0:T(8,128)(2,1)S(1)}) custom-call(bf16[544,2048]{1,0:T(8,128)(2,1)S(1)} %hold_store.1.store.refs_11_, bf16[2,96,64]{2,1,0:T(8,128)(2,1)S(1)} %get-tuple-element.111.onehot.refs_5_, ...), custom_call_target="tpu_custom_call" | custom-call | flops 1 | bytes 1 | tf_op jit(solution)/shard_map/conv_terms/pallas_call | solution.py:46
  64.0 1.0 copy-done.9
  65.9 1.0 collective-permute-start.18
  66.9 2.5 %collective-permute-done.20.refs_4_ = bf16[96,288]{1,0:T(8,128)(2,1)S(1)} collective-permute-done((bf16[96,288]{1,0:T(8,128)(2,1)S(1)}, bf16[96,288]{1,0:T(8,128)(2,1)S(1)}, u32[]{:S(2)}, u32[]{:S(2)}) %collective-permute-start.20) | collective-permute-done | bytes 55328 | tf_op jit(solution)/shard_map/ppermute | solution.py:623
  70.1 10.5 %scan_gate_project.1 = (f32[2,96,1024]{2,1,0:T(8,128)S(1)}, bf16[2,96,1024]{2,1,0:T(8,128)(2,1)S(1)}) custom-call(s32[4]{0:T(128)S(1)} %pad_add_fusion.where.refs_0_, bf16[96,288]{1,0:T(8,128)(2,1)S(1)} %get-tuple-element.131.refs_1_, bf16[96,288]{1,0:T(8,128)(2,1)S(1)} %collective-permute-done.18.refs_2_, ...), custom_call_target="tpu_custom_call" | custom-call | flops 1 | bytes 1 | tf_op jit(solution)/shard_map/scan_gate_project/pallas_call | solution.py:46
  80.9 1.5 %collective-permute-done.21.got = bf16[2,96,1024]{2,1,0:T(8,128)(2,1)S(1)} collective-permute-done((bf16[2,96,1024]{2,1,0:T(8,128)(2,1)S(1)}, bf16[2,96,1024]{2,1,0:T(8,128)(2,1)S(1)}, u32[]{:S(2)}, u32[]{:S(2)}) %collective-permute-start.21) | collective-permute-done | bytes 393248 | tf_op jit(solution)/shard_map/ppermute | solution.py:623
  82.4 1.3 sum_on_chip.1
  83.7 1.5 %collective-permute-start.23 = (bf16[96,1024]{1,0:T(8,128)(2,1)}, bf16[96,1024]{1,0:T(8,128)(2,1)}, u32[]{:S(2)}, u32[]{:S(2)}) collective-permute-start(bf16[96,1024]{1,0:T(8,128)(2,1)} %get-tuple-element.150), channel_id=1, source_target_pairs={{0,66},{1,67},{2,64},{3,65},{64,2},{65,3},{66,0},{67,1},{4,70},{5,... | collective-permute-start | bytes 589832 | tf_op jit(solution)/shard_map/ppermute | solution.py:723
  85.2 1.9 %collective-permute-start.22 = (bf16[96,1024]{1,0:T(8,128)(2,1)S(1)}, bf16[96,1024]{1,0:T(8,128)(2,1)}, u32[]{:S(2)}, u32[]{:S(2)}) collective-permute-start(bf16[96,1024]{1,0:T(8,128)(2,1)S(1)} %get-tuple-element.142.same), channel_id=1, source_target_pairs={{0,64},{64,0},{1,65},{65,1},{2,66},{66,2},{3,67},{67,3},{4,68},{68... | collective-permute-start | bytes 589832 | tf_op jit(solution)/shard_map/ppermute | solution.py:724
  87.1 5.8 %copy-done.3 = bf16[1,2048,4096]{2,1,0:T(8,128)(2,1)S(1)} copy-done((bf16[1,2048,4096]{2,1,0:T(8,128)(2,1)S(1)}, bf16[1,2048,4096]{2,1,0:T(8,128)(2,1)}, u32[]{:S(2)}) %copy-start.3) | copy-done | bytes 16777240
  92.9 1.2 hold_projection.1.big
  94.1 2.4 %collective-permute-done.23.other = bf16[96,1024]{1,0:T(8,128)(2,1)} collective-permute-done((bf16[96,1024]{1,0:T(8,128)(2,1)}, bf16[96,1024]{1,0:T(8,128)(2,1)}, u32[]{:S(2)}, u32[]{:S(2)}) %collective-permute-start.23) | collective-permute-done | bytes 196640 | tf_op jit(solution)/shard_map/ppermute | solution.py:723
  96.5 1.1 add_residual.1.s_own.stream
  97.6 2.0 %collective-permute-start.24 = (bf16[96,1024]{1,0:T(8,128)(2,1)S(1)}, bf16[96,1024]{1,0:T(8,128)(2,1)S(1)}, u32[]{:S(2)}, u32[]{:S(2)}) collective-permute-start(bf16[96,1024]{1,0:T(8,128)(2,1)S(1)} %add_residual.1.s_own.stream), channel_id=1, source_target_pairs={{64,66},{65,67},{66,64},{67,65},{68,70},{69,71},{70,68},{71,69},{7... | collective-permute-start | bytes 589832 | tf_op jit(solution)/shard_map/ppermute | solution.py:644
  99.5 1.9 %collective-permute-start.25 = (bf16[96,1024]{1,0:T(8,128)(2,1)S(1)}, bf16[96,1024]{1,0:T(8,128)(2,1)S(1)}, u32[]{:S(2)}, u32[]{:S(2)}) collective-permute-start(bf16[96,1024]{1,0:T(8,128)(2,1)S(1)} %add_residual.1.s_own.stream), channel_id=1, source_target_pairs={{64,65},{65,64},{66,67},{67,66},{68,69},{69,68},{70,71},{71,70},{7... | collective-permute-start | bytes 589832 | tf_op jit(solution)/shard_map/ppermute | solution.py:644
  101.5 4.2 %collective-permute-done.24.s_a = bf16[96,1024]{1,0:T(8,128)(2,1)S(1)} collective-permute-done((bf16[96,1024]{1,0:T(8,128)(2,1)S(1)}, bf16[96,1024]{1,0:T(8,128)(2,1)S(1)}, u32[]{:S(2)}, u32[]{:S(2)}) %collective-permute-start.24) | collective-permute-done | bytes 196640 | tf_op jit(solution)/shard_map/ppermute | solution.py:644
  105.7 1.9 %collective-permute-start.26 = (bf16[96,1024]{1,0:T(8,128)(2,1)S(1)}, bf16[96,1024]{1,0:T(8,128)(2,1)S(1)}, u32[]{:S(2)}, u32[]{:S(2)}) collective-permute-start(bf16[96,1024]{1,0:T(8,128)(2,1)S(1)} %collective-permute-done.24.s_a), channel_id=1, source_target_pairs={{64,65},{65,64},{66,67},{67,66},{68,69},{69,68},{70,71},{71,70},{7... | collective-permute-start | bytes 589832 | tf_op jit(solution)/shard_map/ppermute | solution.py:644
  108.0 1.0 collective-permute-done.26.s_c
  109.0 8.4 %norm_project_conv.1 = (f32[96,2048]{1,0:T(8,128)S(1)}, bf16[96,288]{1,0:T(8,128)(2,1)S(1)}, bf16[3,32,2048]{2,1,0:T(8,128)(2,1)}) custom-call(s32[4]{0:T(128)S(1)} %copy-done.24, bf16[96,1024]{1,0:T(8,128)(2,1)S(1)} %add_residual.1.s_own.stream, bf16[96,1024]{1,0:T(8,128)(2,1)S(1)} %collective-permute-done.24.s_a, ...), custom_call_target="tpu_custom_call" | custom-call | flops 1 | bytes 1 | tf_op jit(solution)/shard_map/norm_project_conv/pallas_call | solution.py:46
  118.0 1.2 collective-permute-start.29
  119.3 1.5 %add_first.1 = bf16[96,1024]{1,0:T(8,128)(2,1)} custom-call(s32[4]{0:T(128)S(1)} %copy-done.24, bf16[96,1024]{1,0:T(8,128)(2,1)S(1)} %constant_dynamic-slice_fusion.residual, bf16[96,1024]{1,0:T(8,128)(2,1)S(1)} %get-tuple-element.142.same, bf16[96,1024]{1,0:T(8,128)(2,1)S(1)} %collective-permute-done.27.other, bf16[96,1024]{1,0:T(8,128)(2,1)S(1)} %add_residual.1.s_own.stream), custom_call_target="tpu_custom_call" | custom-call | flops 1 | bytes 1 | tf_op jit(solution)/shard_map/add_first/pallas_call | solution.py:46
  120.8 0.9 collective-permute-done.30.refs_4_
  121.7 1.9 %collective-permute-done.29.refs_3_ = bf16[96,288]{1,0:T(8,128)(2,1)S(1)} collective-permute-done((bf16[96,288]{1,0:T(8,128)(2,1)S(1)}, bf16[96,288]{1,0:T(8,128)(2,1)S(1)}, u32[]{:S(2)}, u32[]{:S(2)}) %collective-permute-start.29) | collective-permute-done | bytes 55328 | tf_op jit(solution)/shard_map/ppermute | solution.py:623
  123.6 11.2 %scan_final.1 = (bf16[96,2048]{1,0:T(8,128)(2,1)}, bf16[32,16,2048]{2,1,0:T(8,128)(2,1)}, bf16[16,32]{1,0:T(8,128)(2,1)}) custom-call(s32[4]{0:T(128)S(1)} %copy-done.24, bf16[96,288]{1,0:T(8,128)(2,1)S(1)} %get-tuple-element.155.refs_1_, bf16[96,288]{1,0:T(8,128)(2,1)S(1)} %collective-permute-done.28.refs_2_, ...), custom_call_target="tpu_custom_call" | custom-call | flops 1 | bytes 1 | tf_op jit(solution)/shard_map/scan_final/pallas_call | solution.py:46
  (100 shorter events, 11.5 us)
Async XLA Ops:
  0.6 54.7 %copy-start = (bf16[3,32,4096]{2,1,0:T(8,128)(2,1)S(1)}, bf16[3,32,4096]{2,1,0:T(8,128)(2,1)}, u32[]{:S(2)}) copy-start(bf16[3,32,4096]{2,1,0:T(8,128)(2,1)} %param.22) | copy-start | bytes 2359300
  0.6 54.7 %copy-start.8 = (bf16[1,32,16,2048]{3,2,1,0:T(8,128)(2,1)S(1)}, bf16[1,32,16,2048]{3,2,1,0:T(8,128)(2,1)}, u32[]{:S(2)}) copy-start(bf16[1,32,16,2048]{3,2,1,0:T(8,128)(2,1)} %param.32) | copy-start | bytes 6291460
  2.7 10.3 %collective-permute-start.2 = (bf16[4,20480]{1,0:T(4,128)(2,1)}, bf16[4,20480]{1,0:T(4,128)(2,1)S(1)}, u32[]{:S(2)}, u32[]{:S(2)}) collective-permute-start(bf16[4,20480]{1,0:T(4,128)(2,1)} %get-tuple-element.85.a), channel_id=1, source_target_pairs={{0,12},{4,0},{8,4},{12,8},{16,28},{20,16},{24,20},{28,24},{32,44},... | collective-permute-start | bytes 491528 | tf_op jit(solution)/shard_map/ppermute | solution.py:631
  5.7 12.4 %collective-permute-start.1 = (bf16[4,20480]{1,0:T(4,128)(2,1)}, bf16[4,20480]{1,0:T(4,128)(2,1)}, u32[]{:S(2)}, u32[]{:S(2)}) collective-permute-start(bf16[4,20480]{1,0:T(4,128)(2,1)} %get-tuple-element.85.a), channel_id=1, source_target_pairs={{0,8},{4,12},{8,0},{12,4},{16,24},{20,28},{24,16},{28,20},{32,40},... | collective-permute-start | bytes 491528 | tf_op jit(solution)/shard_map/ppermute | solution.py:631
  6.4 11.8 %collective-permute-start = (bf16[4,20480]{1,0:T(4,128)(2,1)}, bf16[4,20480]{1,0:T(4,128)(2,1)}, u32[]{:S(2)}, u32[]{:S(2)}) collective-permute-start(bf16[4,20480]{1,0:T(4,128)(2,1)} %get-tuple-element.85.a), channel_id=1, source_target_pairs={{0,4},{4,8},{8,12},{12,0},{16,20},{20,24},{24,28},{28,16},{32,36},... | collective-permute-start | bytes 491528 | tf_op jit(solution)/shard_map/ppermute | solution.py:631
  7.3 10.9 %collective-permute-start.5 = (bf16[4,20480]{1,0:T(4,128)(2,1)}, bf16[4,20480]{1,0:T(4,128)(2,1)S(1)}, u32[]{:S(2)}, u32[]{:S(2)}) collective-permute-start(bf16[4,20480]{1,0:T(4,128)(2,1)} %get-tuple-element.90.a), channel_id=1, source_target_pairs={{0,48},{4,52},{8,56},{12,60},{16,0},{20,4},{24,8},{28,12},{32,16},... | collective-permute-start | bytes 491528 | tf_op jit(solution)/shard_map/ppermute | solution.py:631
  11.4 7.1 %collective-permute-start.4 = (bf16[4,20480]{1,0:T(4,128)(2,1)}, bf16[4,20480]{1,0:T(4,128)(2,1)S(1)}, u32[]{:S(2)}, u32[]{:S(2)}) collective-permute-start(bf16[4,20480]{1,0:T(4,128)(2,1)} %get-tuple-element.90.a), channel_id=1, source_target_pairs={{0,32},{4,36},{8,40},{12,44},{16,48},{20,52},{24,56},{28,60},{32,0... | collective-permute-start | bytes 491528 | tf_op jit(solution)/shard_map/ppermute | solution.py:631
  13.7 8.3 %collective-permute-start.3 = (bf16[4,20480]{1,0:T(4,128)(2,1)}, bf16[4,20480]{1,0:T(4,128)(2,1)}, u32[]{:S(2)}, u32[]{:S(2)}) collective-permute-start(bf16[4,20480]{1,0:T(4,128)(2,1)} %get-tuple-element.90.a), channel_id=1, source_target_pairs={{0,16},{4,20},{8,24},{12,28},{16,32},{20,36},{24,40},{28,44},{32,4... | collective-permute-start | bytes 491528 | tf_op jit(solution)/shard_map/ppermute | solution.py:631
  25.3 13.4 %copy-start.16 = (bf16[16,10240]{1,0:T(8,128)(2,1)}, bf16[16,10240]{1,0:T(8,128)(2,1)S(1)}, u32[]{:S(2)}) copy-start(bf16[16,10240]{1,0:T(8,128)(2,1)S(1)} %get-tuple-element.119.refs_4_) | copy-start | bytes 983044
  25.3 11.2 %collective-permute-start.8 = (bf16[16,10240]{1,0:T(8,128)(2,1)S(1)}, bf16[16,10240]{1,0:T(8,128)(2,1)S(1)}, u32[]{:S(2)}, u32[]{:S(2)}) collective-permute-start(bf16[16,10240]{1,0:T(8,128)(2,1)S(1)} %get-tuple-element.115.refs_0_), channel_id=1, source_target_pairs={{0,48},{4,52},{8,56},{12,60},{16,0},{20,4},{24,8},{28,12},{32,16},... | collective-permute-start | bytes 983048 | tf_op jit(solution)/shard_map/ppermute | solution.py:631
  26.7 12.0 %collective-permute-start.6 = (bf16[16,10240]{1,0:T(8,128)(2,1)S(1)}, bf16[16,10240]{1,0:T(8,128)(2,1)}, u32[]{:S(2)}, u32[]{:S(2)}) collective-permute-start(bf16[16,10240]{1,0:T(8,128)(2,1)S(1)} %get-tuple-element.115.refs_0_), channel_id=1, source_target_pairs={{0,16},{4,20},{8,24},{12,28},{16,32},{20,36},{24,40},{28,44},{32,4... | collective-permute-start | bytes 983048 | tf_op jit(solution)/shard_map/ppermute | solution.py:631
  27.4 14.9 %collective-permute-start.10 = (bf16[16,10240]{1,0:T(8,128)(2,1)S(1)}, bf16[16,10240]{1,0:T(8,128)(2,1)}, u32[]{:S(2)}, u32[]{:S(2)}) collective-permute-start(bf16[16,10240]{1,0:T(8,128)(2,1)S(1)} %get-tuple-element.119.refs_4_), channel_id=1, source_target_pairs={{0,48},{4,52},{8,56},{12,60},{16,0},{20,4},{24,8},{28,12},{32,16},... | collective-permute-start | bytes 983048 | tf_op jit(solution)/shard_map/ppermute | solution.py:631
  30.0 12.9 %collective-permute-start.9 = (bf16[16,10240]{1,0:T(8,128)(2,1)S(1)}, bf16[16,10240]{1,0:T(8,128)(2,1)S(1)}, u32[]{:S(2)}, u32[]{:S(2)}) collective-permute-start(bf16[16,10240]{1,0:T(8,128)(2,1)S(1)} %get-tuple-element.119.refs_4_), channel_id=1, source_target_pairs={{0,16},{4,20},{8,24},{12,28},{16,32},{20,36},{24,40},{28,44},{32,4... | collective-permute-start | bytes 983048 | tf_op jit(solution)/shard_map/ppermute | solution.py:631
  32.8 10.0 %copy-start.17 = (bf16[16,10240]{1,0:T(8,128)(2,1)}, bf16[16,10240]{1,0:T(8,128)(2,1)S(1)}, u32[]{:S(2)}) copy-start(bf16[16,10240]{1,0:T(8,128)(2,1)S(1)} %get-tuple-element.123.refs_8_) | copy-start | bytes 983044
  32.9 11.4 %collective-permute-start.14 = (bf16[16,10240]{1,0:T(8,128)(2,1)S(1)}, bf16[16,10240]{1,0:T(8,128)(2,1)S(1)}, u32[]{:S(2)}, u32[]{:S(2)}) collective-permute-start(bf16[16,10240]{1,0:T(8,128)(2,1)S(1)} %get-tuple-element.123.refs_8_), channel_id=1, source_target_pairs={{0,12},{4,0},{8,4},{12,8},{16,28},{20,16},{24,20},{28,24},{32,44},... | collective-permute-start | bytes 983048 | tf_op jit(solution)/shard_map/ppermute | solution.py:631
  36.5 10.7 %copy-start.25 = (bf16[16,10240]{1,0:T(8,128)(2,1)}, bf16[16,10240]{1,0:T(8,128)(2,1)S(1)}, u32[]{:S(2)}) copy-start(bf16[16,10240]{1,0:T(8,128)(2,1)S(1)} %collective-permute-done.8.refs_3_) | copy-start | bytes 983044
  36.5 10.7 %collective-permute-start.12 = (bf16[16,10240]{1,0:T(8,128)(2,1)S(1)}, bf16[16,10240]{1,0:T(8,128)(2,1)}, u32[]{:S(2)}, u32[]{:S(2)}) collective-permute-start(bf16[16,10240]{1,0:T(8,128)(2,1)S(1)} %get-tuple-element.123.refs_8_), channel_id=1, source_target_pairs={{0,4},{4,8},{8,12},{12,0},{16,20},{20,24},{24,28},{28,16},{32,36},... | collective-permute-start | bytes 983048 | tf_op jit(solution)/shard_map/ppermute | solution.py:631
  38.7 9.2 %collective-permute-start.16 = (bf16[16,10240]{1,0:T(8,128)(2,1)}, bf16[16,10240]{1,0:T(8,128)(2,1)}, u32[]{:S(2)}, u32[]{:S(2)}) collective-permute-start(bf16[16,10240]{1,0:T(8,128)(2,1)} %get-tuple-element.127.refs_12_), channel_id=1, source_target_pairs={{0,12},{4,0},{8,4},{12,8},{16,28},{20,16},{24,20},{28,24},{32,44},... | collective-permute-start | bytes 983048 | tf_op jit(solution)/shard_map/ppermute | solution.py:631
  42.3 16.8 %collective-permute-start.15 = (bf16[16,10240]{1,0:T(8,128)(2,1)}, bf16[16,10240]{1,0:T(8,128)(2,1)}, u32[]{:S(2)}, u32[]{:S(2)}) collective-permute-start(bf16[16,10240]{1,0:T(8,128)(2,1)} %get-tuple-element.127.refs_12_), channel_id=1, source_target_pairs={{0,4},{4,8},{8,12},{12,0},{16,20},{20,24},{24,28},{28,16},{32,36},... | collective-permute-start | bytes 983048 | tf_op jit(solution)/shard_map/ppermute | solution.py:631
  42.8 16.2 %collective-permute-start.7 = (bf16[16,10240]{1,0:T(8,128)(2,1)}, bf16[16,10240]{1,0:T(8,128)(2,1)}, u32[]{:S(2)}, u32[]{:S(2)}) collective-permute-start(bf16[16,10240]{1,0:T(8,128)(2,1)} %collective-permute-done.6.refs_1_), channel_id=1, source_target_pairs={{0,16},{4,20},{8,24},{12,28},{16,32},{20,36},{24,40},{28,44},{32,4... | collective-permute-start | bytes 983048 | tf_op jit(solution)/shard_map/ppermute | solution.py:631
  44.3 14.8 %collective-permute-start.11 = (bf16[16,10240]{1,0:T(8,128)(2,1)}, bf16[16,10240]{1,0:T(8,128)(2,1)}, u32[]{:S(2)}, u32[]{:S(2)}) collective-permute-start(bf16[16,10240]{1,0:T(8,128)(2,1)} %collective-permute-done.10.refs_7_), channel_id=1, source_target_pairs={{0,48},{4,52},{8,56},{12,60},{16,0},{20,4},{24,8},{28,12},{32,16},... | collective-permute-start | bytes 983048 | tf_op jit(solution)/shard_map/ppermute | solution.py:631
  47.2 11.8 %collective-permute-start.13 = (bf16[16,10240]{1,0:T(8,128)(2,1)}, bf16[16,10240]{1,0:T(8,128)(2,1)}, u32[]{:S(2)}, u32[]{:S(2)}) collective-permute-start(bf16[16,10240]{1,0:T(8,128)(2,1)} %collective-permute-done.12.refs_9_), channel_id=1, source_target_pairs={{0,4},{4,8},{8,12},{12,0},{16,20},{20,24},{24,28},{28,16},{32,36},... | collective-permute-start | bytes 983048 | tf_op jit(solution)/shard_map/ppermute | solution.py:631
  47.9 11.2 %collective-permute-start.17 = (bf16[16,10240]{1,0:T(8,128)(2,1)}, bf16[16,10240]{1,0:T(8,128)(2,1)}, u32[]{:S(2)}, u32[]{:S(2)}) collective-permute-start(bf16[16,10240]{1,0:T(8,128)(2,1)} %collective-permute-done.16.refs_15_), channel_id=1, source_target_pairs={{0,12},{4,0},{8,4},{12,8},{16,28},{20,16},{24,20},{28,24},{32,44},... | collective-permute-start | bytes 983048 | tf_op jit(solution)/shard_map/ppermute | solution.py:631
  55.4 27.0 %copy-start.23 = (s32[4]{0:T(128)}, s32[4]{0:T(128)S(1)}, u32[]{:S(2)}) copy-start(s32[4]{0:T(128)S(1)} %pad_add_fusion.where.refs_0_) | copy-start | bytes 52
  57.7 12.5 %copy-start.4 = (f32[16,32,2048]{2,1,0:T(8,128)}, f32[16,32,2048]{2,1,0:T(8,128)S(1)}, u32[]{:S(2)}) copy-start(f32[16,32,2048]{2,1,0:T(8,128)S(1)} %unfold_states.1.refs_10_) | copy-start | bytes 12582916
  61.9 8.2 %copy-start.2 = (bf16[4,64,10240]{2,1,0:T(8,128)(2,1)}, bf16[4,64,10240]{2,1,0:T(8,128)(2,1)S(1)}, u32[]{:S(2)}) copy-start(bf16[4,64,10240]{2,1,0:T(8,128)(2,1)S(1)} %pool_rows.1.pool.refs_8_) | copy-start | bytes 15728644
  65.0 4.4 %collective-permute-start.20 = (bf16[96,288]{1,0:T(8,128)(2,1)S(1)}, bf16[96,288]{1,0:T(8,128)(2,1)S(1)}, u32[]{:S(2)}, u32[]{:S(2)}) collective-permute-start(bf16[96,288]{1,0:T(8,128)(2,1)S(1)} %get-tuple-element.131.refs_1_), channel_id=1, source_target_pairs={{0,3},{1,2},{2,1},{3,0},{4,7},{5,6},{6,5},{7,4},{8,11},{9,10},{10,... | collective-permute-start | bytes 165896 | tf_op jit(solution)/shard_map/ppermute | solution.py:623
  65.0 5.1 %collective-permute-start.19 = (bf16[96,288]{1,0:T(8,128)(2,1)S(1)}, bf16[96,288]{1,0:T(8,128)(2,1)S(1)}, u32[]{:S(2)}, u32[]{:S(2)}) collective-permute-start(bf16[96,288]{1,0:T(8,128)(2,1)S(1)} %get-tuple-element.131.refs_1_), channel_id=1, source_target_pairs={{0,2},{1,3},{2,0},{3,1},{4,6},{5,7},{6,4},{7,5},{8,10},{9,11},{10,... | collective-permute-start | bytes 165896 | tf_op jit(solution)/shard_map/ppermute | solution.py:623
  65.9 4.3 %collective-permute-start.18 = (bf16[96,288]{1,0:T(8,128)(2,1)S(1)}, bf16[96,288]{1,0:T(8,128)(2,1)S(1)}, u32[]{:S(2)}, u32[]{:S(2)}) collective-permute-start(bf16[96,288]{1,0:T(8,128)(2,1)S(1)} %get-tuple-element.131.refs_1_), channel_id=1, source_target_pairs={{0,1},{1,0},{2,3},{3,2},{4,5},{5,4},{6,7},{7,6},{8,9},{9,8},{10,11... | collective-permute-start | bytes 165896 | tf_op jit(solution)/shard_map/ppermute | solution.py:623
  80.6 1.8 %collective-permute-start.21 = (bf16[2,96,1024]{2,1,0:T(8,128)(2,1)S(1)}, bf16[2,96,1024]{2,1,0:T(8,128)(2,1)S(1)}, u32[]{:S(2)}, u32[]{:S(2)}) collective-permute-start(bf16[2,96,1024]{2,1,0:T(8,128)(2,1)S(1)} %get-tuple-element.136), channel_id=1, source_target_pairs={{0,1},{1,0},{2,3},{3,2},{4,5},{5,4},{6,7},{7,6},{8,9},{9,8},{10,11... | collective-permute-start | bytes 1179656 | tf_op jit(solution)/shard_map/ppermute | solution.py:623
  83.7 12.8 %collective-permute-start.23 = (bf16[96,1024]{1,0:T(8,128)(2,1)}, bf16[96,1024]{1,0:T(8,128)(2,1)}, u32[]{:S(2)}, u32[]{:S(2)}) collective-permute-start(bf16[96,1024]{1,0:T(8,128)(2,1)} %get-tuple-element.150), channel_id=1, source_target_pairs={{0,66},{1,67},{2,64},{3,65},{64,2},{65,3},{66,0},{67,1},{4,70},{5,... | collective-permute-start | bytes 589832 | tf_op jit(solution)/shard_map/ppermute | solution.py:723
  85.2 11.3 %collective-permute-start.22 = (bf16[96,1024]{1,0:T(8,128)(2,1)S(1)}, bf16[96,1024]{1,0:T(8,128)(2,1)}, u32[]{:S(2)}, u32[]{:S(2)}) collective-permute-start(bf16[96,1024]{1,0:T(8,128)(2,1)S(1)} %get-tuple-element.142.same), channel_id=1, source_target_pairs={{0,64},{64,0},{1,65},{65,1},{2,66},{66,2},{3,67},{67,3},{4,68},{68... | collective-permute-start | bytes 589832 | tf_op jit(solution)/shard_map/ppermute | solution.py:724
  87.1 5.8 %copy-start.3 = (bf16[1,2048,4096]{2,1,0:T(8,128)(2,1)S(1)}, bf16[1,2048,4096]{2,1,0:T(8,128)(2,1)}, u32[]{:S(2)}) copy-start(bf16[1,2048,4096]{2,1,0:T(8,128)(2,1)} %param.23) | copy-start | bytes 50331652
  92.9 16.1 %copy-start.7 = (bf16[1,2048,288]{1,2,0:T(8,128)(2,1)S(1)}, bf16[1,2048,288]{1,2,0:T(8,128)(2,1)}, u32[]{:S(2)}) copy-start(bf16[1,2048,288]{1,2,0:T(8,128)(2,1)} %param.24) | copy-start | bytes 3538948
  92.9 16.1 %copy-start.10 = (bf16[4,3,96,512]{3,2,1,0:T(8,128)(2,1)S(1)}, bf16[4,3,96,512]{3,2,1,0:T(8,128)(2,1)}, u32[]{:S(2)}) copy-start(bf16[4,3,96,512]{3,2,1,0:T(8,128)(2,1)} %copy-done.9) | copy-start | bytes 3538948
  92.9 16.1 %copy-start.22 = (bf16[1,4096]{1,0:T(2,128)(2,1)S(1)}, bf16[1,4096]{1,0:T(2,128)(2,1)}, u32[]{:S(2)}) copy-start(bf16[1,4096]{1,0:T(2,128)(2,1)} %broadcast_in_dim.12.gain) | copy-start | bytes 24580
  92.9 16.1 %copy-start.24 = (s32[4]{0:T(128)S(1)}, s32[4]{0:T(128)}, u32[]{:S(2)}) copy-start(s32[4]{0:T(128)} %copy-done.23) | copy-start | bytes 52
  97.6 8.1 %collective-permute-start.24 = (bf16[96,1024]{1,0:T(8,128)(2,1)S(1)}, bf16[96,1024]{1,0:T(8,128)(2,1)S(1)}, u32[]{:S(2)}, u32[]{:S(2)}) collective-permute-start(bf16[96,1024]{1,0:T(8,128)(2,1)S(1)} %add_residual.1.s_own.stream), channel_id=1, source_target_pairs={{64,66},{65,67},{66,64},{67,65},{68,70},{69,71},{70,68},{71,69},{7... | collective-permute-start | bytes 589832 | tf_op jit(solution)/shard_map/ppermute | solution.py:644
  99.5 8.4 %collective-permute-start.25 = (bf16[96,1024]{1,0:T(8,128)(2,1)S(1)}, bf16[96,1024]{1,0:T(8,128)(2,1)S(1)}, u32[]{:S(2)}, u32[]{:S(2)}) collective-permute-start(bf16[96,1024]{1,0:T(8,128)(2,1)S(1)} %add_residual.1.s_own.stream), channel_id=1, source_target_pairs={{64,65},{65,64},{66,67},{67,66},{68,69},{69,68},{70,71},{71,70},{7... | collective-permute-start | bytes 589832 | tf_op jit(solution)/shard_map/ppermute | solution.py:644
  105.7 3.3 %collective-permute-start.26 = (bf16[96,1024]{1,0:T(8,128)(2,1)S(1)}, bf16[96,1024]{1,0:T(8,128)(2,1)S(1)}, u32[]{:S(2)}, u32[]{:S(2)}) collective-permute-start(bf16[96,1024]{1,0:T(8,128)(2,1)S(1)} %collective-permute-done.24.s_a), channel_id=1, source_target_pairs={{64,65},{65,64},{66,67},{67,66},{68,69},{69,68},{70,71},{71,70},{7... | collective-permute-start | bytes 589832 | tf_op jit(solution)/shard_map/ppermute | solution.py:644
  107.6 11.7 %collective-permute-start.27 = (bf16[96,1024]{1,0:T(8,128)(2,1)}, bf16[96,1024]{1,0:T(8,128)(2,1)S(1)}, u32[]{:S(2)}, u32[]{:S(2)}) collective-permute-start(bf16[96,1024]{1,0:T(8,128)(2,1)} %get-tuple-element.150), channel_id=1, source_target_pairs={{0,2},{1,3},{2,0},{3,1},{4,6},{5,7},{6,4},{7,5},{8,10},{9,11},{10,... | collective-permute-start | bytes 589832 | tf_op jit(solution)/shard_map/ppermute | solution.py:623
  109.0 14.6 %slice-start = ((s8[5242880]{0:T(1024)(128)(4,1)}), s8[4194304]{0:T(1024)(128)(4,1)S(1)}, s32[]{:S(2)}) async-start(s8[5242880]{0:T(1024)(128)(4,1)} %bitcast.35), calls=%async_computation | async-start | bytes 8388608
  109.0 14.6 %slice-start.1 = ((s8[5242880]{0:T(1024)(128)(4,1)}), s8[1048576]{0:T(1024)(128)(4,1)S(1)}, s32[]{:S(2)}) async-start(s8[5242880]{0:T(1024)(128)(4,1)} %bitcast.35), calls=%async_computation.1 | async-start | bytes 2097152
  109.0 14.6 %copy-start.5 = (f32[16,32,2048]{2,1,0:T(8,128)S(1)}, f32[16,32,2048]{2,1,0:T(8,128)}, u32[]{:S(2)}) copy-start(f32[16,32,2048]{2,1,0:T(8,128)} %copy-done.4) | copy-start | bytes 12582916
  117.4 4.2 %collective-permute-start.30 = (bf16[96,288]{1,0:T(8,128)(2,1)S(1)}, bf16[96,288]{1,0:T(8,128)(2,1)S(1)}, u32[]{:S(2)}, u32[]{:S(2)}) collective-permute-start(bf16[96,288]{1,0:T(8,128)(2,1)S(1)} %get-tuple-element.155.refs_1_), channel_id=1, source_target_pairs={{0,3},{1,2},{2,1},{3,0},{4,7},{5,6},{6,5},{7,4},{8,11},{9,10},{10,... | collective-permute-start | bytes 165896 | tf_op jit(solution)/shard_map/ppermute | solution.py:623
  118.0 5.6 %collective-permute-start.29 = (bf16[96,288]{1,0:T(8,128)(2,1)S(1)}, bf16[96,288]{1,0:T(8,128)(2,1)S(1)}, u32[]{:S(2)}, u32[]{:S(2)}) collective-permute-start(bf16[96,288]{1,0:T(8,128)(2,1)S(1)} %get-tuple-element.155.refs_1_), channel_id=1, source_target_pairs={{0,2},{1,3},{2,0},{3,1},{4,6},{5,7},{6,4},{7,5},{8,10},{9,11},{10,... | collective-permute-start | bytes 165896 | tf_op jit(solution)/shard_map/ppermute | solution.py:623
  119.2 4.4 %collective-permute-start.28 = (bf16[96,288]{1,0:T(8,128)(2,1)S(1)}, bf16[96,288]{1,0:T(8,128)(2,1)S(1)}, u32[]{:S(2)}, u32[]{:S(2)}) collective-permute-start(bf16[96,288]{1,0:T(8,128)(2,1)S(1)} %get-tuple-element.155.refs_1_), channel_id=1, source_target_pairs={{0,1},{1,0},{2,3},{3,2},{4,5},{5,4},{6,7},{7,6},{8,9},{9,8},{10,11... | collective-permute-start | bytes 165896 | tf_op jit(solution)/shard_map/ppermute | solution.py:623
  123.6 11.2 %copy-start.1 = (bf16[3,32,4096]{2,1,0:T(8,128)(2,1)S(1)}, bf16[3,32,4096]{2,1,0:T(8,128)(2,1)}, u32[]{:S(2)}) copy-start(bf16[3,32,4096]{2,1,0:T(8,128)(2,1)} %param.22) | copy-start | bytes 2359300
  (13 other events, 29.1 us)

commit v2 on v1

--- a/solution.py
+++ b/solution.py
@@ -55,30 +55,34 @@
     )(*args)
 
 
-def cat_kernel(a, b, c, d, first, last, held, left):
+def cat_kernel(*refs):
+    sources, outs, held, left = refs[:8], refs[8:12], refs[12], refs[13]
     copies = []
-    for block, out in enumerate((first, last)):
-        cols = slice(block * GROUP, (block + 1) * GROUP)
-        held[block] = jnp.concatenate(
-            [a[:, cols], b[:, cols], c[:, cols], d[:, cols]], axis=0
-        )
-        copies.append(pltpu.make_async_copy(held.at[block], out, left.at[block]))
-        copies[-1].start()
+    for half in range(2):
+        for block in range(2):
+            cols = slice(block * GROUP, (block + 1) * GROUP)
+            place = 2 * half + block
+            held[place] = jnp.concatenate(
+                [source[:, cols] for source in sources[4 * half : 4 * half + 4]], axis=0
+            )
+            copies.append(
+                pltpu.make_async_copy(held.at[place], outs[place], left.at[place])
+            )
+            copies[-1].start()
     for copy in copies:
         copy.wait()
 
 
 def cat_rows(pieces):
-    shape = jax.ShapeDtypeStruct((16, GROUP), BF16)
     return call(
         cat_kernel,
         "cat_rows",
-        48,
-        [HELD] * 4,
-        [shape, shape],
-        [pltpu.VMEM((2, 16, GROUP), BF16), pltpu.SemaphoreType.DMA((2,))],
+        60,
+        [HELD] * 8,
+        [jax.ShapeDtypeStruct((16, GROUP), BF16)] * 4,
+        [pltpu.VMEM((4, 16, GROUP), BF16), pltpu.SemaphoreType.DMA((4,))],
         pieces,
-        [ANYWHERE] * 2,
+        [ANYWHERE] * 4,
     )
 
 
@@ -273,7 +277,7 @@
 
 
 def conv_kernel(
-    store, onehot, keep, gains, proj, pool, conv_out, terms, scales, taken_out, taken, left
+    store, onehot, keep, gains, proj, pool, conv_out, terms, scales, taken_out, taken, left, conv_held, gone
 ):
     copies = []
     total = jnp.zeros((ROWS, TERMS), F32)
@@ -294,7 +298,13 @@
         conv, _ = conv_block(
             inputs, store, lambda k, rows: fetched[rows, k * CB : (k + 1) * CB], keep, gains, cols
         )
-        conv_out[:, cols] = conv
+        conv_held[block] = conv
+        copies.append(
+            pltpu.make_async_copy(
+                conv_held.at[block], conv_out.at[:, pl.ds(block * CB, CB)], gone.at[block]
+            )
+        )
+        copies[-1].start()
         total = total + lax.dot_general(
             conv.astype(BF16), proj[:, cols], (((1,), (1,)), ((), ())), preferred_element_type=F32
         )
@@ -315,9 +325,14 @@
             jax.ShapeDtypeStruct((ROWS, LANES), F32),
             jax.ShapeDtypeStruct((STEPS, 3, ROWS, CB), BF16),
         ],
-        [pltpu.VMEM((STEPS, 3, ROWS, CB), BF16), pltpu.SemaphoreType.DMA((STEPS,))],
+        [
+            pltpu.VMEM((STEPS, 3, ROWS, CB), BF16),
+            pltpu.SemaphoreType.DMA((STEPS,)),
+            pltpu.VMEM((STEPS, ROWS, CB), F32),
+            pltpu.SemaphoreType.DMA((STEPS,)),
+        ],
         args,
-        [HELD] * 3 + [ANYWHERE],
+        [ANYWHERE, HELD, HELD, ANYWHERE],
     )
 
 
@@ -631,8 +646,7 @@
     return lax.ppermute(value, "replica", pairs)
 
 
-def gather_far(near, far):
-    first, last = cat_rows(near)
+def gather_far(first, last, far):
     first_below, last_above = along(first, far, 1), along(last, far, 3)
     last_below, first_above = along(last, far, 1), along(first, far, 3)
     first_far, last_far = along(first_below, far, 1), along(last_above, far, 3)
@@ -674,15 +688,20 @@
     rows = cache_window.shape[1]
     cached = arrange_call(cache_codes[0], cache_window[0].transpose(1, 0, 2), cache_scales[0])
 
+    near_a = [cached[0]] + [along(cached[0], "y", k) for k in (1, 2, 3)]
+    near_b = [cached[1]] + [along(cached[1], "z", k) for k in (1, 2, 3)]
+    near_a, near_b = lax.optimization_barrier((near_a, near_b))
+    proj = state_proj[0].T
+    first_a, last_a, first_b, last_b = cat_rows(near_a + near_b)
+
+    raw = (refill_source, finished, norm_gain, conv_weight, conv_bias, decay_rate)
+    raw = (*raw, skip_gain, step_bias, residual, state_scales)
+    raw, first_a, last_a = lax.optimization_barrier((raw, first_a, last_a))
+    refill_source, finished, norm_gain, conv_weight, conv_bias, decay_rate = raw[:6]
+    skip_gain, step_bias, residual, state_scales = raw[6:]
     gains = jnp.concatenate(
         [conv_weight[0], conv_bias, decay_rate[0], skip_gain, step_bias], axis=0
     )
-    near_a = [cached[0]] + [along(cached[0], "y", k) for k in (1, 2, 3)]
-    near_b = [cached[1]] + [along(cached[1], "z", k) for k in (1, 2, 3)]
-    near_a, near_b, gains, proj = lax.optimization_barrier(
-        (near_a, near_b, gains, state_proj[0].T)
-    )
-    pieces = gather_far(near_a, "z") + gather_far(near_b, "y")
 
     sources = lax.dynamic_slice_in_dim(refill_source, replica * SLOTS, SLOTS, 1)
     room = ((0, 0), (0, LANES - ROWS))
@@ -696,16 +715,17 @@
         gate_input.reshape(ROWS, CHANNELS),
         conv_window[0].transpose(1, 0, 2).reshape(ROWS, CHANNELS),
     )
-    small, flat, codes, weight, pieces[0], pieces[8] = lax.optimization_barrier(
-        (small, flat, state_codes[0], projection[0], pieces[0], pieces[8])
+    flat, codes, weight, first_b = lax.optimization_barrier(
+        (flat, state_codes[0], projection[0], first_b)
     )
     sources, ended, where, residual_rows, gain = small
     onehot, keep = plan_call(where, sources, ended)
     store = fill_call("hold_store", list(flat))
     states = unfold_call(codes, state_scales[0])
     column_share = lax.dynamic_slice_in_dim(residual_rows, column * SHARE, SHARE, 1)
-    states, store, onehot, keep, pieces = lax.optimization_barrier(
-        (states, store, onehot, keep, pieces)
+    pieces = gather_far(first_a, last_a, "z") + gather_far(first_b, last_b, "y")
+    states, store, onehot, keep, gains, gain, pieces = lax.optimization_barrier(
+        (states, store, onehot, keep, gains, gain, pieces)
     )
     pool = pool_call(pieces)
 

time: 135 us -> 138 us (1.022)
  waiting for transfers between devices: 23.4 us -> 28.4 us
  local copies, waits for them, and re-layouts: 16.7 us -> 15.2 us
    ppermute x18, waiting for transfers between devices: 8.18 us -> 13.2 us  [along(): return lax.ppermute(value, 'replica', pairs)]
    concatenate x1, local copies, waits for them, and re-layouts: 2.57 us -> 0.26 us  [local(): jnp.concatenate([conv_weight[0], conv_bias, decay_rate[0], skip_gain, ste...]
    unnamed x61 -> x68, local copies, waits for them, and re-layouts: 11.2 us -> 11.9 us
    pallas_call x15 -> x14, Pallas kernels: 48.7 us -> 48.4 us  [call(): pl.pallas_call(kernel, in_specs=in_specs, out_specs=out_specs, out_shape=...]
  transfers between devices with their start and end apart: 31 -> 31, of which waited for: 14 -> 17; matrix products, arithmetic and copies ran while one was open for 5% -> 2% of each run, Pallas kernels for 12% -> 11%
where the time goes in v2:
time: 138 us
  Pallas kernels  48.4 us (35%)
  starting transfers between devices  44.8 us (32%)
  waiting for transfers between devices  28.4 us (21%)
  local copies, waits for them, and re-layouts  15.2 us (11%)
    pallas_call x14, Pallas kernels, call(): pl.pallas_call(kernel, in_specs=in_specs, out_specs=out_specs, out_shape=...  48.4 us
    ppermute x18, starting transfers between devices, along(): return lax.ppermute(value, 'replica', pairs)  31.1 us
    ppermute x18, waiting for transfers between devices, along(): return lax.ppermute(value, 'replica', pairs)  13.2 us
    unnamed x68, local copies, waits for them, and re-layouts  11.9 us
    ppermute x8, waiting for transfers between devices, exchange(): return lax.ppermute(value, 'tensor', [(i, i ^ step) for i in range(4)])  7.56 us
    ppermute x3, starting transfers between devices, in_section_one(): return lax.ppermute(value, ('section', 'tensor'), pairs)  5.77 us
    ppermute x3, waiting for transfers between devices, in_section_one(): return lax.ppermute(value, ('section', 'tensor'), pairs)  5.28 us
    ppermute x8, starting transfers between devices, exchange(): return lax.ppermute(value, 'tensor', [(i, i ^ step) for i in range(4)])  4.42 us
  transfers between devices with their start and end apart: 31, of which 17 were waited for; matrix products, arithmetic and copies ran while one was open for 2% of the time, Pallas kernels for 11%

profile of v2, /device:TPU:6, one launch (start us, length us, event | category | flops | bytes accessed | tf_op | source)
XLA Modules:
  0.0 137.9 jit_solution(4641917976219988720)
XLA Ops:
  0.6 2.0 %arrange_rows.1 = (bf16[4,20480]{1,0:T(4,128)(2,1)}, bf16[4,20480]{1,0:T(4,128)(2,1)}) custom-call(bf16[4,16,2048]{2,1,0:T(8,128)(2,1)} %bitcast.47, bf16[3,4,2048]{2,1,0:T(4,128)(2,1)} %bitcast.50, bf16[4,16]{1,0:T(4,128)(2,1)} %bitcast.52), custom_call_target="tpu_custom_call" | custom-call | flops 1 | bytes 1 | tf_op jit(solution)/shard_map/arrange_rows/pallas_call | solution.py:46
  2.6 3.0 %collective-permute-start.2 = (bf16[4,20480]{1,0:T(4,128)(2,1)}, bf16[4,20480]{1,0:T(4,128)(2,1)S(1)}, u32[]{:S(2)}, u32[]{:S(2)}) collective-permute-start(bf16[4,20480]{1,0:T(4,128)(2,1)} %get-tuple-element.91.refs_0_), channel_id=1, source_target_pairs={{0,12},{4,0},{8,4},{12,8},{16,28},{20,16},{24,20},{28,24},{32,44},... | collective-permute-start | bytes 491528 | tf_op jit(solution)/shard_map/ppermute | solution.py:646
  6.3 1.0 collective-permute-start
  7.2 4.0 %collective-permute-start.5 = (bf16[4,20480]{1,0:T(4,128)(2,1)}, bf16[4,20480]{1,0:T(4,128)(2,1)S(1)}, u32[]{:S(2)}, u32[]{:S(2)}) collective-permute-start(bf16[4,20480]{1,0:T(4,128)(2,1)} %get-tuple-element.95.refs_4_), channel_id=1, source_target_pairs={{0,48},{4,52},{8,56},{12,60},{16,0},{20,4},{24,8},{28,12},{32,16},... | collective-permute-start | bytes 491528 | tf_op jit(solution)/shard_map/ppermute | solution.py:646
  11.3 1.6 %collective-permute-done.2.refs_3_ = bf16[4,20480]{1,0:T(4,128)(2,1)S(1)} collective-permute-done((bf16[4,20480]{1,0:T(4,128)(2,1)}, bf16[4,20480]{1,0:T(4,128)(2,1)S(1)}, u32[]{:S(2)}, u32[]{:S(2)}) %collective-permute-start.2) | collective-permute-done | bytes 163872 | tf_op jit(solution)/shard_map/ppermute | solution.py:646
  12.9 1.9 %collective-permute-start.3 = (bf16[4,20480]{1,0:T(4,128)(2,1)}, bf16[4,20480]{1,0:T(4,128)(2,1)S(1)}, u32[]{:S(2)}, u32[]{:S(2)}) collective-permute-start(bf16[4,20480]{1,0:T(4,128)(2,1)} %get-tuple-element.95.refs_4_), channel_id=1, source_target_pairs={{0,16},{4,20},{8,24},{12,28},{16,32},{20,36},{24,40},{28,44},{32,4... | collective-permute-start | bytes 491528 | tf_op jit(solution)/shard_map/ppermute | solution.py:646
  14.8 1.7 %collective-permute-done.refs_1_ = bf16[4,20480]{1,0:T(4,128)(2,1)S(1)} collective-permute-done((bf16[4,20480]{1,0:T(4,128)(2,1)}, bf16[4,20480]{1,0:T(4,128)(2,1)S(1)}, u32[]{:S(2)}, u32[]{:S(2)}) %collective-permute-start) | collective-permute-done | bytes 163872 | tf_op jit(solution)/shard_map/ppermute | solution.py:646
  16.5 1.2 collective-permute-done.5.refs_7_
  18.4 3.4 %collective-permute-done.3.refs_5_ = bf16[4,20480]{1,0:T(4,128)(2,1)S(1)} collective-permute-done((bf16[4,20480]{1,0:T(4,128)(2,1)}, bf16[4,20480]{1,0:T(4,128)(2,1)S(1)}, u32[]{:S(2)}, u32[]{:S(2)}) %collective-permute-start.3) | collective-permute-done | bytes 163872 | tf_op jit(solution)/shard_map/ppermute | solution.py:646
  22.5 2.6 %cat_rows.1 = (bf16[16,10240]{1,0:T(8,128)(2,1)}, bf16[16,10240]{1,0:T(8,128)(2,1)}, bf16[16,10240]{1,0:T(8,128)(2,1)}, bf16[16,10240]{1,0:T(8,128)(2,1)}) custom-call(bf16[4,20480]{1,0:T(4,128)(2,1)} %get-tuple-element.91.refs_0_, bf16[4,20480]{1,0:T(4,128)(2,1)} %copy-done.22, bf16[4,20480]{1,0:T(4,128)(2,1)} %copy-done.21, bf16[4,20480]{1,0:T(4,128)(2,1)} %copy-done.20, ...), custom_call_target="tpu_custom_call" | custom-call | flops 1 | bytes 1 | tf_op jit(solution)/shard_map/cat_rows/pallas_call | solution.py:46
  25.9 1.4 collective-permute-start.6
  27.2 1.9 %collective-permute-start.10 = (bf16[16,10240]{1,0:T(8,128)(2,1)}, bf16[16,10240]{1,0:T(8,128)(2,1)}, u32[]{:S(2)}, u32[]{:S(2)}) collective-permute-start(bf16[16,10240]{1,0:T(8,128)(2,1)} %get-tuple-element.131.refs_4_), channel_id=1, source_target_pairs={{0,48},{4,52},{8,56},{12,60},{16,0},{20,4},{24,8},{28,12},{32,16},... | collective-permute-start | bytes 983048 | tf_op jit(solution)/shard_map/ppermute | solution.py:646
  29.2 3.5 %collective-permute-start.14 = (bf16[16,10240]{1,0:T(8,128)(2,1)}, bf16[16,10240]{1,0:T(8,128)(2,1)}, u32[]{:S(2)}, u32[]{:S(2)}) collective-permute-start(bf16[16,10240]{1,0:T(8,128)(2,1)} %get-tuple-element.135.refs_8_), channel_id=1, source_target_pairs={{0,12},{4,0},{8,4},{12,8},{16,28},{20,16},{24,20},{28,24},{32,44},... | collective-permute-start | bytes 983048 | tf_op jit(solution)/shard_map/ppermute | solution.py:646
  32.7 3.4 %collective-permute-done.8.refs_3_ = bf16[16,10240]{1,0:T(8,128)(2,1)} collective-permute-done((bf16[16,10240]{1,0:T(8,128)(2,1)}, bf16[16,10240]{1,0:T(8,128)(2,1)}, u32[]{:S(2)}, u32[]{:S(2)}) %collective-permute-start.8) | collective-permute-done | bytes 327712 | tf_op jit(solution)/shard_map/ppermute | solution.py:646
  36.1 1.2 collective-permute-start.12
  38.0 3.6 %collective-permute-start.16 = (bf16[16,10240]{1,0:T(8,128)(2,1)}, bf16[16,10240]{1,0:T(8,128)(2,1)}, u32[]{:S(2)}, u32[]{:S(2)}) collective-permute-start(bf16[16,10240]{1,0:T(8,128)(2,1)} %get-tuple-element.139.refs_12_), channel_id=1, source_target_pairs={{0,12},{4,0},{8,4},{12,8},{16,28},{20,16},{24,20},{28,24},{32,44},... | collective-permute-start | bytes 983048 | tf_op jit(solution)/shard_map/ppermute | solution.py:646
  41.8 1.1 collective-permute-start.15
  43.5 2.8 %collective-permute-start.11 = (bf16[16,10240]{1,0:T(8,128)(2,1)}, bf16[16,10240]{1,0:T(8,128)(2,1)}, u32[]{:S(2)}, u32[]{:S(2)}) collective-permute-start(bf16[16,10240]{1,0:T(8,128)(2,1)} %collective-permute-done.10.refs_7_), channel_id=1, source_target_pairs={{0,48},{4,52},{8,56},{12,60},{16,0},{20,4},{24,8},{28,12},{32,16},... | collective-permute-start | bytes 983048 | tf_op jit(solution)/shard_map/ppermute | solution.py:646
  46.3 1.1 collective-permute-start.13
  47.4 2.8 %collective-permute-start.17 = (bf16[16,10240]{1,0:T(8,128)(2,1)}, bf16[16,10240]{1,0:T(8,128)(2,1)}, u32[]{:S(2)}, u32[]{:S(2)}) collective-permute-start(bf16[16,10240]{1,0:T(8,128)(2,1)} %collective-permute-done.16.refs_15_), channel_id=1, source_target_pairs={{0,12},{4,0},{8,4},{12,8},{16,28},{20,16},{24,20},{28,24},{32,44},... | collective-permute-start | bytes 983048 | tf_op jit(solution)/shard_map/ppermute | solution.py:646
  52.7 1.6 %copy-done.9 = bf16[1,32,16,2048]{3,2,1,0:T(8,128)(2,1)S(1)} copy-done((bf16[1,32,16,2048]{3,2,1,0:T(8,128)(2,1)S(1)}, bf16[1,32,16,2048]{3,2,1,0:T(8,128)(2,1)}, u32[]{:S(2)}) %copy-start.9) | copy-done | bytes 2097176
  54.3 2.2 %unfold_states.1.refs_10_ = f32[16,32,2048]{2,1,0:T(8,128)S(1)} custom-call(bf16[32,16,2048]{2,1,0:T(8,128)(2,1)S(1)} %bitcast.41, bf16[32,16]{1,0:T(8,128)(2,1)S(1)} %bitcast.46), custom_call_target="tpu_custom_call" | custom-call | flops 1 | bytes 1 | tf_op jit(solution)/shard_map/unfold_states/pallas_call | solution.py:46
  56.6 2.0 %copy-done.4 = f32[16,32,2048]{2,1,0:T(8,128)} copy-done((f32[16,32,2048]{2,1,0:T(8,128)}, f32[16,32,2048]{2,1,0:T(8,128)S(1)}, u32[]{:S(2)}) %copy-start.4) | copy-done | bytes 4194328
  61.0 2.7 %pool_rows.1.pool.refs_8_ = bf16[4,64,10240]{2,1,0:T(8,128)(2,1)S(1)} custom-call(bf16[16,10240]{1,0:T(8,128)(2,1)} %get-tuple-element.127.refs_0_, bf16[16,10240]{1,0:T(8,128)(2,1)} %collective-permute-done.6.refs_1_, bf16[16,10240]{1,0:T(8,128)(2,1)} %collective-permute-done.7.refs_2_, bf16[16,10240]{1,0:T(8,128)(2,1)} %collective-permute-done.8.refs_3_, ...), custom_call_target="tpu_custom_call" | custom-call | flops 1 | bytes 1 | tf_op jit(solution)/shard_map/pool_rows/pallas_call | solution.py:46
  63.8 2.6 %conv_terms.1 = (f32[96,2048]{1,0:T(8,128)S(1)}, bf16[96,288]{1,0:T(8,128)(2,1)S(1)}, f32[96,128]{1,0:T(8,128)S(1)}, bf16[4,3,96,512]{3,2,1,0:T(8,128)(2,1)S(1)}) custom-call(bf16[544,2048]{1,0:T(8,128)(2,1)S(1)} %hold_store.1.store.refs_11_, bf16[2,96,64]{2,1,0:T(8,128)(2,1)S(1)} %get-tuple-element.124.onehot.refs_5_, ...), custom_call_target="tpu_custom_call" | custom-call | flops 1 | bytes 1 | tf_op jit(solution)/shard_map/conv_terms/pallas_call | solution.py:46
  66.4 1.0 copy-done.10
  68.3 1.0 collective-permute-start.18
  69.3 2.5 %collective-permute-done.20.refs_4_ = bf16[96,288]{1,0:T(8,128)(2,1)S(1)} collective-permute-done((bf16[96,288]{1,0:T(8,128)(2,1)S(1)}, bf16[96,288]{1,0:T(8,128)(2,1)S(1)}, u32[]{:S(2)}, u32[]{:S(2)}) %collective-permute-start.20) | collective-permute-done | bytes 55328 | tf_op jit(solution)/shard_map/ppermute | solution.py:638
  72.5 10.5 %scan_gate_project.1 = (f32[2,96,1024]{2,1,0:T(8,128)S(1)}, bf16[2,96,1024]{2,1,0:T(8,128)(2,1)S(1)}) custom-call(s32[4]{0:T(128)S(1)} %pad_add_fusion.where.refs_0_, bf16[96,288]{1,0:T(8,128)(2,1)S(1)} %get-tuple-element.143.refs_1_, bf16[96,288]{1,0:T(8,128)(2,1)S(1)} %collective-permute-done.18.refs_2_, ...), custom_call_target="tpu_custom_call" | custom-call | flops 1 | bytes 1 | tf_op jit(solution)/shard_map/scan_gate_project/pallas_call | solution.py:46
  83.3 1.5 %collective-permute-done.21.got = bf16[2,96,1024]{2,1,0:T(8,128)(2,1)S(1)} collective-permute-done((bf16[2,96,1024]{2,1,0:T(8,128)(2,1)S(1)}, bf16[2,96,1024]{2,1,0:T(8,128)(2,1)S(1)}, u32[]{:S(2)}, u32[]{:S(2)}) %collective-permute-start.21) | collective-permute-done | bytes 393248 | tf_op jit(solution)/shard_map/ppermute | solution.py:638
  85.5 1.3 sum_on_chip.1
  86.8 1.5 %collective-permute-start.23 = (bf16[96,1024]{1,0:T(8,128)(2,1)}, bf16[96,1024]{1,0:T(8,128)(2,1)}, u32[]{:S(2)}, u32[]{:S(2)}) collective-permute-start(bf16[96,1024]{1,0:T(8,128)(2,1)} %get-tuple-element.162), channel_id=1, source_target_pairs={{0,66},{1,67},{2,64},{3,65},{64,2},{65,3},{66,0},{67,1},{4,70},{5,... | collective-permute-start | bytes 589832 | tf_op jit(solution)/shard_map/ppermute | solution.py:743
  88.3 1.9 %collective-permute-start.22 = (bf16[96,1024]{1,0:T(8,128)(2,1)S(1)}, bf16[96,1024]{1,0:T(8,128)(2,1)}, u32[]{:S(2)}, u32[]{:S(2)}) collective-permute-start(bf16[96,1024]{1,0:T(8,128)(2,1)S(1)} %get-tuple-element.154.same), channel_id=1, source_target_pairs={{0,64},{64,0},{1,65},{65,1},{2,66},{66,2},{3,67},{67,3},{4,68},{68... | collective-permute-start | bytes 589832 | tf_op jit(solution)/shard_map/ppermute | solution.py:744
  90.2 5.8 %copy-done.3 = bf16[1,2048,4096]{2,1,0:T(8,128)(2,1)S(1)} copy-done((bf16[1,2048,4096]{2,1,0:T(8,128)(2,1)S(1)}, bf16[1,2048,4096]{2,1,0:T(8,128)(2,1)}, u32[]{:S(2)}) %copy-start.3) | copy-done | bytes 16777240
  96.0 1.2 hold_projection.1.big
  97.1 2.4 %collective-permute-done.23.other = bf16[96,1024]{1,0:T(8,128)(2,1)} collective-permute-done((bf16[96,1024]{1,0:T(8,128)(2,1)}, bf16[96,1024]{1,0:T(8,128)(2,1)}, u32[]{:S(2)}, u32[]{:S(2)}) %collective-permute-start.23) | collective-permute-done | bytes 196640 | tf_op jit(solution)/shard_map/ppermute | solution.py:743
  99.5 1.1 add_residual.1.s_own.stream
  100.6 1.9 %collective-permute-start.24 = (bf16[96,1024]{1,0:T(8,128)(2,1)S(1)}, bf16[96,1024]{1,0:T(8,128)(2,1)S(1)}, u32[]{:S(2)}, u32[]{:S(2)}) collective-permute-start(bf16[96,1024]{1,0:T(8,128)(2,1)S(1)} %add_residual.1.s_own.stream), channel_id=1, source_target_pairs={{64,66},{65,67},{66,64},{67,65},{68,70},{69,71},{70,68},{71,69},{7... | collective-permute-start | bytes 589832 | tf_op jit(solution)/shard_map/ppermute | solution.py:658
  102.6 1.9 %collective-permute-start.25 = (bf16[96,1024]{1,0:T(8,128)(2,1)S(1)}, bf16[96,1024]{1,0:T(8,128)(2,1)S(1)}, u32[]{:S(2)}, u32[]{:S(2)}) collective-permute-start(bf16[96,1024]{1,0:T(8,128)(2,1)S(1)} %add_residual.1.s_own.stream), channel_id=1, source_target_pairs={{64,65},{65,64},{66,67},{67,66},{68,69},{69,68},{70,71},{71,70},{7... | collective-permute-start | bytes 589832 | tf_op jit(solution)/shard_map/ppermute | solution.py:658
  104.5 4.2 %collective-permute-done.24.s_a = bf16[96,1024]{1,0:T(8,128)(2,1)S(1)} collective-permute-done((bf16[96,1024]{1,0:T(8,128)(2,1)S(1)}, bf16[96,1024]{1,0:T(8,128)(2,1)S(1)}, u32[]{:S(2)}, u32[]{:S(2)}) %collective-permute-start.24) | collective-permute-done | bytes 196640 | tf_op jit(solution)/shard_map/ppermute | solution.py:658
  108.8 1.9 %collective-permute-start.26 = (bf16[96,1024]{1,0:T(8,128)(2,1)S(1)}, bf16[96,1024]{1,0:T(8,128)(2,1)S(1)}, u32[]{:S(2)}, u32[]{:S(2)}) collective-permute-start(bf16[96,1024]{1,0:T(8,128)(2,1)S(1)} %collective-permute-done.24.s_a), channel_id=1, source_target_pairs={{64,65},{65,64},{66,67},{67,66},{68,69},{69,68},{70,71},{71,70},{7... | collective-permute-start | bytes 589832 | tf_op jit(solution)/shard_map/ppermute | solution.py:658
  111.1 1.0 collective-permute-done.26.s_c
  112.1 8.4 %norm_project_conv.1 = (f32[96,2048]{1,0:T(8,128)S(1)}, bf16[96,288]{1,0:T(8,128)(2,1)S(1)}, bf16[3,32,2048]{2,1,0:T(8,128)(2,1)}) custom-call(s32[4]{0:T(128)S(1)} %copy-done.19, bf16[96,1024]{1,0:T(8,128)(2,1)S(1)} %add_residual.1.s_own.stream, bf16[96,1024]{1,0:T(8,128)(2,1)S(1)} %collective-permute-done.24.s_a, ...), custom_call_target="tpu_custom_call" | custom-call | flops 1 | bytes 1 | tf_op jit(solution)/shard_map/norm_project_conv/pallas_call | solution.py:46
  121.1 1.2 collective-permute-start.29
  122.4 1.5 %add_first.1 = bf16[96,1024]{1,0:T(8,128)(2,1)} custom-call(s32[4]{0:T(128)S(1)} %copy-done.19, bf16[96,1024]{1,0:T(8,128)(2,1)S(1)} %constant_dynamic-slice_fusion.residual, bf16[96,1024]{1,0:T(8,128)(2,1)S(1)} %get-tuple-element.154.same, bf16[96,1024]{1,0:T(8,128)(2,1)S(1)} %collective-permute-done.27.other, bf16[96,1024]{1,0:T(8,128)(2,1)S(1)} %add_residual.1.s_own.stream), custom_call_target="tpu_custom_call" | custom-call | flops 1 | bytes 1 | tf_op jit(solution)/shard_map/add_first/pallas_call | solution.py:46
  123.9 0.9 collective-permute-done.30.refs_4_
  124.8 1.9 %collective-permute-done.29.refs_3_ = bf16[96,288]{1,0:T(8,128)(2,1)S(1)} collective-permute-done((bf16[96,288]{1,0:T(8,128)(2,1)S(1)}, bf16[96,288]{1,0:T(8,128)(2,1)S(1)}, u32[]{:S(2)}, u32[]{:S(2)}) %collective-permute-start.29) | collective-permute-done | bytes 55328 | tf_op jit(solution)/shard_map/ppermute | solution.py:638
  126.7 11.2 %scan_final.1 = (bf16[96,2048]{1,0:T(8,128)(2,1)}, bf16[32,16,2048]{2,1,0:T(8,128)(2,1)}, bf16[16,32]{1,0:T(8,128)(2,1)}) custom-call(s32[4]{0:T(128)S(1)} %copy-done.19, bf16[96,288]{1,0:T(8,128)(2,1)S(1)} %get-tuple-element.167.refs_1_, bf16[96,288]{1,0:T(8,128)(2,1)S(1)} %collective-permute-done.28.refs_2_, ...), custom_call_target="tpu_custom_call" | custom-call | flops 1 | bytes 1 | tf_op jit(solution)/shard_map/scan_final/pallas_call | solution.py:46
  (107 shorter events, 13.0 us)
Async XLA Ops:
  0.6 89.5 %copy-start = (bf16[3,32,4096]{2,1,0:T(8,128)(2,1)S(1)}, bf16[3,32,4096]{2,1,0:T(8,128)(2,1)}, u32[]{:S(2)}) copy-start(bf16[3,32,4096]{2,1,0:T(8,128)(2,1)} %param.22) | copy-start | bytes 2359300
  2.6 10.3 %collective-permute-start.2 = (bf16[4,20480]{1,0:T(4,128)(2,1)}, bf16[4,20480]{1,0:T(4,128)(2,1)S(1)}, u32[]{:S(2)}, u32[]{:S(2)}) collective-permute-start(bf16[4,20480]{1,0:T(4,128)(2,1)} %get-tuple-element.91.refs_0_), channel_id=1, source_target_pairs={{0,12},{4,0},{8,4},{12,8},{16,28},{20,16},{24,20},{28,24},{32,44},... | collective-permute-start | bytes 491528 | tf_op jit(solution)/shard_map/ppermute | solution.py:646
  5.6 9.2 %collective-permute-start.1 = (bf16[4,20480]{1,0:T(4,128)(2,1)}, bf16[4,20480]{1,0:T(4,128)(2,1)S(1)}, u32[]{:S(2)}, u32[]{:S(2)}) collective-permute-start(bf16[4,20480]{1,0:T(4,128)(2,1)} %get-tuple-element.91.refs_0_), channel_id=1, source_target_pairs={{0,8},{4,12},{8,0},{12,4},{16,24},{20,28},{24,16},{28,20},{32,40},... | collective-permute-start | bytes 491528 | tf_op jit(solution)/shard_map/ppermute | solution.py:646
  6.3 10.3 %collective-permute-start = (bf16[4,20480]{1,0:T(4,128)(2,1)}, bf16[4,20480]{1,0:T(4,128)(2,1)S(1)}, u32[]{:S(2)}, u32[]{:S(2)}) collective-permute-start(bf16[4,20480]{1,0:T(4,128)(2,1)} %get-tuple-element.91.refs_0_), channel_id=1, source_target_pairs={{0,4},{4,8},{8,12},{12,0},{16,20},{20,24},{24,28},{28,16},{32,36},... | collective-permute-start | bytes 491528 | tf_op jit(solution)/shard_map/ppermute | solution.py:646
  7.2 10.5 %collective-permute-start.5 = (bf16[4,20480]{1,0:T(4,128)(2,1)}, bf16[4,20480]{1,0:T(4,128)(2,1)S(1)}, u32[]{:S(2)}, u32[]{:S(2)}) collective-permute-start(bf16[4,20480]{1,0:T(4,128)(2,1)} %get-tuple-element.95.refs_4_), channel_id=1, source_target_pairs={{0,48},{4,52},{8,56},{12,60},{16,0},{20,4},{24,8},{28,12},{32,16},... | collective-permute-start | bytes 491528 | tf_op jit(solution)/shard_map/ppermute | solution.py:646
  11.3 7.1 %collective-permute-start.4 = (bf16[4,20480]{1,0:T(4,128)(2,1)}, bf16[4,20480]{1,0:T(4,128)(2,1)S(1)}, u32[]{:S(2)}, u32[]{:S(2)}) collective-permute-start(bf16[4,20480]{1,0:T(4,128)(2,1)} %get-tuple-element.95.refs_4_), channel_id=1, source_target_pairs={{0,32},{4,36},{8,40},{12,44},{16,48},{20,52},{24,56},{28,60},{32,0... | collective-permute-start | bytes 491528 | tf_op jit(solution)/shard_map/ppermute | solution.py:646
  12.9 8.9 %copy-start.20 = (bf16[4,20480]{1,0:T(4,128)(2,1)}, bf16[4,20480]{1,0:T(4,128)(2,1)S(1)}, u32[]{:S(2)}) copy-start(bf16[4,20480]{1,0:T(4,128)(2,1)S(1)} %collective-permute-done.2.refs_3_) | copy-start | bytes 491524
  12.9 8.9 %collective-permute-start.3 = (bf16[4,20480]{1,0:T(4,128)(2,1)}, bf16[4,20480]{1,0:T(4,128)(2,1)S(1)}, u32[]{:S(2)}, u32[]{:S(2)}) collective-permute-start(bf16[4,20480]{1,0:T(4,128)(2,1)} %get-tuple-element.95.refs_4_), channel_id=1, source_target_pairs={{0,16},{4,20},{8,24},{12,28},{16,32},{20,36},{24,40},{28,44},{32,4... | collective-permute-start | bytes 491528 | tf_op jit(solution)/shard_map/ppermute | solution.py:646
  14.8 7.0 %copy-start.21 = (bf16[4,20480]{1,0:T(4,128)(2,1)}, bf16[4,20480]{1,0:T(4,128)(2,1)S(1)}, u32[]{:S(2)}) copy-start(bf16[4,20480]{1,0:T(4,128)(2,1)S(1)} %collective-permute-done.1.refs_2_) | copy-start | bytes 491524
  16.5 5.3 %copy-start.22 = (bf16[4,20480]{1,0:T(4,128)(2,1)}, bf16[4,20480]{1,0:T(4,128)(2,1)S(1)}, u32[]{:S(2)}) copy-start(bf16[4,20480]{1,0:T(4,128)(2,1)S(1)} %collective-permute-done.refs_1_) | copy-start | bytes 491524
  25.1 11.0 %collective-permute-start.8 = (bf16[16,10240]{1,0:T(8,128)(2,1)}, bf16[16,10240]{1,0:T(8,128)(2,1)}, u32[]{:S(2)}, u32[]{:S(2)}) collective-permute-start(bf16[16,10240]{1,0:T(8,128)(2,1)} %get-tuple-element.127.refs_0_), channel_id=1, source_target_pairs={{0,48},{4,52},{8,56},{12,60},{16,0},{20,4},{24,8},{28,12},{32,16},... | collective-permute-start | bytes 983048 | tf_op jit(solution)/shard_map/ppermute | solution.py:646
  25.9 12.2 %collective-permute-start.6 = (bf16[16,10240]{1,0:T(8,128)(2,1)}, bf16[16,10240]{1,0:T(8,128)(2,1)}, u32[]{:S(2)}, u32[]{:S(2)}) collective-permute-start(bf16[16,10240]{1,0:T(8,128)(2,1)} %get-tuple-element.127.refs_0_), channel_id=1, source_target_pairs={{0,16},{4,20},{8,24},{12,28},{16,32},{20,36},{24,40},{28,44},{32,4... | collective-permute-start | bytes 983048 | tf_op jit(solution)/shard_map/ppermute | solution.py:646
  27.2 14.6 %collective-permute-start.10 = (bf16[16,10240]{1,0:T(8,128)(2,1)}, bf16[16,10240]{1,0:T(8,128)(2,1)}, u32[]{:S(2)}, u32[]{:S(2)}) collective-permute-start(bf16[16,10240]{1,0:T(8,128)(2,1)} %get-tuple-element.131.refs_4_), channel_id=1, source_target_pairs={{0,48},{4,52},{8,56},{12,60},{16,0},{20,4},{24,8},{28,12},{32,16},... | collective-permute-start | bytes 983048 | tf_op jit(solution)/shard_map/ppermute | solution.py:646
  29.1 14.0 %collective-permute-start.9 = (bf16[16,10240]{1,0:T(8,128)(2,1)}, bf16[16,10240]{1,0:T(8,128)(2,1)}, u32[]{:S(2)}, u32[]{:S(2)}) collective-permute-start(bf16[16,10240]{1,0:T(8,128)(2,1)} %get-tuple-element.131.refs_4_), channel_id=1, source_target_pairs={{0,16},{4,20},{8,24},{12,28},{16,32},{20,36},{24,40},{28,44},{32,4... | collective-permute-start | bytes 983048 | tf_op jit(solution)/shard_map/ppermute | solution.py:646
  29.2 14.3 %collective-permute-start.14 = (bf16[16,10240]{1,0:T(8,128)(2,1)}, bf16[16,10240]{1,0:T(8,128)(2,1)}, u32[]{:S(2)}, u32[]{:S(2)}) collective-permute-start(bf16[16,10240]{1,0:T(8,128)(2,1)} %get-tuple-element.135.refs_8_), channel_id=1, source_target_pairs={{0,12},{4,0},{8,4},{12,8},{16,28},{20,16},{24,20},{28,24},{32,44},... | collective-permute-start | bytes 983048 | tf_op jit(solution)/shard_map/ppermute | solution.py:646
  36.1 10.2 %collective-permute-start.12 = (bf16[16,10240]{1,0:T(8,128)(2,1)}, bf16[16,10240]{1,0:T(8,128)(2,1)}, u32[]{:S(2)}, u32[]{:S(2)}) collective-permute-start(bf16[16,10240]{1,0:T(8,128)(2,1)} %get-tuple-element.135.refs_8_), channel_id=1, source_target_pairs={{0,4},{4,8},{8,12},{12,0},{16,20},{20,24},{24,28},{28,16},{32,36},... | collective-permute-start | bytes 983048 | tf_op jit(solution)/shard_map/ppermute | solution.py:646
  38.0 9.4 %collective-permute-start.16 = (bf16[16,10240]{1,0:T(8,128)(2,1)}, bf16[16,10240]{1,0:T(8,128)(2,1)}, u32[]{:S(2)}, u32[]{:S(2)}) collective-permute-start(bf16[16,10240]{1,0:T(8,128)(2,1)} %get-tuple-element.139.refs_12_), channel_id=1, source_target_pairs={{0,12},{4,0},{8,4},{12,8},{16,28},{20,16},{24,20},{28,24},{32,44},... | collective-permute-start | bytes 983048 | tf_op jit(solution)/shard_map/ppermute | solution.py:646
  41.8 19.1 %collective-permute-start.15 = (bf16[16,10240]{1,0:T(8,128)(2,1)}, bf16[16,10240]{1,0:T(8,128)(2,1)}, u32[]{:S(2)}, u32[]{:S(2)}) collective-permute-start(bf16[16,10240]{1,0:T(8,128)(2,1)} %get-tuple-element.139.refs_12_), channel_id=1, source_target_pairs={{0,4},{4,8},{8,12},{12,0},{16,20},{20,24},{24,28},{28,16},{32,36},... | collective-permute-start | bytes 983048 | tf_op jit(solution)/shard_map/ppermute | solution.py:646
  43.1 17.9 %collective-permute-start.7 = (bf16[16,10240]{1,0:T(8,128)(2,1)}, bf16[16,10240]{1,0:T(8,128)(2,1)}, u32[]{:S(2)}, u32[]{:S(2)}) collective-permute-start(bf16[16,10240]{1,0:T(8,128)(2,1)} %collective-permute-done.6.refs_1_), channel_id=1, source_target_pairs={{0,16},{4,20},{8,24},{12,28},{16,32},{20,36},{24,40},{28,44},{32,4... | collective-permute-start | bytes 983048 | tf_op jit(solution)/shard_map/ppermute | solution.py:646
  43.5 17.4 %collective-permute-start.11 = (bf16[16,10240]{1,0:T(8,128)(2,1)}, bf16[16,10240]{1,0:T(8,128)(2,1)}, u32[]{:S(2)}, u32[]{:S(2)}) collective-permute-start(bf16[16,10240]{1,0:T(8,128)(2,1)} %collective-permute-done.10.refs_7_), channel_id=1, source_target_pairs={{0,48},{4,52},{8,56},{12,60},{16,0},{20,4},{24,8},{28,12},{32,16},... | collective-permute-start | bytes 983048 | tf_op jit(solution)/shard_map/ppermute | solution.py:646
  46.3 14.6 %collective-permute-start.13 = (bf16[16,10240]{1,0:T(8,128)(2,1)}, bf16[16,10240]{1,0:T(8,128)(2,1)}, u32[]{:S(2)}, u32[]{:S(2)}) collective-permute-start(bf16[16,10240]{1,0:T(8,128)(2,1)} %collective-permute-done.12.refs_9_), channel_id=1, source_target_pairs={{0,4},{4,8},{8,12},{12,0},{16,20},{20,24},{24,28},{28,16},{32,36},... | collective-permute-start | bytes 983048 | tf_op jit(solution)/shard_map/ppermute | solution.py:646
  47.4 13.6 %collective-permute-start.17 = (bf16[16,10240]{1,0:T(8,128)(2,1)}, bf16[16,10240]{1,0:T(8,128)(2,1)}, u32[]{:S(2)}, u32[]{:S(2)}) collective-permute-start(bf16[16,10240]{1,0:T(8,128)(2,1)} %collective-permute-done.16.refs_15_), channel_id=1, source_target_pairs={{0,12},{4,0},{8,4},{12,8},{16,28},{20,16},{24,20},{28,24},{32,44},... | collective-permute-start | bytes 983048 | tf_op jit(solution)/shard_map/ppermute | solution.py:646
  50.3 22.2 %copy-start.17 = (s32[4]{0:T(128)}, s32[4]{0:T(128)S(1)}, u32[]{:S(2)}) copy-start(s32[4]{0:T(128)S(1)} %pad_add_fusion.where.refs_0_) | copy-start | bytes 52
  54.3 4.9 %copy-start.15 = (bf16[1,32,3,2048]{3,1,2,0:T(8,128)(2,1)S(1)}, bf16[1,32,3,2048]{3,1,2,0:T(8,128)(2,1)}, u32[]{:S(2)}) copy-start(bf16[1,32,3,2048]{3,1,2,0:T(8,128)(2,1)} %param.34) | copy-start | bytes 1179652
  63.7 8.8 %copy-start.2 = (bf16[4,64,10240]{2,1,0:T(8,128)(2,1)}, bf16[4,64,10240]{2,1,0:T(8,128)(2,1)S(1)}, u32[]{:S(2)}) copy-start(bf16[4,64,10240]{2,1,0:T(8,128)(2,1)S(1)} %pool_rows.1.pool.refs_8_) | copy-start | bytes 15728644
  63.8 8.7 %copy-start.5 = (f32[16,32,2048]{2,1,0:T(8,128)S(1)}, f32[16,32,2048]{2,1,0:T(8,128)}, u32[]{:S(2)}) copy-start(f32[16,32,2048]{2,1,0:T(8,128)} %copy-done.4) | copy-start | bytes 12582916
  67.4 4.4 %collective-permute-start.20 = (bf16[96,288]{1,0:T(8,128)(2,1)S(1)}, bf16[96,288]{1,0:T(8,128)(2,1)S(1)}, u32[]{:S(2)}, u32[]{:S(2)}) collective-permute-start(bf16[96,288]{1,0:T(8,128)(2,1)S(1)} %get-tuple-element.143.refs_1_), channel_id=1, source_target_pairs={{0,3},{1,2},{2,1},{3,0},{4,7},{5,6},{6,5},{7,4},{8,11},{9,10},{10,... | collective-permute-start | bytes 165896 | tf_op jit(solution)/shard_map/ppermute | solution.py:638
  67.4 5.1 %collective-permute-start.19 = (bf16[96,288]{1,0:T(8,128)(2,1)S(1)}, bf16[96,288]{1,0:T(8,128)(2,1)S(1)}, u32[]{:S(2)}, u32[]{:S(2)}) collective-permute-start(bf16[96,288]{1,0:T(8,128)(2,1)S(1)} %get-tuple-element.143.refs_1_), channel_id=1, source_target_pairs={{0,2},{1,3},{2,0},{3,1},{4,6},{5,7},{6,4},{7,5},{8,10},{9,11},{10,... | collective-permute-start | bytes 165896 | tf_op jit(solution)/shard_map/ppermute | solution.py:638
  68.3 4.3 %collective-permute-start.18 = (bf16[96,288]{1,0:T(8,128)(2,1)S(1)}, bf16[96,288]{1,0:T(8,128)(2,1)S(1)}, u32[]{:S(2)}, u32[]{:S(2)}) collective-permute-start(bf16[96,288]{1,0:T(8,128)(2,1)S(1)} %get-tuple-element.143.refs_1_), channel_id=1, source_target_pairs={{0,1},{1,0},{2,3},{3,2},{4,5},{5,4},{6,7},{7,6},{8,9},{9,8},{10,11... | collective-permute-start | bytes 165896 | tf_op jit(solution)/shard_map/ppermute | solution.py:638
  83.0 1.8 %collective-permute-start.21 = (bf16[2,96,1024]{2,1,0:T(8,128)(2,1)S(1)}, bf16[2,96,1024]{2,1,0:T(8,128)(2,1)S(1)}, u32[]{:S(2)}, u32[]{:S(2)}) collective-permute-start(bf16[2,96,1024]{2,1,0:T(8,128)(2,1)S(1)} %get-tuple-element.148), channel_id=1, source_target_pairs={{0,1},{1,0},{2,3},{3,2},{4,5},{5,4},{6,7},{7,6},{8,9},{9,8},{10,11... | collective-permute-start | bytes 1179656 | tf_op jit(solution)/shard_map/ppermute | solution.py:638
  86.8 12.8 %collective-permute-start.23 = (bf16[96,1024]{1,0:T(8,128)(2,1)}, bf16[96,1024]{1,0:T(8,128)(2,1)}, u32[]{:S(2)}, u32[]{:S(2)}) collective-permute-start(bf16[96,1024]{1,0:T(8,128)(2,1)} %get-tuple-element.162), channel_id=1, source_target_pairs={{0,66},{1,67},{2,64},{3,65},{64,2},{65,3},{66,0},{67,1},{4,70},{5,... | collective-permute-start | bytes 589832 | tf_op jit(solution)/shard_map/ppermute | solution.py:743
  88.3 11.3 %collective-permute-start.22 = (bf16[96,1024]{1,0:T(8,128)(2,1)S(1)}, bf16[96,1024]{1,0:T(8,128)(2,1)}, u32[]{:S(2)}, u32[]{:S(2)}) collective-permute-start(bf16[96,1024]{1,0:T(8,128)(2,1)S(1)} %get-tuple-element.154.same), channel_id=1, source_target_pairs={{0,64},{64,0},{1,65},{65,1},{2,66},{66,2},{3,67},{67,3},{4,68},{68... | collective-permute-start | bytes 589832 | tf_op jit(solution)/shard_map/ppermute | solution.py:744
  90.2 5.8 %copy-start.3 = (bf16[1,2048,4096]{2,1,0:T(8,128)(2,1)S(1)}, bf16[1,2048,4096]{2,1,0:T(8,128)(2,1)}, u32[]{:S(2)}) copy-start(bf16[1,2048,4096]{2,1,0:T(8,128)(2,1)} %param.23) | copy-start | bytes 50331652
  96.0 16.1 %copy-start.8 = (bf16[1,2048,288]{1,2,0:T(8,128)(2,1)S(1)}, bf16[1,2048,288]{1,2,0:T(8,128)(2,1)}, u32[]{:S(2)}) copy-start(bf16[1,2048,288]{1,2,0:T(8,128)(2,1)} %param.24) | copy-start | bytes 3538948
  96.0 16.1 %copy-start.11 = (bf16[4,3,96,512]{3,2,1,0:T(8,128)(2,1)S(1)}, bf16[4,3,96,512]{3,2,1,0:T(8,128)(2,1)}, u32[]{:S(2)}) copy-start(bf16[4,3,96,512]{3,2,1,0:T(8,128)(2,1)} %copy-done.10) | copy-start | bytes 3538948
  96.0 16.1 %copy-start.16 = (bf16[1,4096]{1,0:T(2,128)(2,1)S(1)}, bf16[1,4096]{1,0:T(2,128)(2,1)}, u32[]{:S(2)}) copy-start(bf16[1,4096]{1,0:T(2,128)(2,1)} %broadcast_in_dim.12.gain) | copy-start | bytes 24580
  96.0 16.1 %copy-start.19 = (s32[4]{0:T(128)S(1)}, s32[4]{0:T(128)}, u32[]{:S(2)}) copy-start(s32[4]{0:T(128)} %copy-done.17) | copy-start | bytes 52
  100.6 8.1 %collective-permute-start.24 = (bf16[96,1024]{1,0:T(8,128)(2,1)S(1)}, bf16[96,1024]{1,0:T(8,128)(2,1)S(1)}, u32[]{:S(2)}, u32[]{:S(2)}) collective-permute-start(bf16[96,1024]{1,0:T(8,128)(2,1)S(1)} %add_residual.1.s_own.stream), channel_id=1, source_target_pairs={{64,66},{65,67},{66,64},{67,65},{68,70},{69,71},{70,68},{71,69},{7... | collective-permute-start | bytes 589832 | tf_op jit(solution)/shard_map/ppermute | solution.py:658
  102.6 8.5 %collective-permute-start.25 = (bf16[96,1024]{1,0:T(8,128)(2,1)S(1)}, bf16[96,1024]{1,0:T(8,128)(2,1)S(1)}, u32[]{:S(2)}, u32[]{:S(2)}) collective-permute-start(bf16[96,1024]{1,0:T(8,128)(2,1)S(1)} %add_residual.1.s_own.stream), channel_id=1, source_target_pairs={{64,65},{65,64},{66,67},{67,66},{68,69},{69,68},{70,71},{71,70},{7... | collective-permute-start | bytes 589832 | tf_op jit(solution)/shard_map/ppermute | solution.py:658
  108.8 3.3 %collective-permute-start.26 = (bf16[96,1024]{1,0:T(8,128)(2,1)S(1)}, bf16[96,1024]{1,0:T(8,128)(2,1)S(1)}, u32[]{:S(2)}, u32[]{:S(2)}) collective-permute-start(bf16[96,1024]{1,0:T(8,128)(2,1)S(1)} %collective-permute-done.24.s_a), channel_id=1, source_target_pairs={{64,65},{65,64},{66,67},{67,66},{68,69},{69,68},{70,71},{71,70},{7... | collective-permute-start | bytes 589832 | tf_op jit(solution)/shard_map/ppermute | solution.py:658
  110.7 11.7 %collective-permute-start.27 = (bf16[96,1024]{1,0:T(8,128)(2,1)}, bf16[96,1024]{1,0:T(8,128)(2,1)S(1)}, u32[]{:S(2)}, u32[]{:S(2)}) collective-permute-start(bf16[96,1024]{1,0:T(8,128)(2,1)} %get-tuple-element.162), channel_id=1, source_target_pairs={{0,2},{1,3},{2,0},{3,1},{4,6},{5,7},{6,4},{7,5},{8,10},{9,11},{10,... | collective-permute-start | bytes 589832 | tf_op jit(solution)/shard_map/ppermute | solution.py:638
  112.1 14.6 %slice-start = ((s8[5242880]{0:T(1024)(128)(4,1)}), s8[4194304]{0:T(1024)(128)(4,1)S(1)}, s32[]{:S(2)}) async-start(s8[5242880]{0:T(1024)(128)(4,1)} %bitcast.35), calls=%async_computation | async-start | bytes 8388608
  112.1 14.6 %slice-start.1 = ((s8[5242880]{0:T(1024)(128)(4,1)}), s8[1048576]{0:T(1024)(128)(4,1)S(1)}, s32[]{:S(2)}) async-start(s8[5242880]{0:T(1024)(128)(4,1)} %bitcast.35), calls=%async_computation.1 | async-start | bytes 2097152
  112.1 14.6 %copy-start.6 = (f32[16,32,2048]{2,1,0:T(8,128)S(1)}, f32[16,32,2048]{2,1,0:T(8,128)}, u32[]{:S(2)}) copy-start(f32[16,32,2048]{2,1,0:T(8,128)} %copy-done.4) | copy-start | bytes 12582916
  120.5 4.2 %collective-permute-start.30 = (bf16[96,288]{1,0:T(8,128)(2,1)S(1)}, bf16[96,288]{1,0:T(8,128)(2,1)S(1)}, u32[]{:S(2)}, u32[]{:S(2)}) collective-permute-start(bf16[96,288]{1,0:T(8,128)(2,1)S(1)} %get-tuple-element.167.refs_1_), channel_id=1, source_target_pairs={{0,3},{1,2},{2,1},{3,0},{4,7},{5,6},{6,5},{7,4},{8,11},{9,10},{10,... | collective-permute-start | bytes 165896 | tf_op jit(solution)/shard_map/ppermute | solution.py:638
  121.1 5.6 %collective-permute-start.29 = (bf16[96,288]{1,0:T(8,128)(2,1)S(1)}, bf16[96,288]{1,0:T(8,128)(2,1)S(1)}, u32[]{:S(2)}, u32[]{:S(2)}) collective-permute-start(bf16[96,288]{1,0:T(8,128)(2,1)S(1)} %get-tuple-element.167.refs_1_), channel_id=1, source_target_pairs={{0,2},{1,3},{2,0},{3,1},{4,6},{5,7},{6,4},{7,5},{8,10},{9,11},{10,... | collective-permute-start | bytes 165896 | tf_op jit(solution)/shard_map/ppermute | solution.py:638
  122.3 4.4 %collective-permute-start.28 = (bf16[96,288]{1,0:T(8,128)(2,1)S(1)}, bf16[96,288]{1,0:T(8,128)(2,1)S(1)}, u32[]{:S(2)}, u32[]{:S(2)}) collective-permute-start(bf16[96,288]{1,0:T(8,128)(2,1)S(1)} %get-tuple-element.167.refs_1_), channel_id=1, source_target_pairs={{0,1},{1,0},{2,3},{3,2},{4,5},{5,4},{6,7},{7,6},{8,9},{9,8},{10,11... | collective-permute-start | bytes 165896 | tf_op jit(solution)/shard_map/ppermute | solution.py:638
  126.7 11.2 %copy-start.1 = (bf16[3,32,4096]{2,1,0:T(8,128)(2,1)S(1)}, bf16[3,32,4096]{2,1,0:T(8,128)(2,1)}, u32[]{:S(2)}) copy-start(bf16[3,32,4096]{2,1,0:T(8,128)(2,1)} %param.22) | copy-start | bytes 2359300
  (17 other events, 38.6 us)

commit v3 on v2

--- a/solution.py
+++ b/solution.py
@@ -690,18 +690,8 @@
 
     near_a = [cached[0]] + [along(cached[0], "y", k) for k in (1, 2, 3)]
     near_b = [cached[1]] + [along(cached[1], "z", k) for k in (1, 2, 3)]
-    near_a, near_b = lax.optimization_barrier((near_a, near_b))
-    proj = state_proj[0].T
+    near_a, near_b, proj = lax.optimization_barrier((near_a, near_b, state_proj[0].T))
     first_a, last_a, first_b, last_b = cat_rows(near_a + near_b)
-
-    raw = (refill_source, finished, norm_gain, conv_weight, conv_bias, decay_rate)
-    raw = (*raw, skip_gain, step_bias, residual, state_scales)
-    raw, first_a, last_a = lax.optimization_barrier((raw, first_a, last_a))
-    refill_source, finished, norm_gain, conv_weight, conv_bias, decay_rate = raw[:6]
-    skip_gain, step_bias, residual, state_scales = raw[6:]
-    gains = jnp.concatenate(
-        [conv_weight[0], conv_bias, decay_rate[0], skip_gain, step_bias], axis=0
-    )
 
     sources = lax.dynamic_slice_in_dim(refill_source, replica * SLOTS, SLOTS, 1)
     room = ((0, 0), (0, LANES - ROWS))
@@ -715,8 +705,9 @@
         gate_input.reshape(ROWS, CHANNELS),
         conv_window[0].transpose(1, 0, 2).reshape(ROWS, CHANNELS),
     )
-    flat, codes, weight, first_b = lax.optimization_barrier(
-        (flat, state_codes[0], projection[0], first_b)
+    gain_rows = (conv_weight[0], conv_bias, decay_rate[0], skip_gain, step_bias)
+    small, flat, codes, weight, gain_rows, first_a = lax.optimization_barrier(
+        (small, flat, state_codes[0], projection[0], gain_rows, first_a)
     )
     sources, ended, where, residual_rows, gain = small
     onehot, keep = plan_call(where, sources, ended)
@@ -724,8 +715,9 @@
     states = unfold_call(codes, state_scales[0])
     column_share = lax.dynamic_slice_in_dim(residual_rows, column * SHARE, SHARE, 1)
     pieces = gather_far(first_a, last_a, "z") + gather_far(first_b, last_b, "y")
-    states, store, onehot, keep, gains, gain, pieces = lax.optimization_barrier(
-        (states, store, onehot, keep, gains, gain, pieces)
+    gains = jnp.concatenate(gain_rows, axis=0)
+    states, store, onehot, keep, gains, pieces = lax.optimization_barrier(
+        (states, store, onehot, keep, gains, pieces)
     )
     pool = pool_call(pieces)
 

time: 138 us -> 136 us (0.986)
  waiting for transfers between devices: 28.4 us -> 25.3 us
    ppermute x18, waiting for transfers between devices: 13.2 us -> 10 us  [along(): return lax.ppermute(value, 'replica', pairs)]
    unnamed x68 -> x73, local copies, waits for them, and re-layouts: 11.9 us -> 12.9 us
  transfers between devices with their start and end apart: 31 -> 31, of which waited for: 17 -> 15; matrix products, arithmetic and copies ran while one was open for 2% -> 3% of each run, Pallas kernels for 11% -> 11%
where the time goes in v3:
time: 136 us
  Pallas kernels  48.4 us (36%)
  starting transfers between devices  44.9 us (33%)
  waiting for transfers between devices  25.3 us (19%)
  local copies, waits for them, and re-layouts  16.1 us (12%)
    pallas_call x14, Pallas kernels, call(): pl.pallas_call(kernel, in_specs=in_specs, out_specs=out_specs, out_shape=...  48.4 us
    ppermute x18, starting transfers between devices, along(): return lax.ppermute(value, 'replica', pairs)  31.3 us
    unnamed x73, local copies, waits for them, and re-layouts  12.9 us
    ppermute x18, waiting for transfers between devices, along(): return lax.ppermute(value, 'replica', pairs)  10 us
    ppermute x8, waiting for transfers between devices, exchange(): return lax.ppermute(value, 'tensor', [(i, i ^ step) for i in range(4)])  7.56 us
    ppermute x3, starting transfers between devices, in_section_one(): return lax.ppermute(value, ('section', 'tensor'), pairs)  5.77 us
    ppermute x3, waiting for transfers between devices, in_section_one(): return lax.ppermute(value, ('section', 'tensor'), pairs)  5.28 us
    ppermute x8, starting transfers between devices, exchange(): return lax.ppermute(value, 'tensor', [(i, i ^ step) for i in range(4)])  4.42 us
  transfers between devices with their start and end apart: 31, of which 15 were waited for; matrix products, arithmetic and copies ran while one was open for 3% of the time, Pallas kernels for 11%

profile of v3, /device:TPU:6, one launch (start us, length us, event | category | flops | bytes accessed | tf_op | source)
XLA Modules:
  0.0 135.7 jit_solution(12222697224470232996)
XLA Ops:
  0.6 2.0 %arrange_rows.1 = (bf16[4,20480]{1,0:T(4,128)(2,1)}, bf16[4,20480]{1,0:T(4,128)(2,1)}) custom-call(bf16[4,16,2048]{2,1,0:T(8,128)(2,1)} %bitcast.47, bf16[3,4,2048]{2,1,0:T(4,128)(2,1)} %bitcast.50, bf16[4,16]{1,0:T(4,128)(2,1)} %bitcast.52), custom_call_target="tpu_custom_call" | custom-call | flops 1 | bytes 1 | tf_op jit(solution)/shard_map/arrange_rows/pallas_call | solution.py:46
  2.6 3.0 %collective-permute-start.2 = (bf16[4,20480]{1,0:T(4,128)(2,1)}, bf16[4,20480]{1,0:T(4,128)(2,1)S(1)}, u32[]{:S(2)}, u32[]{:S(2)}) collective-permute-start(bf16[4,20480]{1,0:T(4,128)(2,1)} %get-tuple-element.89.refs_0_), channel_id=1, source_target_pairs={{0,12},{4,0},{8,4},{12,8},{16,28},{20,16},{24,20},{28,24},{32,44},... | collective-permute-start | bytes 491528 | tf_op jit(solution)/shard_map/ppermute | solution.py:646
  6.3 1.0 collective-permute-start
  7.2 4.0 %collective-permute-start.5 = (bf16[4,20480]{1,0:T(4,128)(2,1)}, bf16[4,20480]{1,0:T(4,128)(2,1)S(1)}, u32[]{:S(2)}, u32[]{:S(2)}) collective-permute-start(bf16[4,20480]{1,0:T(4,128)(2,1)} %get-tuple-element.93.refs_4_), channel_id=1, source_target_pairs={{0,48},{4,52},{8,56},{12,60},{16,0},{20,4},{24,8},{28,12},{32,16},... | collective-permute-start | bytes 491528 | tf_op jit(solution)/shard_map/ppermute | solution.py:646
  11.3 1.6 %collective-permute-done.2.refs_3_ = bf16[4,20480]{1,0:T(4,128)(2,1)S(1)} collective-permute-done((bf16[4,20480]{1,0:T(4,128)(2,1)}, bf16[4,20480]{1,0:T(4,128)(2,1)S(1)}, u32[]{:S(2)}, u32[]{:S(2)}) %collective-permute-start.2) | collective-permute-done | bytes 163872 | tf_op jit(solution)/shard_map/ppermute | solution.py:646
  12.9 1.9 %collective-permute-start.3 = (bf16[4,20480]{1,0:T(4,128)(2,1)}, bf16[4,20480]{1,0:T(4,128)(2,1)S(1)}, u32[]{:S(2)}, u32[]{:S(2)}) collective-permute-start(bf16[4,20480]{1,0:T(4,128)(2,1)} %get-tuple-element.93.refs_4_), channel_id=1, source_target_pairs={{0,16},{4,20},{8,24},{12,28},{16,32},{20,36},{24,40},{28,44},{32,4... | collective-permute-start | bytes 491528 | tf_op jit(solution)/shard_map/ppermute | solution.py:646
  16.5 1.3 broadcast_in_dim.12.gain
  18.4 3.4 %collective-permute-done.3.refs_5_ = bf16[4,20480]{1,0:T(4,128)(2,1)S(1)} collective-permute-done((bf16[4,20480]{1,0:T(4,128)(2,1)}, bf16[4,20480]{1,0:T(4,128)(2,1)S(1)}, u32[]{:S(2)}, u32[]{:S(2)}) %collective-permute-start.3) | collective-permute-done | bytes 163872 | tf_op jit(solution)/shard_map/ppermute | solution.py:646
  22.5 2.6 %cat_rows.1 = (bf16[16,10240]{1,0:T(8,128)(2,1)}, bf16[16,10240]{1,0:T(8,128)(2,1)}, bf16[16,10240]{1,0:T(8,128)(2,1)}, bf16[16,10240]{1,0:T(8,128)(2,1)}) custom-call(bf16[4,20480]{1,0:T(4,128)(2,1)} %get-tuple-element.89.refs_0_, bf16[4,20480]{1,0:T(4,128)(2,1)} %copy-done.25, bf16[4,20480]{1,0:T(4,128)(2,1)} %copy-done.24, bf16[4,20480]{1,0:T(4,128)(2,1)} %copy-done.23, ...), custom_call_target="tpu_custom_call" | custom-call | flops 1 | bytes 1 | tf_op jit(solution)/shard_map/cat_rows/pallas_call | solution.py:46
  25.8 1.4 collective-permute-start.6
  27.2 1.9 %collective-permute-start.10 = (bf16[16,10240]{1,0:T(8,128)(2,1)}, bf16[16,10240]{1,0:T(8,128)(2,1)}, u32[]{:S(2)}, u32[]{:S(2)}) collective-permute-start(bf16[16,10240]{1,0:T(8,128)(2,1)} %get-tuple-element.127.refs_4_), channel_id=1, source_target_pairs={{0,48},{4,52},{8,56},{12,60},{16,0},{20,4},{24,8},{28,12},{32,16},... | collective-permute-start | bytes 983048 | tf_op jit(solution)/shard_map/ppermute | solution.py:646
  29.2 3.5 %collective-permute-start.14 = (bf16[16,10240]{1,0:T(8,128)(2,1)}, bf16[16,10240]{1,0:T(8,128)(2,1)S(1)}, u32[]{:S(2)}, u32[]{:S(2)}) collective-permute-start(bf16[16,10240]{1,0:T(8,128)(2,1)} %get-tuple-element.131.refs_8_), channel_id=1, source_target_pairs={{0,12},{4,0},{8,4},{12,8},{16,28},{20,16},{24,20},{28,24},{32,44},... | collective-permute-start | bytes 983048 | tf_op jit(solution)/shard_map/ppermute | solution.py:646
  32.7 3.3 %collective-permute-done.8.refs_3_ = bf16[16,10240]{1,0:T(8,128)(2,1)S(1)} collective-permute-done((bf16[16,10240]{1,0:T(8,128)(2,1)}, bf16[16,10240]{1,0:T(8,128)(2,1)S(1)}, u32[]{:S(2)}, u32[]{:S(2)}) %collective-permute-start.8) | collective-permute-done | bytes 327712 | tf_op jit(solution)/shard_map/ppermute | solution.py:646
  36.0 1.2 collective-permute-start.12
  38.0 3.6 %collective-permute-start.16 = (bf16[16,10240]{1,0:T(8,128)(2,1)}, bf16[16,10240]{1,0:T(8,128)(2,1)}, u32[]{:S(2)}, u32[]{:S(2)}) collective-permute-start(bf16[16,10240]{1,0:T(8,128)(2,1)} %get-tuple-element.135.refs_12_), channel_id=1, source_target_pairs={{0,12},{4,0},{8,4},{12,8},{16,28},{20,16},{24,20},{28,24},{32,44},... | collective-permute-start | bytes 983048 | tf_op jit(solution)/shard_map/ppermute | solution.py:646
  41.8 1.1 collective-permute-start.15
  43.4 2.8 %collective-permute-start.11 = (bf16[16,10240]{1,0:T(8,128)(2,1)}, bf16[16,10240]{1,0:T(8,128)(2,1)}, u32[]{:S(2)}, u32[]{:S(2)}) collective-permute-start(bf16[16,10240]{1,0:T(8,128)(2,1)} %collective-permute-done.10.refs_7_), channel_id=1, source_target_pairs={{0,48},{4,52},{8,56},{12,60},{16,0},{20,4},{24,8},{28,12},{32,16},... | collective-permute-start | bytes 983048 | tf_op jit(solution)/shard_map/ppermute | solution.py:646
  46.2 1.1 collective-permute-start.13
  47.3 2.9 %collective-permute-start.17 = (bf16[16,10240]{1,0:T(8,128)(2,1)}, bf16[16,10240]{1,0:T(8,128)(2,1)}, u32[]{:S(2)}, u32[]{:S(2)}) collective-permute-start(bf16[16,10240]{1,0:T(8,128)(2,1)} %collective-permute-done.16.refs_15_), channel_id=1, source_target_pairs={{0,12},{4,0},{8,4},{12,8},{16,28},{20,16},{24,20},{28,24},{32,44},... | collective-permute-start | bytes 983048 | tf_op jit(solution)/shard_map/ppermute | solution.py:646
  51.0 1.6 %copy-done.9 = bf16[1,32,16,2048]{3,2,1,0:T(8,128)(2,1)S(1)} copy-done((bf16[1,32,16,2048]{3,2,1,0:T(8,128)(2,1)S(1)}, bf16[1,32,16,2048]{3,2,1,0:T(8,128)(2,1)}, u32[]{:S(2)}) %copy-start.9) | copy-done | bytes 2097176
  52.6 2.2 %unfold_states.1.refs_10_ = f32[16,32,2048]{2,1,0:T(8,128)S(1)} custom-call(bf16[32,16,2048]{2,1,0:T(8,128)(2,1)S(1)} %bitcast.41, bf16[32,16]{1,0:T(8,128)(2,1)S(1)} %bitcast.46), custom_call_target="tpu_custom_call" | custom-call | flops 1 | bytes 1 | tf_op jit(solution)/shard_map/unfold_states/pallas_call | solution.py:46
  54.9 2.0 %copy-done.4 = f32[16,32,2048]{2,1,0:T(8,128)} copy-done((f32[16,32,2048]{2,1,0:T(8,128)}, f32[16,32,2048]{2,1,0:T(8,128)S(1)}, u32[]{:S(2)}) %copy-start.4) | copy-done | bytes 4194328
  58.8 2.7 %pool_rows.1.pool.refs_8_ = bf16[4,64,10240]{2,1,0:T(8,128)(2,1)S(1)} custom-call(bf16[16,10240]{1,0:T(8,128)(2,1)} %get-tuple-element.123.refs_0_, bf16[16,10240]{1,0:T(8,128)(2,1)} %collective-permute-done.6.refs_1_, bf16[16,10240]{1,0:T(8,128)(2,1)} %collective-permute-done.7.refs_2_, bf16[16,10240]{1,0:T(8,128)(2,1)} %copy-done.20, ...), custom_call_target="tpu_custom_call" | custom-call | flops 1 | bytes 1 | tf_op jit(solution)/shard_map/pool_rows/pallas_call | solution.py:46
  61.7 2.6 %conv_terms.1 = (f32[96,2048]{1,0:T(8,128)S(1)}, bf16[96,288]{1,0:T(8,128)(2,1)S(1)}, f32[96,128]{1,0:T(8,128)S(1)}, bf16[4,3,96,512]{3,2,1,0:T(8,128)(2,1)S(1)}) custom-call(bf16[544,2048]{1,0:T(8,128)(2,1)S(1)} %hold_store.1.store.refs_11_, bf16[2,96,64]{2,1,0:T(8,128)(2,1)S(1)} %get-tuple-element.119.onehot.refs_5_, ...), custom_call_target="tpu_custom_call" | custom-call | flops 1 | bytes 1 | tf_op jit(solution)/shard_map/conv_terms/pallas_call | solution.py:46
  64.2 1.0 copy-done.10
  65.2 0.9 collective-permute-start.19
  66.1 1.0 collective-permute-start.18
  67.1 2.5 %collective-permute-done.20.refs_4_ = bf16[96,288]{1,0:T(8,128)(2,1)S(1)} collective-permute-done((bf16[96,288]{1,0:T(8,128)(2,1)S(1)}, bf16[96,288]{1,0:T(8,128)(2,1)S(1)}, u32[]{:S(2)}, u32[]{:S(2)}) %collective-permute-start.20) | collective-permute-done | bytes 55328 | tf_op jit(solution)/shard_map/ppermute | solution.py:638
  70.4 10.5 %scan_gate_project.1 = (f32[2,96,1024]{2,1,0:T(8,128)S(1)}, bf16[2,96,1024]{2,1,0:T(8,128)(2,1)S(1)}) custom-call(s32[4]{0:T(128)S(1)} %pad_add_fusion.where.refs_0_, bf16[96,288]{1,0:T(8,128)(2,1)S(1)} %get-tuple-element.139.refs_1_, bf16[96,288]{1,0:T(8,128)(2,1)S(1)} %collective-permute-done.18.refs_2_, ...), custom_call_target="tpu_custom_call" | custom-call | flops 1 | bytes 1 | tf_op jit(solution)/shard_map/scan_gate_project/pallas_call | solution.py:46
  81.2 1.5 %collective-permute-done.21.got = bf16[2,96,1024]{2,1,0:T(8,128)(2,1)S(1)} collective-permute-done((bf16[2,96,1024]{2,1,0:T(8,128)(2,1)S(1)}, bf16[2,96,1024]{2,1,0:T(8,128)(2,1)S(1)}, u32[]{:S(2)}, u32[]{:S(2)}) %collective-permute-start.21) | collective-permute-done | bytes 393248 | tf_op jit(solution)/shard_map/ppermute | solution.py:638
  83.3 1.3 sum_on_chip.1
  84.6 1.5 %collective-permute-start.23 = (bf16[96,1024]{1,0:T(8,128)(2,1)}, bf16[96,1024]{1,0:T(8,128)(2,1)}, u32[]{:S(2)}, u32[]{:S(2)}) collective-permute-start(bf16[96,1024]{1,0:T(8,128)(2,1)} %get-tuple-element.158), channel_id=1, source_target_pairs={{0,66},{1,67},{2,64},{3,65},{64,2},{65,3},{66,0},{67,1},{4,70},{5,... | collective-permute-start | bytes 589832 | tf_op jit(solution)/shard_map/ppermute | solution.py:735
  86.1 1.9 %collective-permute-start.22 = (bf16[96,1024]{1,0:T(8,128)(2,1)S(1)}, bf16[96,1024]{1,0:T(8,128)(2,1)}, u32[]{:S(2)}, u32[]{:S(2)}) collective-permute-start(bf16[96,1024]{1,0:T(8,128)(2,1)S(1)} %get-tuple-element.150.same), channel_id=1, source_target_pairs={{0,64},{64,0},{1,65},{65,1},{2,66},{66,2},{3,67},{67,3},{4,68},{68... | collective-permute-start | bytes 589832 | tf_op jit(solution)/shard_map/ppermute | solution.py:736
  88.0 5.8 %copy-done.3 = bf16[1,2048,4096]{2,1,0:T(8,128)(2,1)S(1)} copy-done((bf16[1,2048,4096]{2,1,0:T(8,128)(2,1)S(1)}, bf16[1,2048,4096]{2,1,0:T(8,128)(2,1)}, u32[]{:S(2)}) %copy-start.3) | copy-done | bytes 16777240
  93.8 1.2 hold_projection.1.big
  95.0 2.4 %collective-permute-done.23.other = bf16[96,1024]{1,0:T(8,128)(2,1)} collective-permute-done((bf16[96,1024]{1,0:T(8,128)(2,1)}, bf16[96,1024]{1,0:T(8,128)(2,1)}, u32[]{:S(2)}, u32[]{:S(2)}) %collective-permute-start.23) | collective-permute-done | bytes 196640 | tf_op jit(solution)/shard_map/ppermute | solution.py:735
  97.4 1.1 add_residual.1.s_own.stream
  98.5 1.9 %collective-permute-start.24 = (bf16[96,1024]{1,0:T(8,128)(2,1)S(1)}, bf16[96,1024]{1,0:T(8,128)(2,1)S(1)}, u32[]{:S(2)}, u32[]{:S(2)}) collective-permute-start(bf16[96,1024]{1,0:T(8,128)(2,1)S(1)} %add_residual.1.s_own.stream), channel_id=1, source_target_pairs={{64,66},{65,67},{66,64},{67,65},{68,70},{69,71},{70,68},{71,69},{7... | collective-permute-start | bytes 589832 | tf_op jit(solution)/shard_map/ppermute | solution.py:658
  100.4 1.9 %collective-permute-start.25 = (bf16[96,1024]{1,0:T(8,128)(2,1)S(1)}, bf16[96,1024]{1,0:T(8,128)(2,1)S(1)}, u32[]{:S(2)}, u32[]{:S(2)}) collective-permute-start(bf16[96,1024]{1,0:T(8,128)(2,1)S(1)} %add_residual.1.s_own.stream), channel_id=1, source_target_pairs={{64,65},{65,64},{66,67},{67,66},{68,69},{69,68},{70,71},{71,70},{7... | collective-permute-start | bytes 589832 | tf_op jit(solution)/shard_map/ppermute | solution.py:658
  102.4 4.2 %collective-permute-done.24.s_a = bf16[96,1024]{1,0:T(8,128)(2,1)S(1)} collective-permute-done((bf16[96,1024]{1,0:T(8,128)(2,1)S(1)}, bf16[96,1024]{1,0:T(8,128)(2,1)S(1)}, u32[]{:S(2)}, u32[]{:S(2)}) %collective-permute-start.24) | collective-permute-done | bytes 196640 | tf_op jit(solution)/shard_map/ppermute | solution.py:658
  106.6 1.9 %collective-permute-start.26 = (bf16[96,1024]{1,0:T(8,128)(2,1)S(1)}, bf16[96,1024]{1,0:T(8,128)(2,1)S(1)}, u32[]{:S(2)}, u32[]{:S(2)}) collective-permute-start(bf16[96,1024]{1,0:T(8,128)(2,1)S(1)} %collective-permute-done.24.s_a), channel_id=1, source_target_pairs={{64,65},{65,64},{66,67},{67,66},{68,69},{69,68},{70,71},{71,70},{7... | collective-permute-start | bytes 589832 | tf_op jit(solution)/shard_map/ppermute | solution.py:658
  108.9 1.0 collective-permute-done.26.s_c
  110.0 8.4 %norm_project_conv.1 = (f32[96,2048]{1,0:T(8,128)S(1)}, bf16[96,288]{1,0:T(8,128)(2,1)S(1)}, bf16[3,32,2048]{2,1,0:T(8,128)(2,1)}) custom-call(s32[4]{0:T(128)S(1)} %copy-done.19, bf16[96,1024]{1,0:T(8,128)(2,1)S(1)} %add_residual.1.s_own.stream, bf16[96,1024]{1,0:T(8,128)(2,1)S(1)} %collective-permute-done.24.s_a, ...), custom_call_target="tpu_custom_call" | custom-call | flops 1 | bytes 1 | tf_op jit(solution)/shard_map/norm_project_conv/pallas_call | solution.py:46
  118.9 1.2 collective-permute-start.29
  120.2 1.5 %add_first.1 = bf16[96,1024]{1,0:T(8,128)(2,1)} custom-call(s32[4]{0:T(128)S(1)} %copy-done.19, bf16[96,1024]{1,0:T(8,128)(2,1)S(1)} %constant_dynamic-slice_fusion.residual, bf16[96,1024]{1,0:T(8,128)(2,1)S(1)} %get-tuple-element.150.same, bf16[96,1024]{1,0:T(8,128)(2,1)S(1)} %collective-permute-done.27.other, bf16[96,1024]{1,0:T(8,128)(2,1)S(1)} %add_residual.1.s_own.stream), custom_call_target="tpu_custom_call" | custom-call | flops 1 | bytes 1 | tf_op jit(solution)/shard_map/add_first/pallas_call | solution.py:46
  121.7 0.9 collective-permute-done.30.refs_4_
  122.6 1.9 %collective-permute-done.29.refs_3_ = bf16[96,288]{1,0:T(8,128)(2,1)S(1)} collective-permute-done((bf16[96,288]{1,0:T(8,128)(2,1)S(1)}, bf16[96,288]{1,0:T(8,128)(2,1)S(1)}, u32[]{:S(2)}, u32[]{:S(2)}) %collective-permute-start.29) | collective-permute-done | bytes 55328 | tf_op jit(solution)/shard_map/ppermute | solution.py:638
  124.6 11.2 %scan_final.1 = (bf16[96,2048]{1,0:T(8,128)(2,1)}, bf16[32,16,2048]{2,1,0:T(8,128)(2,1)}, bf16[16,32]{1,0:T(8,128)(2,1)}) custom-call(s32[4]{0:T(128)S(1)} %copy-done.19, bf16[96,288]{1,0:T(8,128)(2,1)S(1)} %get-tuple-element.163.refs_1_, bf16[96,288]{1,0:T(8,128)(2,1)S(1)} %collective-permute-done.28.refs_2_, ...), custom_call_target="tpu_custom_call" | custom-call | flops 1 | bytes 1 | tf_op jit(solution)/shard_map/scan_final/pallas_call | solution.py:46
  (111 shorter events, 11.5 us)
Async XLA Ops:
  0.6 24.5 %copy-start = (bf16[3,32,4096]{2,1,0:T(8,128)(2,1)S(1)}, bf16[3,32,4096]{2,1,0:T(8,128)(2,1)}, u32[]{:S(2)}) copy-start(bf16[3,32,4096]{2,1,0:T(8,128)(2,1)} %param.22) | copy-start | bytes 2359300
  2.6 10.3 %collective-permute-start.2 = (bf16[4,20480]{1,0:T(4,128)(2,1)}, bf16[4,20480]{1,0:T(4,128)(2,1)S(1)}, u32[]{:S(2)}, u32[]{:S(2)}) collective-permute-start(bf16[4,20480]{1,0:T(4,128)(2,1)} %get-tuple-element.89.refs_0_), channel_id=1, source_target_pairs={{0,12},{4,0},{8,4},{12,8},{16,28},{20,16},{24,20},{28,24},{32,44},... | collective-permute-start | bytes 491528 | tf_op jit(solution)/shard_map/ppermute | solution.py:646
  5.6 12.2 %collective-permute-start.1 = (bf16[4,20480]{1,0:T(4,128)(2,1)}, bf16[4,20480]{1,0:T(4,128)(2,1)S(1)}, u32[]{:S(2)}, u32[]{:S(2)}) collective-permute-start(bf16[4,20480]{1,0:T(4,128)(2,1)} %get-tuple-element.89.refs_0_), channel_id=1, source_target_pairs={{0,8},{4,12},{8,0},{12,4},{16,24},{20,28},{24,16},{28,20},{32,40},... | collective-permute-start | bytes 491528 | tf_op jit(solution)/shard_map/ppermute | solution.py:646
  6.3 11.6 %collective-permute-start = (bf16[4,20480]{1,0:T(4,128)(2,1)}, bf16[4,20480]{1,0:T(4,128)(2,1)S(1)}, u32[]{:S(2)}, u32[]{:S(2)}) collective-permute-start(bf16[4,20480]{1,0:T(4,128)(2,1)} %get-tuple-element.89.refs_0_), channel_id=1, source_target_pairs={{0,4},{4,8},{8,12},{12,0},{16,20},{20,24},{24,28},{28,16},{32,36},... | collective-permute-start | bytes 491528 | tf_op jit(solution)/shard_map/ppermute | solution.py:646
  7.2 10.6 %collective-permute-start.5 = (bf16[4,20480]{1,0:T(4,128)(2,1)}, bf16[4,20480]{1,0:T(4,128)(2,1)S(1)}, u32[]{:S(2)}, u32[]{:S(2)}) collective-permute-start(bf16[4,20480]{1,0:T(4,128)(2,1)} %get-tuple-element.93.refs_4_), channel_id=1, source_target_pairs={{0,48},{4,52},{8,56},{12,60},{16,0},{20,4},{24,8},{28,12},{32,16},... | collective-permute-start | bytes 491528 | tf_op jit(solution)/shard_map/ppermute | solution.py:646
  11.3 7.1 %collective-permute-start.4 = (bf16[4,20480]{1,0:T(4,128)(2,1)}, bf16[4,20480]{1,0:T(4,128)(2,1)S(1)}, u32[]{:S(2)}, u32[]{:S(2)}) collective-permute-start(bf16[4,20480]{1,0:T(4,128)(2,1)} %get-tuple-element.93.refs_4_), channel_id=1, source_target_pairs={{0,32},{4,36},{8,40},{12,44},{16,48},{20,52},{24,56},{28,60},{32,0... | collective-permute-start | bytes 491528 | tf_op jit(solution)/shard_map/ppermute | solution.py:646
  12.9 8.9 %copy-start.23 = (bf16[4,20480]{1,0:T(4,128)(2,1)}, bf16[4,20480]{1,0:T(4,128)(2,1)S(1)}, u32[]{:S(2)}) copy-start(bf16[4,20480]{1,0:T(4,128)(2,1)S(1)} %collective-permute-done.2.refs_3_) | copy-start | bytes 491524
  12.9 8.9 %collective-permute-start.3 = (bf16[4,20480]{1,0:T(4,128)(2,1)}, bf16[4,20480]{1,0:T(4,128)(2,1)S(1)}, u32[]{:S(2)}, u32[]{:S(2)}) collective-permute-start(bf16[4,20480]{1,0:T(4,128)(2,1)} %get-tuple-element.93.refs_4_), channel_id=1, source_target_pairs={{0,16},{4,20},{8,24},{12,28},{16,32},{20,36},{24,40},{28,44},{32,4... | collective-permute-start | bytes 491528 | tf_op jit(solution)/shard_map/ppermute | solution.py:646
  17.8 52.5 %copy-start.17 = (s32[4]{0:T(128)}, s32[4]{0:T(128)S(1)}, u32[]{:S(2)}) copy-start(s32[4]{0:T(128)S(1)} %pad_add_fusion.where.refs_0_) | copy-start | bytes 52
  25.1 10.9 %collective-permute-start.8 = (bf16[16,10240]{1,0:T(8,128)(2,1)}, bf16[16,10240]{1,0:T(8,128)(2,1)S(1)}, u32[]{:S(2)}, u32[]{:S(2)}) collective-permute-start(bf16[16,10240]{1,0:T(8,128)(2,1)} %get-tuple-element.123.refs_0_), channel_id=1, source_target_pairs={{0,48},{4,52},{8,56},{12,60},{16,0},{20,4},{24,8},{28,12},{32,16},... | collective-permute-start | bytes 983048 | tf_op jit(solution)/shard_map/ppermute | solution.py:646
  25.8 12.2 %collective-permute-start.6 = (bf16[16,10240]{1,0:T(8,128)(2,1)}, bf16[16,10240]{1,0:T(8,128)(2,1)}, u32[]{:S(2)}, u32[]{:S(2)}) collective-permute-start(bf16[16,10240]{1,0:T(8,128)(2,1)} %get-tuple-element.123.refs_0_), channel_id=1, source_target_pairs={{0,16},{4,20},{8,24},{12,28},{16,32},{20,36},{24,40},{28,44},{32,4... | collective-permute-start | bytes 983048 | tf_op jit(solution)/shard_map/ppermute | solution.py:646
  27.2 14.6 %collective-permute-start.10 = (bf16[16,10240]{1,0:T(8,128)(2,1)}, bf16[16,10240]{1,0:T(8,128)(2,1)}, u32[]{:S(2)}, u32[]{:S(2)}) collective-permute-start(bf16[16,10240]{1,0:T(8,128)(2,1)} %get-tuple-element.127.refs_4_), channel_id=1, source_target_pairs={{0,48},{4,52},{8,56},{12,60},{16,0},{20,4},{24,8},{28,12},{32,16},... | collective-permute-start | bytes 983048 | tf_op jit(solution)/shard_map/ppermute | solution.py:646
  29.1 13.9 %collective-permute-start.9 = (bf16[16,10240]{1,0:T(8,128)(2,1)}, bf16[16,10240]{1,0:T(8,128)(2,1)S(1)}, u32[]{:S(2)}, u32[]{:S(2)}) collective-permute-start(bf16[16,10240]{1,0:T(8,128)(2,1)} %get-tuple-element.127.refs_4_), channel_id=1, source_target_pairs={{0,16},{4,20},{8,24},{12,28},{16,32},{20,36},{24,40},{28,44},{32,4... | collective-permute-start | bytes 983048 | tf_op jit(solution)/shard_map/ppermute | solution.py:646
  29.2 14.2 %collective-permute-start.14 = (bf16[16,10240]{1,0:T(8,128)(2,1)}, bf16[16,10240]{1,0:T(8,128)(2,1)S(1)}, u32[]{:S(2)}, u32[]{:S(2)}) collective-permute-start(bf16[16,10240]{1,0:T(8,128)(2,1)} %get-tuple-element.131.refs_8_), channel_id=1, source_target_pairs={{0,12},{4,0},{8,4},{12,8},{16,28},{20,16},{24,20},{28,24},{32,44},... | collective-permute-start | bytes 983048 | tf_op jit(solution)/shard_map/ppermute | solution.py:646
  36.0 11.3 %copy-start.20 = (bf16[16,10240]{1,0:T(8,128)(2,1)}, bf16[16,10240]{1,0:T(8,128)(2,1)S(1)}, u32[]{:S(2)}) copy-start(bf16[16,10240]{1,0:T(8,128)(2,1)S(1)} %collective-permute-done.8.refs_3_) | copy-start | bytes 983044
  36.0 10.2 %collective-permute-start.12 = (bf16[16,10240]{1,0:T(8,128)(2,1)}, bf16[16,10240]{1,0:T(8,128)(2,1)}, u32[]{:S(2)}, u32[]{:S(2)}) collective-permute-start(bf16[16,10240]{1,0:T(8,128)(2,1)} %get-tuple-element.131.refs_8_), channel_id=1, source_target_pairs={{0,4},{4,8},{8,12},{12,0},{16,20},{20,24},{24,28},{28,16},{32,36},... | collective-permute-start | bytes 983048 | tf_op jit(solution)/shard_map/ppermute | solution.py:646
  38.0 9.3 %collective-permute-start.16 = (bf16[16,10240]{1,0:T(8,128)(2,1)}, bf16[16,10240]{1,0:T(8,128)(2,1)}, u32[]{:S(2)}, u32[]{:S(2)}) collective-permute-start(bf16[16,10240]{1,0:T(8,128)(2,1)} %get-tuple-element.135.refs_12_), channel_id=1, source_target_pairs={{0,12},{4,0},{8,4},{12,8},{16,28},{20,16},{24,20},{28,24},{32,44},... | collective-permute-start | bytes 983048 | tf_op jit(solution)/shard_map/ppermute | solution.py:646
  41.8 17.0 %collective-permute-start.15 = (bf16[16,10240]{1,0:T(8,128)(2,1)}, bf16[16,10240]{1,0:T(8,128)(2,1)}, u32[]{:S(2)}, u32[]{:S(2)}) collective-permute-start(bf16[16,10240]{1,0:T(8,128)(2,1)} %get-tuple-element.135.refs_12_), channel_id=1, source_target_pairs={{0,4},{4,8},{8,12},{12,0},{16,20},{20,24},{24,28},{28,16},{32,36},... | collective-permute-start | bytes 983048 | tf_op jit(solution)/shard_map/ppermute | solution.py:646
  43.0 11.9 %copy-start.21 = (bf16[16,10240]{1,0:T(8,128)(2,1)}, bf16[16,10240]{1,0:T(8,128)(2,1)S(1)}, u32[]{:S(2)}) copy-start(bf16[16,10240]{1,0:T(8,128)(2,1)S(1)} %collective-permute-done.9.refs_5_) | copy-start | bytes 983044
  43.0 15.8 %collective-permute-start.7 = (bf16[16,10240]{1,0:T(8,128)(2,1)}, bf16[16,10240]{1,0:T(8,128)(2,1)}, u32[]{:S(2)}, u32[]{:S(2)}) collective-permute-start(bf16[16,10240]{1,0:T(8,128)(2,1)} %collective-permute-done.6.refs_1_), channel_id=1, source_target_pairs={{0,16},{4,20},{8,24},{12,28},{16,32},{20,36},{24,40},{28,44},{32,4... | collective-permute-start | bytes 983048 | tf_op jit(solution)/shard_map/ppermute | solution.py:646
  43.4 11.4 %copy-start.22 = (bf16[16,10240]{1,0:T(8,128)(2,1)}, bf16[16,10240]{1,0:T(8,128)(2,1)S(1)}, u32[]{:S(2)}) copy-start(bf16[16,10240]{1,0:T(8,128)(2,1)S(1)} %collective-permute-done.14.refs_11_) | copy-start | bytes 983044
  43.4 15.4 %collective-permute-start.11 = (bf16[16,10240]{1,0:T(8,128)(2,1)}, bf16[16,10240]{1,0:T(8,128)(2,1)}, u32[]{:S(2)}, u32[]{:S(2)}) collective-permute-start(bf16[16,10240]{1,0:T(8,128)(2,1)} %collective-permute-done.10.refs_7_), channel_id=1, source_target_pairs={{0,48},{4,52},{8,56},{12,60},{16,0},{20,4},{24,8},{28,12},{32,16},... | collective-permute-start | bytes 983048 | tf_op jit(solution)/shard_map/ppermute | solution.py:646
  46.2 12.6 %collective-permute-start.13 = (bf16[16,10240]{1,0:T(8,128)(2,1)}, bf16[16,10240]{1,0:T(8,128)(2,1)}, u32[]{:S(2)}, u32[]{:S(2)}) collective-permute-start(bf16[16,10240]{1,0:T(8,128)(2,1)} %collective-permute-done.12.refs_9_), channel_id=1, source_target_pairs={{0,4},{4,8},{8,12},{12,0},{16,20},{20,24},{24,28},{28,16},{32,36},... | collective-permute-start | bytes 983048 | tf_op jit(solution)/shard_map/ppermute | solution.py:646
  47.3 11.5 %collective-permute-start.17 = (bf16[16,10240]{1,0:T(8,128)(2,1)}, bf16[16,10240]{1,0:T(8,128)(2,1)}, u32[]{:S(2)}, u32[]{:S(2)}) collective-permute-start(bf16[16,10240]{1,0:T(8,128)(2,1)} %collective-permute-done.16.refs_15_), channel_id=1, source_target_pairs={{0,12},{4,0},{8,4},{12,8},{16,28},{20,16},{24,20},{28,24},{32,44},... | collective-permute-start | bytes 983048 | tf_op jit(solution)/shard_map/ppermute | solution.py:646
  61.6 8.7 %copy-start.2 = (bf16[4,64,10240]{2,1,0:T(8,128)(2,1)}, bf16[4,64,10240]{2,1,0:T(8,128)(2,1)S(1)}, u32[]{:S(2)}) copy-start(bf16[4,64,10240]{2,1,0:T(8,128)(2,1)S(1)} %pool_rows.1.pool.refs_8_) | copy-start | bytes 15728644
  61.6 8.7 %copy-start.5 = (f32[16,32,2048]{2,1,0:T(8,128)S(1)}, f32[16,32,2048]{2,1,0:T(8,128)}, u32[]{:S(2)}) copy-start(f32[16,32,2048]{2,1,0:T(8,128)} %copy-done.4) | copy-start | bytes 12582916
  65.2 4.4 %collective-permute-start.20 = (bf16[96,288]{1,0:T(8,128)(2,1)S(1)}, bf16[96,288]{1,0:T(8,128)(2,1)S(1)}, u32[]{:S(2)}, u32[]{:S(2)}) collective-permute-start(bf16[96,288]{1,0:T(8,128)(2,1)S(1)} %get-tuple-element.139.refs_1_), channel_id=1, source_target_pairs={{0,3},{1,2},{2,1},{3,0},{4,7},{5,6},{6,5},{7,4},{8,11},{9,10},{10,... | collective-permute-start | bytes 165896 | tf_op jit(solution)/shard_map/ppermute | solution.py:638
  65.2 5.1 %collective-permute-start.19 = (bf16[96,288]{1,0:T(8,128)(2,1)S(1)}, bf16[96,288]{1,0:T(8,128)(2,1)S(1)}, u32[]{:S(2)}, u32[]{:S(2)}) collective-permute-start(bf16[96,288]{1,0:T(8,128)(2,1)S(1)} %get-tuple-element.139.refs_1_), channel_id=1, source_target_pairs={{0,2},{1,3},{2,0},{3,1},{4,6},{5,7},{6,4},{7,5},{8,10},{9,11},{10,... | collective-permute-start | bytes 165896 | tf_op jit(solution)/shard_map/ppermute | solution.py:638
  66.1 4.3 %collective-permute-start.18 = (bf16[96,288]{1,0:T(8,128)(2,1)S(1)}, bf16[96,288]{1,0:T(8,128)(2,1)S(1)}, u32[]{:S(2)}, u32[]{:S(2)}) collective-permute-start(bf16[96,288]{1,0:T(8,128)(2,1)S(1)} %get-tuple-element.139.refs_1_), channel_id=1, source_target_pairs={{0,1},{1,0},{2,3},{3,2},{4,5},{5,4},{6,7},{7,6},{8,9},{9,8},{10,11... | collective-permute-start | bytes 165896 | tf_op jit(solution)/shard_map/ppermute | solution.py:638
  80.9 1.8 %collective-permute-start.21 = (bf16[2,96,1024]{2,1,0:T(8,128)(2,1)S(1)}, bf16[2,96,1024]{2,1,0:T(8,128)(2,1)S(1)}, u32[]{:S(2)}, u32[]{:S(2)}) collective-permute-start(bf16[2,96,1024]{2,1,0:T(8,128)(2,1)S(1)} %get-tuple-element.144), channel_id=1, source_target_pairs={{0,1},{1,0},{2,3},{3,2},{4,5},{5,4},{6,7},{7,6},{8,9},{9,8},{10,11... | collective-permute-start | bytes 1179656 | tf_op jit(solution)/shard_map/ppermute | solution.py:638
  84.6 12.8 %collective-permute-start.23 = (bf16[96,1024]{1,0:T(8,128)(2,1)}, bf16[96,1024]{1,0:T(8,128)(2,1)}, u32[]{:S(2)}, u32[]{:S(2)}) collective-permute-start(bf16[96,1024]{1,0:T(8,128)(2,1)} %get-tuple-element.158), channel_id=1, source_target_pairs={{0,66},{1,67},{2,64},{3,65},{64,2},{65,3},{66,0},{67,1},{4,70},{5,... | collective-permute-start | bytes 589832 | tf_op jit(solution)/shard_map/ppermute | solution.py:735
  86.1 11.3 %collective-permute-start.22 = (bf16[96,1024]{1,0:T(8,128)(2,1)S(1)}, bf16[96,1024]{1,0:T(8,128)(2,1)}, u32[]{:S(2)}, u32[]{:S(2)}) collective-permute-start(bf16[96,1024]{1,0:T(8,128)(2,1)S(1)} %get-tuple-element.150.same), channel_id=1, source_target_pairs={{0,64},{64,0},{1,65},{65,1},{2,66},{66,2},{3,67},{67,3},{4,68},{68... | collective-permute-start | bytes 589832 | tf_op jit(solution)/shard_map/ppermute | solution.py:736
  88.0 5.8 %copy-start.3 = (bf16[1,2048,4096]{2,1,0:T(8,128)(2,1)S(1)}, bf16[1,2048,4096]{2,1,0:T(8,128)(2,1)}, u32[]{:S(2)}) copy-start(bf16[1,2048,4096]{2,1,0:T(8,128)(2,1)} %param.23) | copy-start | bytes 50331652
  93.8 16.1 %copy-start.8 = (bf16[1,2048,288]{1,2,0:T(8,128)(2,1)S(1)}, bf16[1,2048,288]{1,2,0:T(8,128)(2,1)}, u32[]{:S(2)}) copy-start(bf16[1,2048,288]{1,2,0:T(8,128)(2,1)} %param.24) | copy-start | bytes 3538948
  93.8 16.1 %copy-start.11 = (bf16[4,3,96,512]{3,2,1,0:T(8,128)(2,1)S(1)}, bf16[4,3,96,512]{3,2,1,0:T(8,128)(2,1)}, u32[]{:S(2)}) copy-start(bf16[4,3,96,512]{3,2,1,0:T(8,128)(2,1)} %copy-done.10) | copy-start | bytes 3538948
  93.8 16.1 %copy-start.16 = (bf16[1,4096]{1,0:T(2,128)(2,1)S(1)}, bf16[1,4096]{1,0:T(2,128)(2,1)}, u32[]{:S(2)}) copy-start(bf16[1,4096]{1,0:T(2,128)(2,1)} %broadcast_in_dim.12.gain) | copy-start | bytes 24580
  93.8 16.1 %copy-start.19 = (s32[4]{0:T(128)S(1)}, s32[4]{0:T(128)}, u32[]{:S(2)}) copy-start(s32[4]{0:T(128)} %copy-done.17) | copy-start | bytes 52
  98.5 8.1 %collective-permute-start.24 = (bf16[96,1024]{1,0:T(8,128)(2,1)S(1)}, bf16[96,1024]{1,0:T(8,128)(2,1)S(1)}, u32[]{:S(2)}, u32[]{:S(2)}) collective-permute-start(bf16[96,1024]{1,0:T(8,128)(2,1)S(1)} %add_residual.1.s_own.stream), channel_id=1, source_target_pairs={{64,66},{65,67},{66,64},{67,65},{68,70},{69,71},{70,68},{71,69},{7... | collective-permute-start | bytes 589832 | tf_op jit(solution)/shard_map/ppermute | solution.py:658
  100.4 8.5 %collective-permute-start.25 = (bf16[96,1024]{1,0:T(8,128)(2,1)S(1)}, bf16[96,1024]{1,0:T(8,128)(2,1)S(1)}, u32[]{:S(2)}, u32[]{:S(2)}) collective-permute-start(bf16[96,1024]{1,0:T(8,128)(2,1)S(1)} %add_residual.1.s_own.stream), channel_id=1, source_target_pairs={{64,65},{65,64},{66,67},{67,66},{68,69},{69,68},{70,71},{71,70},{7... | collective-permute-start | bytes 589832 | tf_op jit(solution)/shard_map/ppermute | solution.py:658
  106.6 3.3 %collective-permute-start.26 = (bf16[96,1024]{1,0:T(8,128)(2,1)S(1)}, bf16[96,1024]{1,0:T(8,128)(2,1)S(1)}, u32[]{:S(2)}, u32[]{:S(2)}) collective-permute-start(bf16[96,1024]{1,0:T(8,128)(2,1)S(1)} %collective-permute-done.24.s_a), channel_id=1, source_target_pairs={{64,65},{65,64},{66,67},{67,66},{68,69},{69,68},{70,71},{71,70},{7... | collective-permute-start | bytes 589832 | tf_op jit(solution)/shard_map/ppermute | solution.py:658
  108.5 11.7 %collective-permute-start.27 = (bf16[96,1024]{1,0:T(8,128)(2,1)}, bf16[96,1024]{1,0:T(8,128)(2,1)S(1)}, u32[]{:S(2)}, u32[]{:S(2)}) collective-permute-start(bf16[96,1024]{1,0:T(8,128)(2,1)} %get-tuple-element.158), channel_id=1, source_target_pairs={{0,2},{1,3},{2,0},{3,1},{4,6},{5,7},{6,4},{7,5},{8,10},{9,11},{10,... | collective-permute-start | bytes 589832 | tf_op jit(solution)/shard_map/ppermute | solution.py:638
  109.9 14.6 %slice-start = ((s8[5242880]{0:T(1024)(128)(4,1)}), s8[4194304]{0:T(1024)(128)(4,1)S(1)}, s32[]{:S(2)}) async-start(s8[5242880]{0:T(1024)(128)(4,1)} %bitcast.35), calls=%async_computation | async-start | bytes 8388608
  110.0 14.6 %slice-start.1 = ((s8[5242880]{0:T(1024)(128)(4,1)}), s8[1048576]{0:T(1024)(128)(4,1)S(1)}, s32[]{:S(2)}) async-start(s8[5242880]{0:T(1024)(128)(4,1)} %bitcast.35), calls=%async_computation.1 | async-start | bytes 2097152
  110.0 14.6 %copy-start.6 = (f32[16,32,2048]{2,1,0:T(8,128)S(1)}, f32[16,32,2048]{2,1,0:T(8,128)}, u32[]{:S(2)}) copy-start(f32[16,32,2048]{2,1,0:T(8,128)} %copy-done.4) | copy-start | bytes 12582916
  118.4 4.2 %collective-permute-start.30 = (bf16[96,288]{1,0:T(8,128)(2,1)S(1)}, bf16[96,288]{1,0:T(8,128)(2,1)S(1)}, u32[]{:S(2)}, u32[]{:S(2)}) collective-permute-start(bf16[96,288]{1,0:T(8,128)(2,1)S(1)} %get-tuple-element.163.refs_1_), channel_id=1, source_target_pairs={{0,3},{1,2},{2,1},{3,0},{4,7},{5,6},{6,5},{7,4},{8,11},{9,10},{10,... | collective-permute-start | bytes 165896 | tf_op jit(solution)/shard_map/ppermute | solution.py:638
  118.9 5.6 %collective-permute-start.29 = (bf16[96,288]{1,0:T(8,128)(2,1)S(1)}, bf16[96,288]{1,0:T(8,128)(2,1)S(1)}, u32[]{:S(2)}, u32[]{:S(2)}) collective-permute-start(bf16[96,288]{1,0:T(8,128)(2,1)S(1)} %get-tuple-element.163.refs_1_), channel_id=1, source_target_pairs={{0,2},{1,3},{2,0},{3,1},{4,6},{5,7},{6,4},{7,5},{8,10},{9,11},{10,... | collective-permute-start | bytes 165896 | tf_op jit(solution)/shard_map/ppermute | solution.py:638
  120.2 4.4 %collective-permute-start.28 = (bf16[96,288]{1,0:T(8,128)(2,1)S(1)}, bf16[96,288]{1,0:T(8,128)(2,1)S(1)}, u32[]{:S(2)}, u32[]{:S(2)}) collective-permute-start(bf16[96,288]{1,0:T(8,128)(2,1)S(1)} %get-tuple-element.163.refs_1_), channel_id=1, source_target_pairs={{0,1},{1,0},{2,3},{3,2},{4,5},{5,4},{6,7},{7,6},{8,9},{9,8},{10,11... | collective-permute-start | bytes 165896 | tf_op jit(solution)/shard_map/ppermute | solution.py:638
  124.5 11.2 %copy-start.1 = (bf16[3,32,4096]{2,1,0:T(8,128)(2,1)S(1)}, bf16[3,32,4096]{2,1,0:T(8,128)(2,1)}, u32[]{:S(2)}) copy-start(bf16[3,32,4096]{2,1,0:T(8,128)(2,1)} %param.22) | copy-start | bytes 2359300
  (19 other events, 48.4 us)
